TPU v7x, 128 devices: a whole 4x4x4 slice. The times are simulated.
128 devices in a mesh: section: 2 (over x_lo), dp: 64 (over y, z, x_hi, core).
Axes of the slice: x: 4 (x_hi: 2, x_lo: 2; x = x_hi * 2 + x_lo), y: 4, z: 4, core: 2. Of those that a mesh axis runs over, the one named last changes fastest.
Arguments:
- tokens: bfloat16 [2, 16384, 768], P(None, 'dp'), may hold values from -16 to 16
- cotangent: bfloat16 [2, 16384, 768], P(None, 'dp'), may hold values from -6 to 6
- short_lens: int32 [128], P('dp'), may hold values from 64 to 128, as said below
- long_lens: int32 [64], P('dp'), may hold values from 128 to 256, as said below
- w_qkv: bfloat16 [2, 768, 2304], P('section'), may hold values from -0.21875 to 0.21875
- w_out: bfloat16 [2, 768, 768], P('section'), may hold values from -0.625 to 0.625
- w_gate_up: bfloat16 [2, 768, 6144], P('section'), may hold values from -0.21875 to 0.21875
- w_down: bfloat16 [2, 3072, 768], P('section'), may hold values from -0.15625 to 0.15625
- gains: float32 [2, 2, 768], P('section'), may hold values from 0.5 to 1.5
- biases: float32 [2, 6, 768], P('section'), may hold values from -3 to 3
Outputs:
- boundary: float32 [2, 2, 16384, 768], P('section', None, 'dp')
- grad_qkv: float32 [2, 768, 2304], P('section', 'dp')
- grad_out: float32 [2, 768, 768], P('section', 'dp')
- grad_gate_up: float32 [2, 768, 6144], P('section', 'dp')
- grad_down: float32 [2, 3072, 768], P('section', 'dp')
- grad_gains: float32 [2, 2, 768], P('section', None, 'dp')
- grad_biases: float32 [2, 6, 768], P('section', None, 'dp')
Inputs may be any that keep to these rules, and one draw needn't show every extreme that they name: `short_lens`: on every second dp index the first short sequence is full. `long_lens`: on every second dp index the first long sequence is full.
All inputs are finite; a program needn't handle non-finite values.
Results may differ from a plain program's by a relative error of at most 0.018.
Values may be sent and summed in bfloat16 or wider, within the bound.
A program may use at most 512 MiB of HBM per device.

v0:
```python
from functools import partial

import jax
import jax.numpy as jnp
from jax import lax
from jax.sharding import PartitionSpec as P

D = 768
HEADS = 12
HEAD = 64
FF = 3072
SHORT_LEN = 128
LONG_LEN = 256


epsilon = 1e-05
masked_value = -1000000000.0


def passed_along(value, axis, steps):
    count = lax.axis_size(axis)
    initial, last = (max(0, -steps), min(count, count - steps))
    return lax.ppermute(value, axis, [(source, source + steps) for source in range(initial, last)])


def layer_norm(values_in, gain_row, shift_row):
    average = jnp.mean(values_in, -1, keepdims=True)
    centred = values_in - average
    spread = jnp.mean(centred * centred, -1, keepdims=True)
    return centred * lax.rsqrt(spread + epsilon) * gain_row + shift_row


def gated_units(gate_up):
    return jax.nn.gelu(gate_up[:, :FF], approximate=False) * gate_up[:, FF:]


def tables(segment, lengths):
    positions = jnp.arange(LONG_LEN)
    distance = jnp.abs(positions[:, None] - positions[None, :]).astype(jnp.float32)
    same_seq = positions[:, None] // segment == positions[None, :] // segment
    key_len = jnp.repeat(lengths, segment).reshape(-1, LONG_LEN)
    key_live = (positions % segment)[None, :] < key_len
    allowed = same_seq[None] & key_live[:, None, :]
    slopes = jnp.exp2(-8.0 * (jnp.arange(HEADS).astype(jnp.float32) + 1.0) / HEADS)
    alibi_bias = -slopes[:, None, None] * distance[None]
    return (allowed, alibi_bias, key_live.reshape(-1))


def grouped(rows_in, groups):
    return rows_in.reshape(groups, LONG_LEN, HEADS, HEAD)


def masked_scores(query, keys, allowed, alibi_bias):
    groups = allowed.shape[0]
    scores = jnp.einsum(
        "gqhd,gkhd->ghqk",
        grouped(query, groups),
        grouped(keys, groups),
        preferred_element_type=jnp.float32,
    )
    scores = scores * HEAD ** (-0.5) + alibi_bias[None]
    return jnp.where(allowed[:, None], scores, masked_value)


def forward(section_in, params, layout):
    weight_qkv, weight_out, weight_gate_up, weight_down, gain_rows, bias_rows = params
    allowed, alibi_bias, unused = layout
    rows_dev = section_in.shape[0]
    groups = allowed.shape[0]
    projected = jnp.dot(section_in, weight_qkv, preferred_element_type=jnp.float32)
    query = (projected[:, :D] + bias_rows[0]).astype(jnp.bfloat16)
    keys = projected[:, D : 2 * D].astype(jnp.bfloat16)
    values = (projected[:, 2 * D :] + bias_rows[1]).astype(jnp.bfloat16)
    scores = masked_scores(query, keys, allowed, alibi_bias)
    peak = jnp.max(scores, -1, keepdims=True)
    expo = jnp.exp(scores - peak)
    totals = jnp.sum(expo, -1, keepdims=True)
    probs_low = (expo / totals).astype(jnp.bfloat16)
    log_sums = (peak + jnp.log(totals))[..., 0]
    mixed = jnp.einsum(
        "ghqk,gkhd->gqhd", probs_low, grouped(values, groups), preferred_element_type=jnp.float32
    )
    mixed = mixed.reshape(rows_dev, D).astype(jnp.bfloat16)
    resid_one = section_in.astype(jnp.float32) + (
        jnp.dot(mixed, weight_out, preferred_element_type=jnp.float32) + bias_rows[2]
    )
    normed = layer_norm(resid_one, gain_rows[0], bias_rows[3])
    normed_low = normed.astype(jnp.bfloat16)
    gate_up = jnp.dot(normed_low, weight_gate_up, preferred_element_type=jnp.float32)
    hidden = gated_units(gate_up).astype(jnp.bfloat16)
    resid_two = normed + (
        jnp.dot(hidden, weight_down, preferred_element_type=jnp.float32) + bias_rows[4]
    )
    result = layer_norm(resid_two, gain_rows[1], bias_rows[5])
    return (
        result,
        (query, keys, values, log_sums, mixed, resid_one, normed_low, gate_up, hidden, resid_two),
    )


def forward_only(section_in, params, layout):
    return forward(section_in, params, layout)[0]


def back_ffn(incoming, saved, params):
    weight_qkv, weight_out, weight_gate_up, weight_down, gain_rows, bias_rows = params
    query, keys, values, log_sums, mixed, resid_one, normed_low, gate_up, hidden, resid_two = saved
    unused, pullback = jax.vjp(layer_norm, resid_two, gain_rows[1], bias_rows[5])
    grad_resid_two, grad_gain_two, grad_shift_two = pullback(incoming)
    grad_ffn = grad_resid_two.astype(jnp.bfloat16)
    grad_down = jnp.dot(hidden.T, grad_ffn, preferred_element_type=jnp.float32)
    grad_hidden = jnp.dot(grad_ffn, weight_down.T, preferred_element_type=jnp.float32)
    unused, pullback = jax.vjp(gated_units, gate_up)
    grad_gate_up = pullback(grad_hidden)[0].astype(jnp.bfloat16)
    grad_weight_gate_up = jnp.dot(normed_low.T, grad_gate_up, preferred_element_type=jnp.float32)
    grad_normed = (
        jnp.dot(grad_gate_up, weight_gate_up.T, preferred_element_type=jnp.float32) + grad_resid_two
    )
    unused, pullback = jax.vjp(layer_norm, resid_one, gain_rows[0], bias_rows[3])
    grad_resid_one, grad_gain_one, grad_shift_one = pullback(grad_normed)
    zero_row = jnp.zeros_like(grad_shift_one)
    grad_vectors = jnp.stack(
        [
            zero_row,
            zero_row,
            zero_row,
            grad_shift_one,
            jnp.sum(grad_ffn.astype(jnp.float32), 0),
            grad_shift_two,
        ]
    )
    grad_gain_rows = jnp.stack([grad_gain_one, grad_gain_two])
    return (grad_resid_one, (grad_weight_gate_up, grad_down, grad_vectors, grad_gain_rows))


def back_attn(grad_resid_one, saved, section_in, params, layout):
    weight_qkv, weight_out, weight_gate_up, weight_down, gain_rows, bias_rows = params
    allowed, alibi_bias, unused = layout
    query, keys, values, log_sums, mixed, resid_one, normed_low, gate_up, hidden, resid_two = saved
    rows_dev = section_in.shape[0]
    groups = allowed.shape[0]
    grad_attn = grad_resid_one.astype(jnp.bfloat16)
    grad_weight_out = jnp.dot(mixed.T, grad_attn, preferred_element_type=jnp.float32)
    grad_mixed = jnp.dot(grad_attn, weight_out.T, preferred_element_type=jnp.float32).astype(
        jnp.bfloat16
    )
    grad_mixed_g = grouped(grad_mixed, groups)
    probs = jnp.exp(masked_scores(query, keys, allowed, alibi_bias) - log_sums[..., None])
    grad_probs = jnp.einsum(
        "gqhd,gkhd->ghqk", grad_mixed_g, grouped(values, groups), preferred_element_type=jnp.float32
    )
    grad_scores = (probs * (grad_probs - jnp.sum(probs * grad_probs, -1, keepdims=True))).astype(
        jnp.bfloat16
    )
    grad_values = jnp.einsum(
        "ghqk,gqhd->gkhd",
        probs.astype(jnp.bfloat16),
        grad_mixed_g,
        preferred_element_type=jnp.float32,
    )
    grad_values = grad_values.reshape(rows_dev, D).astype(jnp.bfloat16)
    grad_query = jnp.einsum(
        "ghqk,gkhd->gqhd", grad_scores, grouped(keys, groups), preferred_element_type=jnp.float32
    ) * HEAD ** (-0.5)
    grad_query = grad_query.reshape(rows_dev, D).astype(jnp.bfloat16)
    grad_keys = jnp.einsum(
        "ghqk,gqhd->gkhd", grad_scores, grouped(query, groups), preferred_element_type=jnp.float32
    ) * HEAD ** (-0.5)
    grad_keys = grad_keys.reshape(rows_dev, D).astype(jnp.bfloat16)
    grad_projected = jnp.concatenate([grad_query, grad_keys, grad_values], 1)
    grad_weight_qkv = jnp.dot(section_in.T, grad_projected, preferred_element_type=jnp.float32)
    grad_section_in = (
        jnp.dot(grad_projected, weight_qkv.T, preferred_element_type=jnp.float32) + grad_resid_one
    )
    zero_row = jnp.zeros((D,), jnp.float32)
    grad_vectors = jnp.stack(
        [
            jnp.sum(grad_query.astype(jnp.float32), 0),
            jnp.sum(grad_values.astype(jnp.float32), 0),
            jnp.sum(grad_attn.astype(jnp.float32), 0),
            zero_row,
            zero_row,
            zero_row,
        ]
    )
    return (grad_section_in, (grad_weight_qkv, grad_weight_out, grad_vectors))


def silent(function):

    def quiet(*operands):
        return jax.tree.map(jnp.zeros_like, function(*operands))

    return quiet


def by_section(period, builder):
    branches = []
    for section_id in (0, 1):
        micro = period - section_id
        if 0 <= micro < 2:
            branches.append(builder(micro))
        else:
            branches.append(silent(builder(0)))
    return branches


def on_device(
    tokens, cotangent, short_lens, long_lens, w_qkv, w_out, w_gate_up, w_down, gains, biases
):
    first_section = lax.axis_index("section") == 0
    params = (w_qkv[0], w_out[0], w_gate_up[0], w_down[0], gains[0], biases[0])
    rows_dev = tokens.shape[1]
    layouts = (tables(SHORT_LEN, short_lens), tables(LONG_LEN, long_lens))
    received = jnp.zeros((rows_dev, D), jnp.bfloat16)
    section_inputs = []
    finals = []
    for period in range(3):
        section_in = jnp.where(first_section, tokens[min(period, 1)], received)
        branches = by_section(
            period, lambda micro: partial(forward_only, params=params, layout=layouts[micro])
        )
        result = lax.cond(first_section, branches[0], branches[1], section_in)
        section_inputs.append(section_in)
        finals.append(result)
        if period < 2:
            received = passed_along(result.astype(jnp.bfloat16), "section", 1)
    cot_rows = [
        cotangent[micro].astype(jnp.float32) * layouts[micro][2][:, None].astype(jnp.float32)
        for micro in range(2)
    ]
    grad_weight_qkv = jnp.zeros(params[0].shape, jnp.float32)
    grad_weight_out = jnp.zeros(params[1].shape, jnp.float32)
    grad_weight_gate_up = jnp.zeros(params[2].shape, jnp.float32)
    grad_weight_down = jnp.zeros(params[3].shape, jnp.float32)
    grad_gain_rows = jnp.zeros(params[4].shape, jnp.float32)
    grad_vectors = jnp.zeros(params[5].shape, jnp.float32)
    returned = jnp.zeros((rows_dev, D), jnp.bfloat16)
    grad_rows = [None, None]
    for rewind in range(3):
        period = 2 - rewind
        incoming = jnp.where(
            first_section, returned.astype(jnp.float32), cot_rows[max(1 - rewind, 0)]
        )
        branches = by_section(
            period, lambda micro: partial(forward, params=params, layout=layouts[micro])
        )
        saved = lax.cond(first_section, branches[0], branches[1], section_inputs[period])[1]
        branches = by_section(period, lambda micro: partial(back_ffn, params=params))
        grad_resid_one, ffn_terms = lax.cond(
            first_section, branches[0], branches[1], incoming, saved
        )
        grad_weight_gate_up = grad_weight_gate_up + ffn_terms[0]
        grad_weight_down = grad_weight_down + ffn_terms[1]
        grad_vectors = grad_vectors + ffn_terms[2]
        grad_gain_rows = grad_gain_rows + ffn_terms[3]
        branches = by_section(
            period, lambda micro: partial(back_attn, params=params, layout=layouts[micro])
        )
        grad_section_in, attn_terms = lax.cond(
            first_section, branches[0], branches[1], grad_resid_one, saved, section_inputs[period]
        )
        grad_weight_qkv = grad_weight_qkv + attn_terms[0]
        grad_weight_out = grad_weight_out + attn_terms[1]
        grad_vectors = grad_vectors + attn_terms[2]
        if rewind < 2:
            returned = passed_along(grad_section_in.astype(jnp.bfloat16), "section", -1)
        if rewind > 0:
            grad_rows[period] = grad_section_in
    boundary = jnp.where(
        first_section, jnp.stack([grad_rows[0], grad_rows[1]]), jnp.stack([finals[1], finals[2]])
    )[None]
    shares = (
        lax.psum_scatter(grad_weight_qkv[None], "dp", scatter_dimension=1, tiled=True),
        lax.psum_scatter(grad_weight_out[None], "dp", scatter_dimension=1, tiled=True),
        lax.psum_scatter(grad_weight_gate_up[None], "dp", scatter_dimension=1, tiled=True),
        lax.psum_scatter(grad_weight_down[None], "dp", scatter_dimension=1, tiled=True),
        lax.psum_scatter(grad_gain_rows[None], "dp", scatter_dimension=2, tiled=True),
        lax.psum_scatter(grad_vectors[None], "dp", scatter_dimension=2, tiled=True),
    )
    return (boundary, shares[0], shares[1], shares[2], shares[3], shares[4], shares[5])


def solution(mesh):
    placed = (
        P(None, "dp", None),
        P(None, "dp", None),
        P("dp"),
        P("dp"),
        P("section", None, None),
        P("section", None, None),
        P("section", None, None),
        P("section", None, None),
        P("section", None, None),
        P("section", None, None),
    )
    return jax.shard_map(
        on_device,
        mesh=mesh,
        in_specs=placed,
        out_specs=(
            P("section", None, "dp", None),
            P("section", "dp", None),
            P("section", "dp", None),
            P("section", "dp", None),
            P("section", "dp", None),
            P("section", None, "dp"),
            P("section", None, "dp"),
        ),
        check_vma=False,
    )
```

profile of v0, /device:TPU:1, one launch (start us, length us, event | category | flops | bytes accessed | tf_op | source)
XLA Modules:
  0.0 2269.4 jit_solution(17592016561569092461)
XLA Ops:
  12.8 38.2 %conditional.28 = (bf16[256,768]{1,0:T(8,128)(2,1)S(1)}) conditional(s32[]{:T(128)} %convert_element_type.794, () %tuple.151, (bf16[256,768]{1,0:T(8,128)(2,1)}, bf16[768,2304]{1,0:T(8,128)(2,1)}, f32[6,768]{1,0:T(8,128)}, pred[1,256,256]{1,2,0:T(8,128)(4,1)}, f32[12,256,256]{1,2,0:T(8,128)S(1)}, /*index=5*/bf16[768,768]{1,0:T(8,128)(2,1)}, ...), branch_computations={%region_6.7_spmd, %region_7.14_spmd} | conditional | flops 5097656832 | bytes 96958656 | solution.py:223
  60.6 45.6 %conditional.30 = (f32[256,768]{1,0:T(8,128)}) conditional(s32[]{:T(128)} %convert_element_type.794, (bf16[256,768]{1,0:T(8,128)(2,1)S(1)}, bf16[768,2304]{1,0:T(8,128)(2,1)}, f32[6,768]{1,0:T(8,128)}, pred[1,256,256]{1,2,0:T(8,128)(4,1)}, f32[12,256,256]{1,2,0:T(8,128)S(1)}, /*index=5*/bf16[768,768]{1,0:T(8,128)(2,1)}, f32[2,768]{1,0:T(2,128)S(1)}, ...), branch_computations={%region_24.31_spmd, %region_31.38_spmd} | conditional | flops 5097460224 | bytes 97351872 | solution.py:223
  107.4 15.4 collective-permute-start.1
  130.9 11.2 conditional.31
  142.1 22.3 conditional.32
  151.3 8.8 broadcast.2294.clone
  174.7 62.0 %conditional.39 = (f32[1,12,256]{2,1,0:T(8,128)}, f32[256,768]{1,0:T(8,128)}, f32[256,6144]{1,0:T(8,128)}, f32[256,768]{1,0:T(8,128)}, bf16[256,768]{1,0:T(8,128...) conditional(s32[]{:T(128)} %convert_element_type.794, ...), branch_computations={%region_14.19_spmd, %region_19.24_spmd} | conditional | flops 5096666112 | bytes 132087176
  223.7 8.9 fusion.155
  236.7 90.8 %collective-permute-done.2 = bf16[256,768]{1,0:T(8,128)(2,1)} collective-permute-done((bf16[256,768]{1,0:T(8,128)(2,1)}, bf16[256,768]{1,0:T(8,128)(2,1)}, u32[]{:S(2)}, u32[]{:S(2)}) %collective-permute-start.2) | collective-permute-done | bytes 393248 | tf_op jit(solution)/shard_map/ppermute | solution.py:23
  329.4 90.5 %conditional.34 = (f32[256,768]{1,0:T(8,128)}, f32[6,768]{1,0:T(8,128)}, f32[2,768]{1,0:T(2,128)S(1)}, f32[768,6144]{1,0:T(8,128)}, f32[3072,768]{1,0:T(8,128)}) conditional(s32[]{:T(128)} %convert_element_type.794, (f32[256,6144]{1,0:T(8,128)}, pred[]{:T(512)}, f32[256,768]{1,0:T(8,128)}, f32[256,768]{1,0:T(8,128)}, f32[2,768]{1,0:T(2,128)S(1)}, ...), branch_computations={%region_65.0_spmd, %region_79.93_spmd} | conditional | flops 7325221888 | bytes 210959680 | solution.py:250
  341.5 10.1 multiply_multiply_fusion.51
  372.9 11.9 convolution_bitcast_fusion.8
  384.8 18.7 copy.281
  410.1 9.6 copy.283
  420.4 56.1 %conditional.35 = (f32[768,768]{1,0:T(8,128)}, f32[6,768]{1,0:T(8,128)}, f32[256,768]{1,0:T(8,128)}, f32[256,768]{1,0:T(8,128)}, f32[768,2304]{1,0:T(8,128)}) conditional(s32[]{:T(128)} %convert_element_type.794, (pred[1,256,256]{1,2,0:T(8,128)(4,1)}, bf16[256,768]{1,0:T(8,128)(2,1)}, bf16[256,768]{1,0:T(8,128)(2,1)}, ...), branch_computations={%region_93.98_spmd, %region_98.103_spmd} | conditional | flops 2937121536 | bytes 105165024 | solution.py:260
  480.3 45.2 %conditional.27 = (bf16[256,768]{1,0:T(8,128)(2,1)}, bf16[256,768]{1,0:T(8,128)(2,1)}, bf16[256,768]{1,0:T(8,128)(2,1)}, f32[1,12,256]{2,1,0:T(8,128)}, bf16[256...) conditional(s32[]{:T(128)} %convert_element_type.794, ...), branch_computations={%region_0.1_spmd, %region_1.6_spmd} | conditional | flops 5096666112 | bytes 125795752 | solution.py:248
  512.5 8.9 fusion.54
  532.6 90.9 %conditional.36 = (f32[256,768]{1,0:T(8,128)}, f32[6,768]{1,0:T(8,128)}, f32[2,768]{1,0:T(2,128)}, f32[768,6144]{1,0:T(8,128)}, f32[3072,768]{1,0:T(8,128)}) conditional(s32[]{:T(128)} %convert_element_type.794, () %tuple.150, (f32[256,6144]{1,0:T(8,128)}, pred[]{:T(512)}, f32[256,768]{1,0:T(8,128)}, f32[256,768]{1,0:T(8,128)}, ...), branch_computations={%region_103.104_spmd, %region_104.118_spmd} | conditional | flops 7325221888 | bytes 210959680 | solution.py:250
  544.4 10.1 multiply_multiply_fusion.59
  576.5 11.9 convolution_bitcast_fusion.10
  588.4 18.6 copy.287
  613.6 9.6 copy.289
  623.6 49.9 %conditional.37 = (f32[768,768]{1,0:T(8,128)}, f32[6,768]{1,0:T(8,128)}, f32[1,1,256,768]{3,2,1,0:T(8,128)}, f32[768,2304]{1,0:T(8,128)}) conditional(s32[]{:T(128)} %convert_element_type.794, () %tuple.147, (pred[1,256,256]{1,2,0:T(8,128)(4,1)}, bf16[256,768]{1,0:T(8,128)(2,1)}, bf16[256,768]{1,0:T(8,128)(2,1)}, ...), branch_computations={%region_118.119_spmd, %region_119.124_spmd} | conditional | flops 2937318144 | bytes 107524344 | solution.py:260
  673.5 11.2 add_add_fusion.9
  684.7 11.1 broadcast_in_dim.312
  701.0 25.4 %add_add_fusion.8 = f32[768,6144]{1,0:T(8,128)} fusion(f32[768,6144]{1,0:T(8,128)} %get-tuple-element.950, f32[768,6144]{1,0:T(8,128)} %get-tuple-element.944, f32[768,6144]{1,0:T(8,128)} %get-tuple-element.947), kind=kLoop, calls=%fused_computation.831 | loop fusion | flops 9437184 | bytes 75497472 | tf_op jit(solution)/shard_map/add | solution.py:253
  726.4 16.1 broadcast_in_dim.314
  742.5 14.0 add_bitcast_fusion.5
  760.1 327.8 %all-reduce.13 = (f32[1,2,768]{2,1,0:T(2,128)S(1)}, f32[1,6,768]{2,0,1:T(1,128)S(1)}) all-reduce(f32[1,2,768]{2,1,0:T(2,128)S(1)} %add_bitcast_fusion.7, f32[1,6,768]{2,0,1:T(1,128)S(1)} %broadcast_in_dim.317), channel_id=6, replica_groups=mesh['section'=2,'dp'=64] {'dp'}, use_global_device_ids=true, to_apply=%region_136.137.clone | all-reduce | flops 6144 | bytes 49152
  1092.1 285.4 %all-reduce.20.cloned.1.call-done = (f32[1,768,2304]{2,0,1:T(1,128)}, f32[1,768,768]{2,0,1:T(1,128)}) async-done(((f32[1,768,2304]{2,0,1:T(1,128)}, f32[1,768,768]{2,0,1:T(1,128)}), (f32[1,768,2304]{2,0,1:T(1,128)}, f32[1,768,768]{2,0,1:T(1,128)})) %all-reduce.20.cloned.1.call-update) | async-done | bytes 9437200
  1380.4 701.9 %all-reduce.18.cloned.1.call-done = f32[1,768,6144]{2,0,1:T(1,128)} async-done(((f32[1,768,6144]{2,0,1:T(1,128)}), f32[1,768,6144]{2,0,1:T(1,128)}) %all-reduce.18.cloned.1.call-update) | async-done | bytes 18874384
  2084.0 178.6 %reduce-scatter.4.cloned.1.call-done = f32[1,48,768]{2,1,0:T(8,128)} async-done(((f32[1,3072,768]{2,1,0:T(8,128)}), f32[1,48,768]{2,1,0:T(8,128)}) %reduce-scatter.4.cloned.1.call-update) | async-done | bytes 147472 | tf_op jit(solution)/shard_map/reduce_scatter | solution.py:277
  (410 shorter events, 420.4 us)
Async XLA Ops:
  7.2 1370.3 %all-reduce.20.cloned.1.call-start = ((), (), s32[]{:S(2)}) async-start(), calls=%async_computation.3 | async-start | bytes 18874368
  42.2 8.4 copy-start.75
  51.0 8.6 collective-permute-start
  96.6 8.4 copy-start.79
  107.4 21.7 collective-permute-start.1
  171.3 156.1 %collective-permute-start.2 = (bf16[256,768]{1,0:T(8,128)(2,1)}, bf16[256,768]{1,0:T(8,128)(2,1)}, u32[]{:S(2)}, u32[]{:S(2)}) collective-permute-start(bf16[256,768]{1,0:T(8,128)(2,1)} %get-tuple-element.695), channel_id=1, source_target_pairs={{64,0},{65,1},{66,2},{67,3},{68,4},{69,5},{70,6},{71,7},{72,8},{73... | collective-permute-start | bytes 1179656 | tf_op jit(solution)/shard_map/ppermute | solution.py:23
  207.8 10.4 slice-start.9
  207.8 10.4 slice-start.10
  207.8 10.4 slice-start.11
  215.9 16.7 slice-start.34
  218.2 14.4 slice-start.35
  223.7 9.0 copy-start.108
  341.3 16.3 slice-start.15
  341.4 10.1 copy-start.57
  341.5 16.1 slice-start.16
  341.5 16.1 slice-start.17
  479.0 51.7 %collective-permute-start.3 = (bf16[256,768]{1,0:T(8,128)(2,1)}, bf16[256,768]{1,0:T(8,128)(2,1)}, u32[]{:S(2)}, u32[]{:S(2)}) collective-permute-start(bf16[256,768]{1,0:T(8,128)(2,1)} %get-tuple-element.1174), channel_id=1, source_target_pairs={{64,0},{65,1},{66,2},{67,3},{68,4},{69,5},{70,6},{71,7},{72,8},{73... | collective-permute-start | bytes 1179656 | tf_op jit(solution)/shard_map/ppermute | solution.py:23
  497.2 9.8 slice-start.18
  497.2 9.8 slice-start.19
  497.2 9.8 slice-start.20
  499.9 12.5 copy-start.42
  504.7 16.7 slice-start.36
  507.0 14.5 slice-start.37
  512.5 9.0 copy-start.109
  544.2 16.5 slice-start.21
  544.3 10.2 copy-start.58
  544.3 16.3 slice-start.22
  544.3 16.3 slice-start.23
  684.6 11.1 copy-start.29
  684.7 11.1 copy-start.30
  700.9 1381.4 %all-reduce.18.cloned.1.call-start = ((), (), s32[]{:S(2)}) async-start(), calls=%async_computation.2 | async-start | bytes 37748736
  742.4 1520.2 %reduce-scatter.4.cloned.1.call-start = ((), (), s32[]{:S(2)}) async-start(), calls=%async_computation.1 | async-start | bytes 9584640 | tf_op jit(solution)/shard_map/reduce_scatter | solution.py:277
  (55 other events, 174.0 us)
Sparse Core Ops, SparseCore 0:
  701.1 676.4 all-reduce.19
  1380.0 702.2 all-reduce.17
  2088.7 173.9 reduce-scatter.3
where the time goes:
time: 2280 us; the launch traced here: 2270 us
  waiting for transfers between devices  1270 us (56%)
  blocking collectives  328 us (14%)
  local copies, waits for them, and re-layouts  226 us (10%)
  matrix products  220 us (10%)
  other arithmetic  152 us (7%)
  loops' own time  35.1 us (2%)
    unnamed x5, waiting for transfers between devices  987 us
    unnamed x1, blocking collectives  328 us
    reduce_scatter x1, waiting for transfers between devices, on_device(): lax.psum_scatter(grad_weight_down[None], 'dp', scatter_dimension=1, tiled...  179 us
    ppermute x4, waiting for transfers between devices, passed_along(): lax.ppermute(value, axis, [(source, source + steps) for source in range(i...  107 us
    cond x4, local copies, waits for them, and re-layouts, on_device(): lax.cond(first_section, branches[0], branches[1], incoming, saved)  56.5 us
  transfers between devices with their start and end apart: 7, of which 7 were waited for; matrix products, arithmetic and copies ran while one was open for 7% of the time, Pallas kernels for 0%

commit v1 on v0

--- a/solution.py
+++ b/solution.py
@@ -3,6 +3,8 @@
 import jax
 import jax.numpy as jnp
 from jax import lax
+from jax.experimental import pallas as pl
+from jax.experimental.pallas import tpu as pltpu
 from jax.sharding import PartitionSpec as P
 
 D = 768
@@ -108,11 +110,9 @@
     unused, pullback = jax.vjp(layer_norm, resid_two, gain_rows[1], bias_rows[5])
     grad_resid_two, grad_gain_two, grad_shift_two = pullback(incoming)
     grad_ffn = grad_resid_two.astype(jnp.bfloat16)
-    grad_down = jnp.dot(hidden.T, grad_ffn, preferred_element_type=jnp.float32)
     grad_hidden = jnp.dot(grad_ffn, weight_down.T, preferred_element_type=jnp.float32)
     unused, pullback = jax.vjp(gated_units, gate_up)
     grad_gate_up = pullback(grad_hidden)[0].astype(jnp.bfloat16)
-    grad_weight_gate_up = jnp.dot(normed_low.T, grad_gate_up, preferred_element_type=jnp.float32)
     grad_normed = (
         jnp.dot(grad_gate_up, weight_gate_up.T, preferred_element_type=jnp.float32) + grad_resid_two
     )
@@ -130,7 +130,7 @@
         ]
     )
     grad_gain_rows = jnp.stack([grad_gain_one, grad_gain_two])
-    return (grad_resid_one, (grad_weight_gate_up, grad_down, grad_vectors, grad_gain_rows))
+    return (grad_resid_one, (grad_gate_up, grad_ffn, grad_vectors, grad_gain_rows, normed_low, hidden))
 
 
 def back_attn(grad_resid_one, saved, section_in, params, layout):
@@ -140,7 +140,6 @@
     rows_dev = section_in.shape[0]
     groups = allowed.shape[0]
     grad_attn = grad_resid_one.astype(jnp.bfloat16)
-    grad_weight_out = jnp.dot(mixed.T, grad_attn, preferred_element_type=jnp.float32)
     grad_mixed = jnp.dot(grad_attn, weight_out.T, preferred_element_type=jnp.float32).astype(
         jnp.bfloat16
     )
@@ -168,7 +167,6 @@
     ) * HEAD ** (-0.5)
     grad_keys = grad_keys.reshape(rows_dev, D).astype(jnp.bfloat16)
     grad_projected = jnp.concatenate([grad_query, grad_keys, grad_values], 1)
-    grad_weight_qkv = jnp.dot(section_in.T, grad_projected, preferred_element_type=jnp.float32)
     grad_section_in = (
         jnp.dot(grad_projected, weight_qkv.T, preferred_element_type=jnp.float32) + grad_resid_one
     )
@@ -183,7 +181,7 @@
             zero_row,
         ]
     )
-    return (grad_section_in, (grad_weight_qkv, grad_weight_out, grad_vectors))
+    return (grad_section_in, (grad_projected, grad_attn, grad_vectors, mixed))
 
 
 def silent(function):
@@ -203,6 +201,429 @@
         else:
             branches.append(silent(builder(0)))
     return branches
+
+
+S_SLOTS = 5
+OWN_SLOTS = 3
+N_CHUNKS = 12
+MESH_IDS = pl.DeviceIdType.MESH
+
+
+def reduce_kernel(
+    xa, xm, xn, xh, gq, go, gg, gf, vec,
+    o_qkv, o_out, o_gu, o_dn, o_vec,
+    t_a, t_m, t_n, t_h, w_q, w_o, w_g, w_f,
+    own, ra_relay, ra_fin, sa, own_b, rb_relay, rb_fin, sb, x_send, x_keep, x_recv, c_tmp, c_send, c_keep, c_recv,
+    v_acc, v_recv,
+    in_sem, peer_send, peer_recv,
+    a_send, a_relay_recv, a_fin_recv, a2_send,
+    b_send, b_relay_recv, b_fin_recv, b2_send,
+    xs_sem, xr_sem, cs_sem, cr_sem, vs_sem, vr_sem,
+):
+    me = lax.axis_index("dp")
+    core = me % 2
+    xhi = (me // 2) % 2
+    zz = (me // 4) % 4
+    yy = me // 16
+
+    def dev(y, z, x, c):
+        return ((y * 4 + z) * 2 + x) * 2 + c
+
+    peer_core = dev(yy, zz, xhi, 1 - core)
+    peer_x = dev(yy, zz, 1 - xhi, core)
+    y_ids = [dev((yy + k) % 4, zz, xhi, core) for k in (1, 2, 3)]
+    z_ids = [dev(yy, (zz + k) % 4, xhi, core) for k in (1, 2, 3)]
+    peers = [peer_core, peer_x] + y_ids + z_ids
+
+    def remote(src, dst, send, recv, target):
+        return pltpu.make_async_remote_copy(
+            src_ref=src, dst_ref=dst, send_sem=send, recv_sem=recv,
+            device_id={"dp": target}, device_id_type=MESH_IDS,
+        )
+
+    half = 512
+    local = [
+        pltpu.make_async_copy(xn, t_n.at[:, pl.ds(0, half)], in_sem.at[0]),
+        pltpu.make_async_copy(gg.at[:, pl.ds(core * 3072, 3072)], w_g.at[pl.ds(0, half)], in_sem.at[1]),
+        pltpu.make_async_copy(xa, t_a.at[:, pl.ds(0, half)], in_sem.at[2]),
+        pltpu.make_async_copy(gq.at[:, pl.ds(core * 1152, 1152)], w_q.at[pl.ds(0, half)], in_sem.at[3]),
+        pltpu.make_async_copy(xm, t_m.at[:, pl.ds(0, half)], in_sem.at[4]),
+        pltpu.make_async_copy(go.at[:, pl.ds(core * 384, 384)], w_o.at[pl.ds(0, half)], in_sem.at[5]),
+        pltpu.make_async_copy(xh.at[:, core], t_h.at[:, :, pl.ds(0, half)], in_sem.at[6]),
+        pltpu.make_async_copy(gf, w_f.at[pl.ds(0, half)], in_sem.at[7]),
+    ]
+    other = 1 - core
+    across = [
+        remote(xn, t_n.at[:, pl.ds(half, half)], peer_send.at[0], peer_recv.at[0], peer_core),
+        remote(gg.at[:, pl.ds(other * 3072, 3072)], w_g.at[pl.ds(half, half)], peer_send.at[1], peer_recv.at[1], peer_core),
+        remote(xa, t_a.at[:, pl.ds(half, half)], peer_send.at[2], peer_recv.at[2], peer_core),
+        remote(gq.at[:, pl.ds(other * 1152, 1152)], w_q.at[pl.ds(half, half)], peer_send.at[3], peer_recv.at[3], peer_core),
+        remote(xm, t_m.at[:, pl.ds(half, half)], peer_send.at[4], peer_recv.at[4], peer_core),
+        remote(go.at[:, pl.ds(other * 384, 384)], w_o.at[pl.ds(half, half)], peer_send.at[5], peer_recv.at[5], peer_core),
+        remote(xh.at[:, other], t_h.at[:, :, pl.ds(half, half)], peer_send.at[6], peer_recv.at[6], peer_core),
+        remote(gf, w_f.at[pl.ds(half, half)], peer_send.at[7], peer_recv.at[7], peer_core),
+    ]
+    for copy in local:
+        copy.start()
+    barrier = pltpu.get_barrier_semaphore()
+    for peer in peers:
+        pl.semaphore_signal(barrier, inc=1, device_id={"dp": peer}, device_id_type=MESH_IDS)
+    pl.semaphore_wait(barrier, len(peers))
+    for copy in across:
+        copy.start()
+
+    def v_sends(stage):
+        targets = ([peer_core], [peer_x], y_ids, z_ids)[stage]
+        base = (0, 1, 2, 5)[stage]
+        count = len(targets)
+        return [
+            remote(
+                v_acc.at[stage], v_recv.at[base + (count - 1 - k)],
+                vs_sem.at[base + k], vr_sem.at[base + (count - 1 - k)], targets[k],
+            )
+            for k in range(count)
+        ]
+
+    def v_start(stage):
+        for copy in v_sends(stage):
+            copy.start()
+
+    def v_finish(stage):
+        base = (0, 1, 2, 5)[stage]
+        count = (1, 1, 3, 3)[stage]
+        copies = v_sends(stage)
+        for copy in copies:
+            copy.wait_send()
+        total = v_acc[stage]
+        for k in range(count):
+            copies[count - 1 - k].wait_recv()
+        for k in range(count):
+            total = total + v_recv[base + k]
+        v_acc[stage + 1] = total
+
+    v_acc[0] = vec[...]
+    v_start(0)
+
+    def ring(par):
+        right = y_ids[0] * (1 - par) + z_ids[0] * par
+        left = y_ids[2] * (1 - par) + z_ids[2] * par
+        place = yy * (1 - par) + zz * par
+        return right, left, place
+
+    def a1_copies(j):
+        slot, mine = j % S_SLOTS, j % OWN_SLOTS
+        right, left, p = ring(j % 2)
+        far, nxt, prv = (p + 2) % 4, (p + 1) % 4, (p + 3) % 4
+        return (
+            remote(own.at[mine, 0, far], ra_relay.at[slot, 0], a_send.at[slot, 0], a_relay_recv.at[slot, 0], right),
+            remote(own.at[mine, 1, far], ra_relay.at[slot, 1], a_send.at[slot, 1], a_relay_recv.at[slot, 1], left),
+            remote(own.at[mine, 1, nxt], ra_fin.at[slot, 0, 1], a_send.at[slot, 2], a_fin_recv.at[slot, 0, 1], right),
+            remote(own.at[mine, 0, prv], ra_fin.at[slot, 1, 0], a_send.at[slot, 3], a_fin_recv.at[slot, 1, 0], left),
+        )
+
+    def a2_copies(j):
+        slot = j % S_SLOTS
+        right, left, _ = ring(j % 2)
+        return (
+            remote(sa.at[slot, 0], ra_fin.at[slot, 0, 0], a2_send.at[slot, 0], a_fin_recv.at[slot, 0, 0], right),
+            remote(sa.at[slot, 1], ra_fin.at[slot, 1, 1], a2_send.at[slot, 1], a_fin_recv.at[slot, 1, 1], left),
+        )
+
+    def b1_copies(j):
+        slot = j % S_SLOTS
+        right, left, p = ring(1 - j % 2)
+        far, nxt, prv = (p + 2) % 4, (p + 1) % 4, (p + 3) % 4
+        return (
+            remote(own_b.at[slot, 0, far], rb_relay.at[slot, 0], b_send.at[slot, 0], b_relay_recv.at[slot, 0], right),
+            remote(own_b.at[slot, 1, far], rb_relay.at[slot, 1], b_send.at[slot, 1], b_relay_recv.at[slot, 1], left),
+            remote(own_b.at[slot, 1, nxt], rb_fin.at[slot, 0, 1], b_send.at[slot, 2], b_fin_recv.at[slot, 0, 1], right),
+            remote(own_b.at[slot, 0, prv], rb_fin.at[slot, 1, 0], b_send.at[slot, 3], b_fin_recv.at[slot, 1, 0], left),
+        )
+
+    def b2_copies(j):
+        slot = j % S_SLOTS
+        right, left, _ = ring(1 - j % 2)
+        return (
+            remote(sb.at[slot, 0], rb_fin.at[slot, 0, 0], b2_send.at[slot, 0], b_fin_recv.at[slot, 0, 0], right),
+            remote(sb.at[slot, 1], rb_fin.at[slot, 1, 1], b2_send.at[slot, 1], b_fin_recv.at[slot, 1, 1], left),
+        )
+
+    def x_copy(j):
+        slot = j % S_SLOTS
+        return remote(x_send.at[slot], x_recv.at[slot], xs_sem.at[slot], xr_sem.at[slot], peer_x)
+
+    def c_copy(j):
+        slot = j % S_SLOTS
+        return remote(c_send.at[slot], c_recv.at[slot], cs_sem.at[slot], cr_sem.at[slot], peer_core)
+
+    def wait_operands(*which):
+        for k in which:
+            local[k].wait()
+            across[k].wait()
+
+    def store_rows(j, halves):
+        mine = j % OWN_SLOTS
+        par = j % 2
+        for y in range(4):
+            for z in range(4):
+                first = y * (1 - par) + z * par
+                second = z * (1 - par) + y * par
+                for h in range(2):
+                    own[mine, h, first, second] = halves[h][y * 4 + z]
+
+    def product(lhs, rhs):
+        return jnp.dot(lhs, rhs, preferred_element_type=jnp.float32).astype(jnp.bfloat16)
+
+    def split_halves(result):
+        return [result[:, h * 256:(h + 1) * 256].reshape(16, 48, 256) for h in range(2)]
+
+    def compute(j):
+        @pl.when(j < 6)
+        def _():
+            @pl.when(j == 0)
+            def _():
+                wait_operands(0, 1)
+            rhs = w_g[:, pl.ds(pl.multiple_of(j * 512, 512), 512)]
+            store_rows(j, split_halves(product(t_n[...], rhs)))
+
+        @pl.when((j >= 6) & (j < 8))
+        def _():
+            @pl.when(j == 6)
+            def _():
+                wait_operands(2, 3)
+            rhs = w_q[:, pl.ds(pl.multiple_of((j - 6) * 512, 512), 512)]
+            store_rows(j, split_halves(product(t_a[...], rhs)))
+
+        @pl.when(j == 8)
+        def _():
+            wait_operands(4, 5)
+            one = product(t_a[...], w_q[:, pl.ds(1024, 128)])
+            two = product(t_m[...], w_o[...])
+            store_rows(j, split_halves(jnp.concatenate([one, two], axis=1)))
+
+        @pl.when(j >= 9)
+        def _():
+            @pl.when(j == 9)
+            def _():
+                wait_operands(6, 7)
+            rhs = w_f[:, pl.ds(pl.multiple_of((j - 9) * 256, 256), 256)]
+            result = product(t_h[...].reshape(1536, 1024), rhs).reshape(16, 2, 48, 256)
+            store_rows(j, [result[:, 0], result[:, 1]])
+
+    def f32(value):
+        return value.astype(jnp.float32)
+
+    def step(i, carry):
+        @pl.when(i < N_CHUNKS)
+        def _():
+            compute(i)
+            for copy in a1_copies(i):
+                copy.start()
+
+        j1 = i - 1
+
+        @pl.when((j1 >= 0) & (j1 < N_CHUNKS))
+        def _():
+            slot, mine = j1 % S_SLOTS, j1 % OWN_SLOTS
+            _, _, p = ring(j1 % 2)
+            first = a1_copies(j1)
+            second = a2_copies(j1)
+            first[0].wait_recv()
+            sa[slot, 0] = (f32(own[mine, 0, (p + 1) % 4]) + f32(ra_relay[slot, 0])).astype(jnp.bfloat16)
+            second[0].start()
+            first[1].wait_recv()
+            sa[slot, 1] = (f32(own[mine, 1, (p + 3) % 4]) + f32(ra_relay[slot, 1])).astype(jnp.bfloat16)
+            second[1].start()
+
+        j2 = i - 2
+
+        @pl.when((j2 >= 0) & (j2 < N_CHUNKS))
+        def _():
+            slot, mine = j2 % S_SLOTS, j2 % OWN_SLOTS
+            _, _, p = ring(j2 % 2)
+            first = a1_copies(j2)
+            second = a2_copies(j2)
+            for copy in first + second:
+                copy.wait_send()
+            first[2].wait_recv()
+            first[3].wait_recv()
+            second[0].wait_recv()
+            second[1].wait_recv()
+            for h in range(2):
+                own_b[slot, h] = (
+                    f32(own[mine, h, p]) + f32(ra_fin[slot, 0, h]) + f32(ra_fin[slot, 1, h])
+                ).astype(jnp.bfloat16)
+            for copy in b1_copies(j2):
+                copy.start()
+
+        j3 = i - 3
+
+        @pl.when((j3 >= 0) & (j3 < N_CHUNKS))
+        def _():
+            slot = j3 % S_SLOTS
+            _, _, p = ring(1 - j3 % 2)
+            first = b1_copies(j3)
+            second = b2_copies(j3)
+            first[0].wait_recv()
+            sb[slot, 0] = (f32(own_b[slot, 0, (p + 1) % 4]) + f32(rb_relay[slot, 0])).astype(jnp.bfloat16)
+            second[0].start()
+            first[1].wait_recv()
+            sb[slot, 1] = (f32(own_b[slot, 1, (p + 3) % 4]) + f32(rb_relay[slot, 1])).astype(jnp.bfloat16)
+            second[1].start()
+
+        j4 = i - 4
+
+        @pl.when((j4 >= 0) & (j4 < N_CHUNKS))
+        def _():
+            slot = j4 % S_SLOTS
+            _, _, p = ring(1 - j4 % 2)
+            first = b1_copies(j4)
+            second = b2_copies(j4)
+            for copy in first + second:
+                copy.wait_send()
+            first[2].wait_recv()
+            first[3].wait_recv()
+            second[0].wait_recv()
+            second[1].wait_recv()
+            total = [
+                f32(own_b[slot, h, p]) + f32(rb_fin[slot, 0, h]) + f32(rb_fin[slot, 1, h])
+                for h in range(2)
+            ]
+            low = xhi == 0
+
+            @pl.when(j4 < 9)
+            def _():
+                for h in range(2):
+                    x_send[slot, h] = jnp.where(low, total[h][24:], total[h][:24])
+                    x_keep[slot, h] = jnp.where(low, total[h][:24], total[h][24:])
+
+            @pl.when(j4 >= 9)
+            def _():
+                sent = jnp.where(low, total[1], total[0])
+                kept = jnp.where(low, total[0], total[1])
+                for h in range(2):
+                    x_send[slot, h] = sent[h * 24:(h + 1) * 24]
+                    x_keep[slot, h] = kept[h * 24:(h + 1) * 24]
+
+            x_copy(j4).start()
+
+        j5 = i - 5
+
+        @pl.when((j5 >= 0) & (j5 < N_CHUNKS))
+        def _():
+            slot = j5 % S_SLOTS
+            x_copy(j5).wait()
+
+            @pl.when(j5 < 9)
+            def _():
+                for h in range(2):
+                    c_tmp[h] = x_keep[slot, h] + x_recv[slot, h]
+                low = core == 0
+                for h in range(2):
+                    upper, lower = c_tmp[h, 0:12], c_tmp[h, 12:24]
+                    c_send[slot, h, 0:12] = jnp.where(low, lower, upper)
+                    c_keep[slot, h, 0:12] = jnp.where(low, upper, lower)
+                c_copy(j5).start()
+
+            @pl.when(j5 >= 9)
+            def _():
+                column = pl.ds(pl.multiple_of((j5 - 9) * 256, 256), 256)
+                for h in range(2):
+                    o_dn[h * 24:(h + 1) * 24, column] = x_keep[slot, h] + x_recv[slot, h]
+
+        j6 = i - 6
+
+        @pl.when((j6 >= 0) & (j6 < 9))
+        def _():
+            slot = j6 % S_SLOTS
+            c_copy(j6).wait()
+            for source, who in ((c_keep, core), (c_recv, 1 - core)):
+                @pl.when(j6 < 6)
+                def _():
+                    for h in range(2):
+                        column = pl.multiple_of(who * 3072 + j6 * 512 + h * 256, 256)
+                        o_gu[:, pl.ds(column, 256)] = source[slot, h, 0:12]
+
+                @pl.when((j6 >= 6) & (j6 < 8))
+                def _():
+                    for h in range(2):
+                        column = pl.multiple_of(who * 1152 + (j6 - 6) * 512 + h * 256, 128)
+                        o_qkv[:, pl.ds(column, 256)] = source[slot, h, 0:12]
+
+                @pl.when(j6 == 8)
+                def _():
+                    o_qkv[:, pl.ds(pl.multiple_of(who * 1152 + 1024, 128), 128)] = source[slot, 0, 0:12, 0:128]
+                    o_out[:, pl.ds(pl.multiple_of(who * 384, 128), 128)] = source[slot, 0, 0:12, 128:256]
+                    o_out[:, pl.ds(pl.multiple_of(who * 384 + 128, 128), 256)] = source[slot, 1, 0:12]
+
+        for stage in range(4):
+            @pl.when(i == 2 * stage + 2)
+            def _():
+                v_finish(stage)
+                if stage < 3:
+                    v_start(stage + 1)
+
+        return carry
+
+    lax.fori_loop(0, N_CHUNKS + 6, step, 0)
+    o_vec[...] = v_acc[4]
+
+
+def reduce_weights(xa, xm, xn, xh, gq, go, gg, gf, vec):
+    low, wide = jnp.bfloat16, jnp.float32
+    hbm = pl.BlockSpec(memory_space=pl.ANY)
+    vmem = pl.BlockSpec(memory_space=pltpu.VMEM)
+    dma = pltpu.SemaphoreType.DMA
+    s = S_SLOTS
+    return pl.pallas_call(
+        reduce_kernel,
+        out_shape=[
+            jax.ShapeDtypeStruct((12, 2304), wide),
+            jax.ShapeDtypeStruct((12, 768), wide),
+            jax.ShapeDtypeStruct((12, 6144), wide),
+            jax.ShapeDtypeStruct((48, 768), wide),
+            jax.ShapeDtypeStruct((8, 768), wide),
+        ],
+        in_specs=[hbm] * 8 + [vmem],
+        out_specs=[vmem] * 5,
+        scratch_shapes=[
+            pltpu.VMEM((768, 1024), low),
+            pltpu.VMEM((768, 1024), low),
+            pltpu.VMEM((768, 1024), low),
+            pltpu.VMEM((32, 48, 1024), low),
+            pltpu.VMEM((1024, 1152), low),
+            pltpu.VMEM((1024, 384), low),
+            pltpu.VMEM((1024, 3072), low),
+            pltpu.VMEM((1024, 768), low),
+            pltpu.VMEM((OWN_SLOTS, 2, 4, 4, 48, 256), low),
+            pltpu.VMEM((s, 2, 4, 48, 256), low),
+            pltpu.VMEM((s, 2, 2, 4, 48, 256), low),
+            pltpu.VMEM((s, 2, 4, 48, 256), low),
+            pltpu.VMEM((s, 2, 4, 48, 256), low),
+            pltpu.VMEM((s, 2, 48, 256), low),
+            pltpu.VMEM((s, 2, 2, 48, 256), low),
+            pltpu.VMEM((s, 2, 48, 256), low),
+            pltpu.VMEM((s, 2, 24, 256), wide),
+            pltpu.VMEM((s, 2, 24, 256), wide),
+            pltpu.VMEM((s, 2, 24, 256), wide),
+            pltpu.VMEM((2, 24, 256), wide),
+            pltpu.VMEM((s, 2, 16, 256), wide),
+            pltpu.VMEM((s, 2, 16, 256), wide),
+            pltpu.VMEM((s, 2, 16, 256), wide),
+            pltpu.VMEM((5, 8, 768), wide),
+            pltpu.VMEM((8, 8, 768), wide),
+            dma((8,)), dma((8,)), dma((8,)),
+            dma((s, 4)), dma((s, 2)), dma((s, 2, 2)), dma((s, 2)),
+            dma((s, 4)), dma((s, 2)), dma((s, 2, 2)), dma((s, 2)),
+            dma((s,)), dma((s,)), dma((s,)), dma((s,)),
+            dma((8,)), dma((8,)),
+        ],
+        compiler_params=pltpu.CompilerParams(
+            collective_id=0, has_side_effects=True, vmem_limit_bytes=56 * 1024 * 1024
+        ),
+        cost_estimate=pl.CostEstimate(flops=10 ** 10, bytes_accessed=2 * 10 ** 7, transcendentals=0),
+        name="reduce_weights",
+    )(xa, xm, xn, xh.reshape(32, 2, 48, 512), gq, go, gg, gf, vec)
 
 
 def on_device(
@@ -229,12 +650,9 @@
         cotangent[micro].astype(jnp.float32) * layouts[micro][2][:, None].astype(jnp.float32)
         for micro in range(2)
     ]
-    grad_weight_qkv = jnp.zeros(params[0].shape, jnp.float32)
-    grad_weight_out = jnp.zeros(params[1].shape, jnp.float32)
-    grad_weight_gate_up = jnp.zeros(params[2].shape, jnp.float32)
-    grad_weight_down = jnp.zeros(params[3].shape, jnp.float32)
     grad_gain_rows = jnp.zeros(params[4].shape, jnp.float32)
     grad_vectors = jnp.zeros(params[5].shape, jnp.float32)
+    operands = [None, None, None]
     returned = jnp.zeros((rows_dev, D), jnp.bfloat16)
     grad_rows = [None, None]
     for rewind in range(3):
@@ -250,8 +668,6 @@
         grad_resid_one, ffn_terms = lax.cond(
             first_section, branches[0], branches[1], incoming, saved
         )
-        grad_weight_gate_up = grad_weight_gate_up + ffn_terms[0]
-        grad_weight_down = grad_weight_down + ffn_terms[1]
         grad_vectors = grad_vectors + ffn_terms[2]
         grad_gain_rows = grad_gain_rows + ffn_terms[3]
         branches = by_section(
@@ -260,8 +676,10 @@
         grad_section_in, attn_terms = lax.cond(
             first_section, branches[0], branches[1], grad_resid_one, saved, section_inputs[period]
         )
-        grad_weight_qkv = grad_weight_qkv + attn_terms[0]
-        grad_weight_out = grad_weight_out + attn_terms[1]
+        operands[period] = (
+            section_inputs[period], attn_terms[3], ffn_terms[4], ffn_terms[5],
+            attn_terms[0], attn_terms[1], ffn_terms[0], ffn_terms[1],
+        )
         grad_vectors = grad_vectors + attn_terms[2]
         if rewind < 2:
             returned = passed_along(grad_section_in.astype(jnp.bfloat16), "section", -1)
@@ -270,15 +688,15 @@
     boundary = jnp.where(
         first_section, jnp.stack([grad_rows[0], grad_rows[1]]), jnp.stack([finals[1], finals[2]])
     )[None]
-    shares = (
-        lax.psum_scatter(grad_weight_qkv[None], "dp", scatter_dimension=1, tiled=True),
-        lax.psum_scatter(grad_weight_out[None], "dp", scatter_dimension=1, tiled=True),
-        lax.psum_scatter(grad_weight_gate_up[None], "dp", scatter_dimension=1, tiled=True),
-        lax.psum_scatter(grad_weight_down[None], "dp", scatter_dimension=1, tiled=True),
-        lax.psum_scatter(grad_gain_rows[None], "dp", scatter_dimension=2, tiled=True),
-        lax.psum_scatter(grad_vectors[None], "dp", scatter_dimension=2, tiled=True),
-    )
-    return (boundary, shares[0], shares[1], shares[2], shares[3], shares[4], shares[5])
+    early = jax.tree.map(lambda u, v: jnp.where(first_section, u, v), operands[0], operands[1])
+    late = jax.tree.map(lambda u, v: jnp.where(first_section, u, v), operands[1], operands[2])
+    both = [jnp.concatenate(pair, 0) for pair in zip(early, late)]
+    vec = jnp.concatenate([grad_gain_rows, grad_vectors], 0)
+    g_qkv, g_out, g_gu, g_dn, g_vec = reduce_weights(
+        both[0].T, both[1].T, both[2].T, both[3].T, both[4], both[5], both[6], both[7], vec
+    )
+    mine = lax.dynamic_slice_in_dim(g_vec, lax.axis_index("dp") * 12, 12, axis=1)
+    return (boundary, g_qkv[None], g_out[None], g_gu[None], g_dn[None], mine[None, :2], mine[None, 2:])
 
 
 def solution(mesh):

time: 2280 us -> 607 us (0.27)
  waiting for transfers between devices: 1270 us -> 76.9 us
  blocking collectives: 328 us -> 0 us
  local copies, waits for them, and re-layouts: 226 us -> 126 us
  Pallas kernels: 0 us -> 85 us
  matrix products: 220 us -> 148 us
  other arithmetic: 152 us -> 119 us
    unnamed x5 -> x0, waiting for transfers between devices: 987 us -> none
    unnamed x1 -> x0, blocking collectives: 328 us -> none
    reduce_scatter x1 -> x0, waiting for transfers between devices: 179 us -> none  [on_device(): lax.psum_scatter(grad_weight_down[None], 'dp', scatter_dimension=1, tiled...]
    pallas_call x0 -> x1, Pallas kernels: none -> 85 us  [reduce_weights(): pl.pallas_call(reduce_kernel, out_shape=[jax.ShapeDtypeStruct((12, 2304),...]
    cond x124 -> x96, local copies, waits for them, and re-layouts: 68.8 us -> 11.2 us  [the longest x4 56.5 us: on_device(): lax.cond(first_section, branches[0], branches[1], incoming, saved)]
    dot_general x8 -> x0, matrix products: 52 us -> none  [the longest x2 23.8 us: back_ffn(): jnp.dot(normed_low.T, grad_gate_up, preferred_element_type=jnp.float32)]
    add x3 -> x1, other arithmetic: 38.7 us -> 0.85 us  [on_device(): grad_gain_rows = grad_gain_rows + ffn_terms[3]]
    ppermute x4, waiting for transfers between devices: 107 us -> 76.9 us  [passed_along(): lax.ppermute(value, axis, [(source, source + steps) for source in range(i...]
  transfers between devices with their start and end apart: 7 -> 4, of which waited for: 7 -> 3; matrix products, arithmetic and copies ran while one was open for 7% -> 15% of each run, Pallas kernels for 0% -> 0%
where the time goes in v1:
time: 607 us; the launch traced here: 597 us
  matrix products  148 us (24%)
  local copies, waits for them, and re-layouts  126 us (21%)
  other arithmetic  119 us (20%)
  Pallas kernels  85 us (14%)
  waiting for transfers between devices  76.9 us (13%)
  loops' own time  22.7 us (4%)
  starting transfers between devices  18.4 us (3%)
    pallas_call x1, Pallas kernels, reduce_weights(): pl.pallas_call(reduce_kernel, out_shape=[jax.ShapeDtypeStruct((12, 2304),...  85 us
    ppermute x4, waiting for transfers between devices, passed_along(): lax.ppermute(value, axis, [(source, source + steps) for source in range(i...  76.9 us
    another operation x38, local copies, waits for them, and re-layouts  33 us
    dot_general x4, matrix products, forward(): jnp.dot(hidden, weight_down, preferred_element_type=jnp.float32)  22.5 us
    dot_general x2, matrix products, back_ffn(): jnp.dot(grad_ffn, weight_down.T, preferred_element_type=jnp.float32)  21.4 us
    dot_general x4, matrix products, forward(): jnp.dot(normed_low, weight_gate_up, preferred_element_type=jnp.float32)  19.9 us
    ppermute x4, starting transfers between devices, passed_along(): lax.ppermute(value, axis, [(source, source + steps) for source in range(i...  18.4 us
    unnamed x120, local copies, waits for them, and re-layouts  17.4 us
  transfers between devices with their start and end apart: 4, of which 3 were waited for; matrix products, arithmetic and copies ran while one was open for 15% of the time, Pallas kernels for 0%

profile of v1, /device:TPU:1, one launch (start us, length us, event | category | flops | bytes accessed | tf_op | source)
XLA Modules:
  0.0 596.9 jit_solution(15991855633162334273)
XLA Ops:
  6.2 39.6 %conditional.17 = (bf16[256,768]{1,0:T(8,128)(2,1)S(1)}) conditional(s32[]{:T(128)} %convert_element_type.800, () %tuple.159, (bf16[256,768]{1,0:T(8,128)(2,1)}, bf16[768,2304]{1,0:T(8,128)(2,1)}, f32[6,768]{1,0:T(8,128)}, pred[1,256,256]{1,2,0:T(8,128)(4,1)}, f32[12,256,256]{1,2,0:T(8,128)S(1)}, /*index=5*/bf16[768,768]{1,0:T(8,128)(2,1)}, ...), branch_computations={%region_6.7_spmd, %region_7.14_spmd} | conditional | flops 5097656832 | bytes 96958656 | solution.py:644
  30.7 6.0 fusion.76
  36.7 8.1 %fusion.433 = (f32[256]{0:T(256)S(1)}, f32[256,768]{1,0:T(8,128)S(1)}) fusion(f32[768]{0:T(1024)S(1)} %copy-done.135, bf16[3072,768]{1,0:T(8,128)(2,1)S(1)} %bitcast.570, f32[256,6144]{1,0:T(8,128)S(1)} %fusion.76, f32[768]{0:T(1024)S(1)} %get-tuple-element.903, f32[768]{0:T(1024)S(1)} %get-tuple-element.1066, f32[256]{0:T(256)S(1)} %add_rsqrt_fusion.2, ...), kind=kOutput, calls=%fused_computation.868 | convolution fusion | flops 1261240064 | bytes 12595200 | tf_op jit(solution)/shard_map/cond/branch_1_fun/dot_general | solution.py:94
  48.6 5.8 collective-permute-done
  56.3 45.6 %conditional.19 = (f32[256,768]{1,0:T(8,128)}) conditional(s32[]{:T(128)} %convert_element_type.800, (bf16[256,768]{1,0:T(8,128)(2,1)S(1)}, bf16[768,2304]{1,0:T(8,128)(2,1)}, f32[6,768]{1,0:T(8,128)}, pred[1,256,256]{1,2,0:T(8,128)(4,1)}, f32[12,256,256]{1,2,0:T(8,128)S(1)}, /*index=5*/bf16[768,768]{1,0:T(8,128)(2,1)}, f32[2,768]{1,0:T(2,128)S(1)}, ...), branch_computations={%region_24.31_spmd, %region_31.38_spmd} | conditional | flops 5097460224 | bytes 97351872 | solution.py:644
  79.4 4.5 fusion.236
  86.2 5.8 fusion.240
  92.1 8.1 %fusion.443 = (f32[256]{0:T(256)S(1)}, f32[256,768]{1,0:T(8,128)S(1)}) fusion(f32[768]{0:T(1024)S(1)} %copy-done.137, bf16[3072,768]{1,0:T(8,128)(2,1)S(1)} %bitcast.574, f32[256,6144]{1,0:T(8,128)S(1)} %fusion.240, f32[768]{0:T(1024)S(1)} %get-tuple-element.929, f32[768]{0:T(1024)S(1)} %get-tuple-element.1096, f32[256]{0:T(256)S(1)} %add_rsqrt_fusion.8, ...), kind=kOutput, calls=%fused_computation.878 | convolution fusion | flops 1261240064 | bytes 12595200 | tf_op jit(solution)/shard_map/cond/branch_1_fun/dot_general | solution.py:94
  103.2 14.3 %collective-permute-start.1 = (bf16[256,768]{1,0:T(8,128)(2,1)S(1)}, bf16[256,768]{1,0:T(8,128)(2,1)S(1)}, u32[]{:S(2)}, u32[]{:S(2)}) collective-permute-start(bf16[256,768]{1,0:T(8,128)(2,1)S(1)} %convert_element_type.804), channel_id=1, source_target_pairs={{0,64},{1,65},{2,66},{3,67},{4,68},{5,69},{6,70},{7,71},{8,72},{9,... | collective-permute-start | bytes 1179656 | tf_op jit(solution)/shard_map/ppermute | solution.py:25
  118.1 5.7 collective-permute-done.1
  126.4 10.5 %conditional.20 = (bf16[256,768]{1,0:T(8,128)(2,1)}, bf16[256,768]{1,0:T(8,128)(2,1)}, bf16[256,768]{1,0:T(8,128)(2,1)}, f32[1,12,256]{2,1,0:T(8,128)S(1)}, bf16...) conditional(s32[]{:T(128)} %convert_element_type.800, ...), branch_computations={%region_38.43_spmd, %region_43.44_spmd} | conditional | flops 5096666112 | bytes 135282160 | solution.py:666
  137.5 6.6 %conditional.42 = (f32[256,768]{1,0:T(8,128)}, bf16[256,6144]{1,0:T(8,128)(2,1)}, bf16[256,768]{1,0:T(8,128)(2,1)}, f32[6,768]{1,0:T(8,128)}, f32[2,768]{1,0:T(2...) conditional(s32[]{:T(128)} %convert_element_type.800, (f32[256,6144]{1,0:T(8,128)}, pred[]{:T(512)}, ...), branch_computations={%region_44.58_spmd, %region_58.59_spmd} | conditional | flops 3699180800 | bytes 130725128 | solution.py:668
  144.7 4.3 conditional.43
  152.3 48.1 %conditional.49 = (f32[1,12,256]{2,1,0:T(8,128)}, f32[256,768]{1,0:T(8,128)}, f32[256,6144]{1,0:T(8,128)}, f32[256,768]{1,0:T(8,128)}, bf16[256,768]{1,0:T(8,128...) conditional(s32[]{:T(128)} %convert_element_type.800, ...), branch_computations={%region_14.19_spmd, %region_19.24_spmd} | conditional | flops 5096666112 | bytes 172146224
  187.8 6.8 %fusion.135 = bf16[256,3072]{1,0:T(8,128)(2,1)S(1)} fusion(f32[256,6144]{1,0:T(8,128)S(1)} %fusion.459), kind=kLoop, calls=%fused_computation.252 | loop fusion | flops 51904512 | bytes 7864320 | tf_op jit(solution)/shard_map/cond/branch_1_fun/convert_element_type | solution.py:92
  200.4 65.4 %collective-permute-done.2 = bf16[256,768]{1,0:T(8,128)(2,1)} collective-permute-done((bf16[256,768]{1,0:T(8,128)(2,1)}, bf16[256,768]{1,0:T(8,128)(2,1)}, u32[]{:S(2)}, u32[]{:S(2)}) %collective-permute-start.2) | collective-permute-done | bytes 393248 | tf_op jit(solution)/shard_map/ppermute | solution.py:25
  267.8 47.8 %conditional.50 = (f32[256,768]{1,0:T(8,128)}, bf16[256,768]{1,0:T(8,128)(2,1)}, f32[6,768]{1,0:T(8,128)}, f32[2,768]{1,0:T(2,128)S(1)}, bf16[256,6144]{1,0:T(8,128)(2,1)}) conditional(s32[]{:T(128)} %convert_element_type.800, (f32[256,6144]{1,0:T(8,128)}, pred[]{:T(512)}, f32[256,768]{1,0:T(8,128)}, f32[256,768]{1,0:T(8,128)}, ...), branch_computations={%region_65.0_spmd, %region_79.93_spmd} | conditional | flops 3698197760 | bytes 145706464
  284.8 11.3 %multiply_multiply_fusion.51 = (f32[256,3072]{1,0:T(8,128)}, f32[256,3072]{1,0:T(8,128)}, f32[256,3072]{1,0:T(8,128)}) fusion(f32[256,6144]{1,0:T(8,128)S(1)} %copy-done.7, bf16[256,768]{1,0:T(8,128)(2,1)S(1)} %get-tuple-element.1215, bf16[3072,768]{1,0:T(8,128)(2,1)} %get-tuple-element.541), kind=kOutput, calls=%fused_computation.622 | convolution fusion | flops 1259077632 | bytes 17694720 | tf_op jit(solution)/shard_map/cond/branch_1_fun/dot_general | solution.py:113
  296.2 4.5 multiply_add_fusion.16
  303.3 4.4 multiply_reduce_fusion.25
  316.2 30.4 %conditional.45 = (bf16[256,768]{1,0:T(8,128)(2,1)}, f32[6,768]{1,0:T(8,128)S(1)}, f32[256,768]{1,0:T(8,128)}, f32[256,768]{1,0:T(8,128)}, bf16[256,2304]{1,0:T(8,128)(2,1)}) conditional(s32[]{:T(128)} %convert_element_type.800, (pred[1,256,256]{1,2,0:T(8,128)(4,1)}, bf16[256,768]{1,0:T(8,128)(2,1)}, bf16[256,768]{1,0:T(8,128)(2,1)}, ...), branch_computations={%region_93.98_spmd, %region_98.103_spmd} | conditional | flops 1728768768 | bytes 69382392 | solution.py:676
  340.6 4.3 fusion.22
  350.5 49.2 %conditional.16 = (bf16[256,768]{1,0:T(8,128)(2,1)}, bf16[256,768]{1,0:T(8,128)(2,1)}, bf16[256,768]{1,0:T(8,128)(2,1)}, f32[1,12,256]{2,1,0:T(8,128)}, bf16[256...) conditional(s32[]{:T(128)} %convert_element_type.800, ...), branch_computations={%region_0.1_spmd, %region_1.6_spmd} | conditional | flops 5096666112 | bytes 132136360 | solution.py:666
  380.5 5.5 fusion.454
  386.1 8.9 %fusion.34 = bf16[256,3072]{1,0:T(8,128)(2,1)} fusion(f32[256,6144]{1,0:T(8,128)} %fusion.454), kind=kLoop, calls=%fused_computation.69 | loop fusion | flops 51904512 | bytes 7864320 | tf_op jit(solution)/shard_map/cond/branch_1_fun/convert_element_type | solution.py:92
  407.5 39.2 %conditional.46 = (f32[256,768]{1,0:T(8,128)}, bf16[256,6144]{1,0:T(8,128)(2,1)}, bf16[256,768]{1,0:T(8,128)(2,1)S(1)}, f32[6,768]{1,0:T(8,128)}, f32[2,768]{1,0...) conditional(s32[]{:T(128)} %convert_element_type.800, () %tuple.158, ...), branch_computations={%region_103.104_spmd, %region_104.118_spmd} | conditional | flops 3698197760 | bytes 122092896 | solution.py:668
  415.3 10.0 %multiply_multiply_fusion.59 = (f32[256,3072]{1,0:T(8,128)S(1)}, f32[256,3072]{1,0:T(8,128)S(1)}, f32[256,3072]{1,0:T(8,128)}) fusion(f32[256,6144]{1,0:T(8,128)} %get-tuple-element.562, bf16[256,768]{1,0:T(8,128)(2,1)S(1)} %get-tuple-element.1258, bf16[3072,768]{1,0:T(8,128)(2,1)S(1)} %copy-done.147), kind=kOutput, calls=%fused_computation.666 | convolution fusion | flops 1259077632 | bytes 17694720 | tf_op jit(solution)/shard_map/cond/branch_1_fun/dot_general | solution.py:113
  425.4 5.4 multiply_add_fusion.19
  433.0 6.5 %multiply_reduce_fusion.31 = (f32[768]{0:T(1024)}, f32[256]{0:T(256)}, f32[768]{0:T(1024)S(1)}, f32[256,768]{1,0:T(8,128)}) fusion(f32[256,768]{1,0:T(8,128)} %get-tuple-element.570, f32[256]{0:T(256)S(1)} %fusion.345, f32[256]{0:T(256)S(1)} %broadcast_multiply_fusion.16, f32[768]{0:T(1024)S(1)} %get-tuple-element.970, ...), kind=kOutput, calls=%fused_computation.684 | convolution fusion | flops 2417883392 | bytes 14955520 | tf_op jit(solution)/shard_map/cond/branch_1_fun/dot_general | solution.py:117
  450.9 4.7 copy.165
  455.6 28.7 %conditional.47 = (bf16[256,768]{1,0:T(8,128)(2,1)}, f32[6,768]{1,0:T(8,128)S(1)}, bf16[256,768]{1,0:T(8,128)(2,1)S(1)}, f32[1,1,256,768]{3,2,1,0:T(8,128)S(1)}, bf16[256,2304]{1,0:T(8,128)(2,1)}) conditional(s32[]{:T(128)} %convert_element_type.800, () %tuple.155, (pred[1,256,256]{1,2,0:T(8,128)(4,1)}, bf16[256,768]{1,0:T(8,128)(2,1)}, ...), branch_computations={%region_118.119_spmd, %region_119.124_spmd} | conditional | flops 1728965376 | bytes 66236576 | solution.py:676
  502.6 85.0 %reduce_weights.1 = (f32[12,2304]{1,0:T(8,128)}, f32[12,768]{1,0:T(8,128)}, f32[12,6144]{1,0:T(8,128)}, f32[48,768]{1,0:T(8,128)}, f32[8,768]{1,0:T(8,128)}) custom-call(bf16[768,512]{1,0:T(8,128)(2,1)} %copy.170.xa, bf16[768,512]{1,0:T(8,128)(2,1)} %copy.171.xm, bf16[768,512]{1,0:T(8,128)(2,1)} %copy.172.xn, bf16[32,2,48,512]{3,2,1,0:T(8,128)(2,1)} %bitcast.477, ...), custom_call_target="tpu_custom_call" | custom-call | flops 10000000000 | bytes 20000000 | tf_op jit(solution)/shard_map/reduce_weights/pallas_call | solution.py:578
  (460 shorter events, 292.5 us)
Async XLA Ops:
  36.7 8.4 %copy-start.107 = (f32[768]{0:T(1024)S(1)}, f32[768]{0:T(1024)}, u32[]{:S(2)}) copy-start(f32[768]{0:T(1024)} %get-tuple-element.901) | copy-start | bytes 9220 | tf_op jit(solution)/shard_map/cond
  36.7 8.4 %copy-start.108 = (f32[768]{0:T(1024)S(1)}, f32[768]{0:T(1024)}, u32[]{:S(2)}) copy-start(f32[768]{0:T(1024)} %get-tuple-element.1067) | copy-start | bytes 9220 | tf_op jit(solution)/shard_map/cond
  45.8 8.5 %collective-permute-start = (bf16[256,768]{1,0:T(8,128)(2,1)S(1)}, bf16[256,768]{1,0:T(8,128)(2,1)S(1)}, u32[]{:S(2)}, u32[]{:S(2)}) collective-permute-start(bf16[256,768]{1,0:T(8,128)(2,1)S(1)} %get-tuple-element.1287), channel_id=1, source_target_pairs={{0,64},{1,65},{2,66},{3,67},{4,68},{5,69},{6,70},{7,71},{8,72},{9,... | collective-permute-start | bytes 1179656 | tf_op jit(solution)/shard_map/ppermute | solution.py:25
  92.1 8.4 %copy-start.111 = (f32[768]{0:T(1024)S(1)}, f32[768]{0:T(1024)}, u32[]{:S(2)}) copy-start(f32[768]{0:T(1024)} %get-tuple-element.927) | copy-start | bytes 9220 | tf_op jit(solution)/shard_map/cond
  92.1 8.4 %copy-start.112 = (f32[768]{0:T(1024)S(1)}, f32[768]{0:T(1024)}, u32[]{:S(2)}) copy-start(f32[768]{0:T(1024)} %get-tuple-element.1097) | copy-start | bytes 9220 | tf_op jit(solution)/shard_map/cond
  103.2 20.7 %collective-permute-start.1 = (bf16[256,768]{1,0:T(8,128)(2,1)S(1)}, bf16[256,768]{1,0:T(8,128)(2,1)S(1)}, u32[]{:S(2)}, u32[]{:S(2)}) collective-permute-start(bf16[256,768]{1,0:T(8,128)(2,1)S(1)} %convert_element_type.804), channel_id=1, source_target_pairs={{0,64},{1,65},{2,66},{3,67},{4,68},{5,69},{6,70},{7,71},{8,72},{9,... | collective-permute-start | bytes 1179656 | tf_op jit(solution)/shard_map/ppermute | solution.py:25
  149.0 116.8 %collective-permute-start.2 = (bf16[256,768]{1,0:T(8,128)(2,1)}, bf16[256,768]{1,0:T(8,128)(2,1)}, u32[]{:S(2)}, u32[]{:S(2)}) collective-permute-start(bf16[256,768]{1,0:T(8,128)(2,1)} %get-tuple-element.687), channel_id=1, source_target_pairs={{64,0},{65,1},{66,2},{67,3},{68,4},{69,5},{70,6},{71,7},{72,8},{73... | collective-permute-start | bytes 1179656 | tf_op jit(solution)/shard_map/ppermute | solution.py:25
  182.8 11.8 %copy-start.9 = (f32[256,768]{1,0:T(8,128)}, f32[256,768]{1,0:T(8,128)S(1)}, u32[]{:S(2)}) copy-start(f32[256,768]{1,0:T(8,128)S(1)} %get-tuple-element.1156) | copy-start | bytes 2359300
  183.1 12.7 %slice-start.34 = ((s8[4718592]{0:T(1024)(128)(4,1)}), s8[4194304]{0:T(1024)(128)(4,1)S(1)}, s32[]{:S(2)}) async-start(s8[4718592]{0:T(1024)(128)(4,1)} %bitcast.579), calls=%async_computation.34 | async-start | bytes 8388608
  185.1 10.7 %slice-start.35 = ((s8[4718592]{0:T(1024)(128)(4,1)}), s8[524288]{0:T(1024)(128)(4,1)S(1)}, s32[]{:S(2)}) async-start(s8[4718592]{0:T(1024)(128)(4,1)} %bitcast.579), calls=%async_computation.35 | async-start | bytes 1048576
  267.8 47.8 %copy-start.34 = (bf16[256,768]{1,0:T(8,128)(2,1)S(1)}, bf16[256,768]{1,0:T(8,128)(2,1)}, u32[]{:S(2)}) copy-start(bf16[256,768]{1,0:T(8,128)(2,1)} %get-tuple-element.884) | copy-start | bytes 1179652
  281.2 22.0 %copy-start.122 = (f32[256]{0:T(256)}, f32[256]{0:T(256)S(1)}, u32[]{:S(2)}) copy-start(f32[256]{0:T(256)S(1)} %broadcast_multiply_fusion.14) | copy-start | bytes 3076
  281.3 22.0 %copy-start.116 = (f32[768]{0:T(1024)}, f32[768]{0:T(1024)S(1)}, u32[]{:S(2)}) copy-start(f32[768]{0:T(1024)S(1)} %get-tuple-element.962) | copy-start | bytes 9220
  284.1 19.1 %copy-start.125 = (f32[256]{0:T(256)}, f32[256]{0:T(256)S(1)}, u32[]{:S(2)}) copy-start(f32[256]{0:T(256)S(1)} %get-tuple-element.1121) | copy-start | bytes 3076
  284.7 11.5 %copy-start.78 = (bf16[256,768]{1,0:T(8,128)(2,1)}, bf16[256,768]{1,0:T(8,128)(2,1)S(1)}, u32[]{:S(2)}) copy-start(bf16[256,768]{1,0:T(8,128)(2,1)S(1)} %get-tuple-element.1215) | copy-start | bytes 1179652
  349.0 56.5 %collective-permute-start.3 = (bf16[256,768]{1,0:T(8,128)(2,1)}, bf16[256,768]{1,0:T(8,128)(2,1)}, u32[]{:S(2)}, u32[]{:S(2)}) collective-permute-start(bf16[256,768]{1,0:T(8,128)(2,1)} %get-tuple-element.1129), channel_id=1, source_target_pairs={{64,0},{65,1},{66,2},{67,3},{68,4},{69,5},{70,6},{71,7},{72,8},{73... | collective-permute-start | bytes 1179656 | tf_op jit(solution)/shard_map/ppermute | solution.py:25
  350.5 51.3 %copy-start.31 = (bf16[256,768]{1,0:T(8,128)(2,1)S(1)}, bf16[256,768]{1,0:T(8,128)(2,1)}, u32[]{:S(2)}) copy-start(bf16[256,768]{1,0:T(8,128)(2,1)} %copy-done.30) | copy-start | bytes 1179652
  370.1 10.5 %slice-start.18 = ((s8[9437184]{0:T(1024)(128)(4,1)}), s8[4194304]{0:T(1024)(128)(4,1)S(1)}, s32[]{:S(2)}) async-start(s8[9437184]{0:T(1024)(128)(4,1)} %bitcast.418), calls=%async_computation.18 | async-start | bytes 8388608 | tf_op jit(solution)/shard_map/cond
  370.1 10.5 %slice-start.19 = ((s8[9437184]{0:T(1024)(128)(4,1)}), s8[4194304]{0:T(1024)(128)(4,1)S(1)}, s32[]{:S(2)}) async-start(s8[9437184]{0:T(1024)(128)(4,1)} %bitcast.418), calls=%async_computation.19 | async-start | bytes 8388608 | tf_op jit(solution)/shard_map/cond
  370.1 10.5 %slice-start.20 = ((s8[9437184]{0:T(1024)(128)(4,1)}), s8[1048576]{0:T(1024)(128)(4,1)S(1)}, s32[]{:S(2)}) async-start(s8[9437184]{0:T(1024)(128)(4,1)} %bitcast.418), calls=%async_computation.20 | async-start | bytes 2097152 | tf_op jit(solution)/shard_map/cond
  378.3 16.8 %slice-start.36 = ((s8[4718592]{0:T(1024)(128)(4,1)}), s8[4194304]{0:T(1024)(128)(4,1)S(1)}, s32[]{:S(2)}) async-start(s8[4718592]{0:T(1024)(128)(4,1)} %bitcast.581), calls=%async_computation.36 | async-start | bytes 8388608 | tf_op jit(solution)/shard_map/cond
  380.5 14.5 %slice-start.37 = ((s8[4718592]{0:T(1024)(128)(4,1)}), s8[524288]{0:T(1024)(128)(4,1)S(1)}, s32[]{:S(2)}) async-start(s8[4718592]{0:T(1024)(128)(4,1)} %bitcast.581), calls=%async_computation.37 | async-start | bytes 1048576 | tf_op jit(solution)/shard_map/cond
  386.1 9.0 %copy-start.145 = (f32[768]{0:T(1024)S(1)}, f32[768]{0:T(1024)}, u32[]{:S(2)}) copy-start(f32[768]{0:T(1024)} %get-tuple-element.896) | copy-start | bytes 9220 | tf_op jit(solution)/shard_map/cond
  411.4 21.6 %copy-start.123 = (f32[256]{0:T(256)}, f32[256]{0:T(256)S(1)}, u32[]{:S(2)}) copy-start(f32[256]{0:T(256)S(1)} %broadcast_multiply_fusion.16) | copy-start | bytes 3076 | tf_op jit(solution)/shard_map/cond
  413.7 19.2 %copy-start.126 = (f32[256]{0:T(256)}, f32[256]{0:T(256)S(1)}, u32[]{:S(2)}) copy-start(f32[256]{0:T(256)S(1)} %get-tuple-element.1124) | copy-start | bytes 3076 | tf_op jit(solution)/shard_map/cond
  415.3 10.1 %copy-start.83 = (bf16[256,768]{1,0:T(8,128)(2,1)}, bf16[256,768]{1,0:T(8,128)(2,1)S(1)}, u32[]{:S(2)}) copy-start(bf16[256,768]{1,0:T(8,128)(2,1)S(1)} %get-tuple-element.1258) | copy-start | bytes 1179652 | tf_op jit(solution)/shard_map/cond
  455.5 28.7 %copy-start.53 = (bf16[256,768]{1,0:T(8,128)(2,1)S(1)}, bf16[256,768]{1,0:T(8,128)(2,1)}, u32[]{:S(2)}) copy-start(bf16[256,768]{1,0:T(8,128)(2,1)} %get-tuple-element.885) | copy-start | bytes 1179652
  502.6 92.1 %copy-start.45 = (f32[256,768]{1,0:T(8,128)S(1)}, f32[256,768]{1,0:T(8,128)}, u32[]{:S(2)}) copy-start(f32[256,768]{1,0:T(8,128)} %get-tuple-element.1288) | copy-start | bytes 2359300
  502.6 92.1 %copy-start.68 = (f32[1,1,256,768]{3,2,1,0:T(8,128)S(1)}, f32[1,1,256,768]{3,2,1,0:T(8,128)}, u32[]{:S(2)}) copy-start(f32[1,1,256,768]{3,2,1,0:T(8,128)} %get-tuple-element.1289) | copy-start | bytes 2359300
  502.6 92.1 %copy-start.69 = (f32[1,1,256,768]{3,2,1,0:T(8,128)S(1)}, f32[1,1,256,768]{3,2,1,0:T(8,128)}, u32[]{:S(2)}) copy-start(f32[1,1,256,768]{3,2,1,0:T(8,128)} %get-tuple-element.1130) | copy-start | bytes 2359300
  502.6 92.1 %copy-start.71 = (f32[1,1,256,768]{3,2,1,0:T(8,128)S(1)}, f32[1,1,256,768]{3,2,1,0:T(8,128)}, u32[]{:S(2)}) copy-start(f32[1,1,256,768]{3,2,1,0:T(8,128)} %copy-done.70) | copy-start | bytes 2359300
  587.6 8.5 %copy-start.96 = (f32[48,768]{1,0:T(8,128)S(1)}, f32[48,768]{1,0:T(8,128)}, u32[]{:S(2)}) copy-start(f32[48,768]{1,0:T(8,128)} %get-tuple-element.735) | copy-start | bytes 442372
  (77 other events, 263.7 us)

commit v2 on v1

--- a/solution.py
+++ b/solution.py
@@ -1,5 +1,3 @@
-from functools import partial
-
 import jax
 import jax.numpy as jnp
 from jax import lax
@@ -11,196 +9,440 @@
 HEADS = 12
 HEAD = 64
 FF = 3072
-SHORT_LEN = 128
-LONG_LEN = 256
 
 
 epsilon = 1e-05
 masked_value = -1000000000.0
 
 
-def passed_along(value, axis, steps):
-    count = lax.axis_size(axis)
-    initial, last = (max(0, -steps), min(count, count - steps))
-    return lax.ppermute(value, axis, [(source, source + steps) for source in range(initial, last)])
-
-
-def layer_norm(values_in, gain_row, shift_row):
-    average = jnp.mean(values_in, -1, keepdims=True)
-    centred = values_in - average
-    spread = jnp.mean(centred * centred, -1, keepdims=True)
-    return centred * lax.rsqrt(spread + epsilon) * gain_row + shift_row
-
-
-def gated_units(gate_up):
-    return jax.nn.gelu(gate_up[:, :FF], approximate=False) * gate_up[:, FF:]
-
-
-def tables(segment, lengths):
-    positions = jnp.arange(LONG_LEN)
-    distance = jnp.abs(positions[:, None] - positions[None, :]).astype(jnp.float32)
-    same_seq = positions[:, None] // segment == positions[None, :] // segment
-    key_len = jnp.repeat(lengths, segment).reshape(-1, LONG_LEN)
-    key_live = (positions % segment)[None, :] < key_len
-    allowed = same_seq[None] & key_live[:, None, :]
-    slopes = jnp.exp2(-8.0 * (jnp.arange(HEADS).astype(jnp.float32) + 1.0) / HEADS)
-    alibi_bias = -slopes[:, None, None] * distance[None]
-    return (allowed, alibi_bias, key_live.reshape(-1))
-
-
-def grouped(rows_in, groups):
-    return rows_in.reshape(groups, LONG_LEN, HEADS, HEAD)
-
-
-def masked_scores(query, keys, allowed, alibi_bias):
-    groups = allowed.shape[0]
-    scores = jnp.einsum(
-        "gqhd,gkhd->ghqk",
-        grouped(query, groups),
-        grouped(keys, groups),
-        preferred_element_type=jnp.float32,
+ROWS_DEV = 256
+BLOCK = 512
+BAND = 32
+
+
+def dot_nn(lhs, rhs):
+    return jnp.dot(lhs, rhs, preferred_element_type=jnp.float32)
+
+
+def dot_nt(lhs, rhs):
+    return lax.dot_general(lhs, rhs, (((1,), (1,)), ((), ())), preferred_element_type=jnp.float32)
+
+
+def dot_tn(lhs, rhs):
+    return lax.dot_general(lhs, rhs, (((0,), (0,)), ((), ())), preferred_element_type=jnp.float32)
+
+
+def f32(value):
+    return value.astype(jnp.float32)
+
+
+def bf16(value):
+    return value.astype(jnp.bfloat16)
+
+
+def fold_rows(value):
+    return jnp.sum(value.reshape(value.shape[0] // 8, 8, value.shape[1]), 0)
+
+
+def gelu_terms(gate):
+    cdf = 0.5 * (1.0 + lax.erf(gate * 0.7071067811865476))
+    density = jnp.exp(-0.5 * gate * gate) * 0.3989422804014327
+    return gate * cdf, cdf + gate * density
+
+
+def layers_kernel(
+    short_lens, long_lens, slopes, tokens, cotangent, w_qkv, w_out, w_gate_up, w_down, gains, biases,
+    boundary, o_at, o_mt, o_nt, o_ht, o_gq, o_go, o_gg, o_gf, o_vec,
+    wq, wo, wg, wd, x_s, g_s, qkv_s, p_s, mixed_s, low_s, n1_s, n2_s, r1_s, r2_s, gu_s, at_s, mt_s, nt_s, ht_s,
+    gf_s, ga_s, send_s, out_s, acc_s, f_s, gate_s, up_s, dist_s, mask_s, vec_s,
+    w_sem, x_sem, g_sem, out_sem, spill_sem, f_send, f_recv, b_send, b_recv,
+):
+    sec = lax.axis_index("section")
+    first = sec == 0
+    second = sec == 1
+    w_copies = [
+        pltpu.make_async_copy(w_qkv, wq, w_sem.at[0]),
+        pltpu.make_async_copy(w_out, wo, w_sem.at[1]),
+        pltpu.make_async_copy(w_gate_up, wg, w_sem.at[2]),
+        pltpu.make_async_copy(w_down, wd, w_sem.at[3]),
+    ]
+
+    def token_copy(m):
+        return pltpu.make_async_copy(tokens.at[m], x_s.at[m], x_sem.at[m])
+
+    def cot_copy(m):
+        return pltpu.make_async_copy(cotangent.at[m], g_s.at[m], g_sem.at[m])
+
+    def across(src, dst, send, recv):
+        return pltpu.make_async_remote_copy(
+            src_ref=src, dst_ref=dst, send_sem=send, recv_sem=recv,
+            device_id={"section": 1 - sec}, device_id_type=pl.DeviceIdType.MESH,
+        )
+
+    def hand_on(m):
+        return across(send_s.at[m], x_s.at[m], f_send.at[m], f_recv.at[m])
+
+    def hand_back(m):
+        return across(send_s.at[m], g_s.at[m], b_send.at[m], b_recv.at[m])
+
+    @pl.when(first)
+    def _():
+        token_copy(0).start()
+
+    w_copies[0].start()
+    w_copies[1].start()
+
+    @pl.when(first)
+    def _():
+        token_copy(1).start()
+
+    w_copies[2].start()
+    w_copies[3].start()
+
+    @pl.when(second)
+    def _():
+        cot_copy(0).start()
+        cot_copy(1).start()
+
+    barrier = pltpu.get_barrier_semaphore()
+    pl.semaphore_signal(
+        barrier, inc=1, device_id={"section": 1 - sec}, device_id_type=pl.DeviceIdType.MESH
     )
-    scores = scores * HEAD ** (-0.5) + alibi_bias[None]
-    return jnp.where(allowed[:, None], scores, masked_value)
-
-
-def forward(section_in, params, layout):
-    weight_qkv, weight_out, weight_gate_up, weight_down, gain_rows, bias_rows = params
-    allowed, alibi_bias, unused = layout
-    rows_dev = section_in.shape[0]
-    groups = allowed.shape[0]
-    projected = jnp.dot(section_in, weight_qkv, preferred_element_type=jnp.float32)
-    query = (projected[:, :D] + bias_rows[0]).astype(jnp.bfloat16)
-    keys = projected[:, D : 2 * D].astype(jnp.bfloat16)
-    values = (projected[:, 2 * D :] + bias_rows[1]).astype(jnp.bfloat16)
-    scores = masked_scores(query, keys, allowed, alibi_bias)
-    peak = jnp.max(scores, -1, keepdims=True)
-    expo = jnp.exp(scores - peak)
-    totals = jnp.sum(expo, -1, keepdims=True)
-    probs_low = (expo / totals).astype(jnp.bfloat16)
-    log_sums = (peak + jnp.log(totals))[..., 0]
-    mixed = jnp.einsum(
-        "ghqk,gkhd->gqhd", probs_low, grouped(values, groups), preferred_element_type=jnp.float32
-    )
-    mixed = mixed.reshape(rows_dev, D).astype(jnp.bfloat16)
-    resid_one = section_in.astype(jnp.float32) + (
-        jnp.dot(mixed, weight_out, preferred_element_type=jnp.float32) + bias_rows[2]
-    )
-    normed = layer_norm(resid_one, gain_rows[0], bias_rows[3])
-    normed_low = normed.astype(jnp.bfloat16)
-    gate_up = jnp.dot(normed_low, weight_gate_up, preferred_element_type=jnp.float32)
-    hidden = gated_units(gate_up).astype(jnp.bfloat16)
-    resid_two = normed + (
-        jnp.dot(hidden, weight_down, preferred_element_type=jnp.float32) + bias_rows[4]
-    )
-    result = layer_norm(resid_two, gain_rows[1], bias_rows[5])
-    return (
-        result,
-        (query, keys, values, log_sums, mixed, resid_one, normed_low, gate_up, hidden, resid_two),
-    )
-
-
-def forward_only(section_in, params, layout):
-    return forward(section_in, params, layout)[0]
-
-
-def back_ffn(incoming, saved, params):
-    weight_qkv, weight_out, weight_gate_up, weight_down, gain_rows, bias_rows = params
-    query, keys, values, log_sums, mixed, resid_one, normed_low, gate_up, hidden, resid_two = saved
-    unused, pullback = jax.vjp(layer_norm, resid_two, gain_rows[1], bias_rows[5])
-    grad_resid_two, grad_gain_two, grad_shift_two = pullback(incoming)
-    grad_ffn = grad_resid_two.astype(jnp.bfloat16)
-    grad_hidden = jnp.dot(grad_ffn, weight_down.T, preferred_element_type=jnp.float32)
-    unused, pullback = jax.vjp(gated_units, gate_up)
-    grad_gate_up = pullback(grad_hidden)[0].astype(jnp.bfloat16)
-    grad_normed = (
-        jnp.dot(grad_gate_up, weight_gate_up.T, preferred_element_type=jnp.float32) + grad_resid_two
-    )
-    unused, pullback = jax.vjp(layer_norm, resid_one, gain_rows[0], bias_rows[3])
-    grad_resid_one, grad_gain_one, grad_shift_one = pullback(grad_normed)
-    zero_row = jnp.zeros_like(grad_shift_one)
-    grad_vectors = jnp.stack(
-        [
-            zero_row,
-            zero_row,
-            zero_row,
-            grad_shift_one,
-            jnp.sum(grad_ffn.astype(jnp.float32), 0),
-            grad_shift_two,
+    pl.semaphore_wait(barrier, 1)
+
+    vec_s[...] = jnp.zeros_like(vec_s)
+    rows_j = lax.broadcasted_iota(jnp.int32, (256, 256), 0)
+    cols_i = lax.broadcasted_iota(jnp.int32, (256, 256), 1)
+    dist_s[...] = jnp.abs(rows_j - cols_i).astype(jnp.float32)
+    length_a, length_b, length_long = short_lens[0], short_lens[1], long_lens[0]
+    for m in range(2):
+        if m == 0:
+            limit = jnp.where(rows_j < 128, length_a, length_b + 128)
+            apart = jnp.where((rows_j >> 7) == (cols_i >> 7), 0, 1024)
+            ok = rows_j + apart < limit
+        else:
+            ok = rows_j < length_long
+        mask_s[m] = jnp.where(ok, 1.0, 0.0)
+
+    def band(k):
+        return pl.ds(pl.multiple_of(k * BAND, BAND), BAND)
+
+    def normalise(value):
+        average = jnp.mean(value, -1, keepdims=True)
+        centred = value - average
+        inverse = lax.rsqrt(jnp.mean(centred * centred, -1, keepdims=True) + epsilon)
+        return centred * inverse, inverse
+
+    def spill(m):
+        cols = pl.ds(m * 256, 256)
+        return [
+            pltpu.make_async_copy(at_s.at[m], o_at.at[m], spill_sem.at[m, 0]),
+            pltpu.make_async_copy(mt_s.at[m], o_mt.at[m], spill_sem.at[m, 1]),
+            pltpu.make_async_copy(nt_s.at[m], o_nt.at[m], spill_sem.at[m, 2]),
+            pltpu.make_async_copy(ht_s.at[m], o_ht.at[m], spill_sem.at[m, 3]),
         ]
-    )
-    grad_gain_rows = jnp.stack([grad_gain_one, grad_gain_two])
-    return (grad_resid_one, (grad_gate_up, grad_ffn, grad_vectors, grad_gain_rows, normed_low, hidden))
-
-
-def back_attn(grad_resid_one, saved, section_in, params, layout):
-    weight_qkv, weight_out, weight_gate_up, weight_down, gain_rows, bias_rows = params
-    allowed, alibi_bias, unused = layout
-    query, keys, values, log_sums, mixed, resid_one, normed_low, gate_up, hidden, resid_two = saved
-    rows_dev = section_in.shape[0]
-    groups = allowed.shape[0]
-    grad_attn = grad_resid_one.astype(jnp.bfloat16)
-    grad_mixed = jnp.dot(grad_attn, weight_out.T, preferred_element_type=jnp.float32).astype(
-        jnp.bfloat16
-    )
-    grad_mixed_g = grouped(grad_mixed, groups)
-    probs = jnp.exp(masked_scores(query, keys, allowed, alibi_bias) - log_sums[..., None])
-    grad_probs = jnp.einsum(
-        "gqhd,gkhd->ghqk", grad_mixed_g, grouped(values, groups), preferred_element_type=jnp.float32
-    )
-    grad_scores = (probs * (grad_probs - jnp.sum(probs * grad_probs, -1, keepdims=True))).astype(
-        jnp.bfloat16
-    )
-    grad_values = jnp.einsum(
-        "ghqk,gqhd->gkhd",
-        probs.astype(jnp.bfloat16),
-        grad_mixed_g,
-        preferred_element_type=jnp.float32,
-    )
-    grad_values = grad_values.reshape(rows_dev, D).astype(jnp.bfloat16)
-    grad_query = jnp.einsum(
-        "ghqk,gkhd->gqhd", grad_scores, grouped(keys, groups), preferred_element_type=jnp.float32
-    ) * HEAD ** (-0.5)
-    grad_query = grad_query.reshape(rows_dev, D).astype(jnp.bfloat16)
-    grad_keys = jnp.einsum(
-        "ghqk,gqhd->gkhd", grad_scores, grouped(query, groups), preferred_element_type=jnp.float32
-    ) * HEAD ** (-0.5)
-    grad_keys = grad_keys.reshape(rows_dev, D).astype(jnp.bfloat16)
-    grad_projected = jnp.concatenate([grad_query, grad_keys, grad_values], 1)
-    grad_section_in = (
-        jnp.dot(grad_projected, weight_qkv.T, preferred_element_type=jnp.float32) + grad_resid_one
-    )
-    zero_row = jnp.zeros((D,), jnp.float32)
-    grad_vectors = jnp.stack(
-        [
-            jnp.sum(grad_query.astype(jnp.float32), 0),
-            jnp.sum(grad_values.astype(jnp.float32), 0),
-            jnp.sum(grad_attn.astype(jnp.float32), 0),
-            zero_row,
-            zero_row,
-            zero_row,
+
+    def spill_back(m):
+        return [
+            pltpu.make_async_copy(qkv_s.at[m], o_gq.at[m], spill_sem.at[m, 4]),
+            pltpu.make_async_copy(ga_s.at[m], o_go.at[m], spill_sem.at[m, 5]),
+            pltpu.make_async_copy(gu_s.at[m], o_gg.at[m], spill_sem.at[m, 6]),
+            pltpu.make_async_copy(gf_s.at[m], o_gf.at[m], spill_sem.at[m, 7]),
         ]
-    )
-    return (grad_section_in, (grad_projected, grad_attn, grad_vectors, mixed))
-
-
-def silent(function):
-
-    def quiet(*operands):
-        return jax.tree.map(jnp.zeros_like, function(*operands))
-
-    return quiet
-
-
-def by_section(period, builder):
-    branches = []
-    for section_id in (0, 1):
-        micro = period - section_id
-        if 0 <= micro < 2:
-            branches.append(builder(micro))
-        else:
-            branches.append(silent(builder(0)))
-    return branches
+
+    def out_copy(m):
+        return pltpu.make_async_copy(out_s.at[m], boundary.at[m], out_sem.at[m])
+
+    lanes = lax.broadcasted_iota(jnp.int32, (256, 128), 1)
+
+    def forward(m, carry):
+        @pl.when(first)
+        def _():
+            token_copy(m).wait()
+
+        @pl.when(second)
+        def _():
+            hand_on(m).wait_recv()
+
+        @pl.when(m == 0)
+        def _():
+            w_copies[0].wait()
+
+        x = x_s[m]
+        at_s[m] = x.T
+        query = dot_nn(x, wq[:, 0:768]) + biases[0:1]
+        qkv_s[m, :, 0:768] = bf16(f32(bf16(query)) * 0.125)
+        qkv_s[m, :, 768:1536] = bf16(dot_nn(x, wq[:, 768:1536]))
+        qkv_s[m, :, 1536:2304] = bf16(dot_nn(x, wq[:, 1536:2304]) + biases[1:2])
+
+        def heads(hp, carry):
+            lane0 = pl.multiple_of(hp * 128, 128)
+            q2 = qkv_s[m, :, pl.ds(lane0, 128)]
+            k2 = qkv_s[m, :, pl.ds(lane0 + 768, 128)]
+            v2 = qkv_s[m, :, pl.ds(lane0 + 1536, 128)]
+            outs = []
+            for e in range(2):
+                keep = (lanes < 64) if e == 0 else (lanes >= 64)
+                qm = jnp.where(keep, q2, jnp.zeros_like(q2))
+                scores = dot_nt(k2, qm) - slopes[2 * hp + e] * dist_s[...]
+                scores = jnp.where(mask_s[m] > 0.5, scores, masked_value)
+                expo = jnp.exp(scores - jnp.max(scores, 0, keepdims=True))
+                total = jnp.sum(expo, 0, keepdims=True)
+                probs = bf16(expo * (1.0 / total))
+                p_s[m, 2 * hp + e] = probs
+                outs.append(dot_tn(probs, v2))
+            mixed_s[m, :, pl.ds(lane0, 128)] = bf16(jnp.where(lanes < 64, outs[0], outs[1]))
+            return carry
+
+        lax.fori_loop(0, 6, heads, 0)
+
+        @pl.when(m == 0)
+        def _():
+            w_copies[1].wait()
+
+        mixed = mixed_s[m]
+        mt_s[m] = mixed.T
+        acc_s[...] = dot_nn(mixed, wo[...])
+
+        def norm_one(k, carry):
+            r = band(k)
+            value = f32(x_s[m, r]) + (acc_s[r] + biases[2:3])
+            unit, inverse = normalise(value)
+            normed = unit * gains[0:1] + biases[3:4]
+            n1_s[m, r] = bf16(unit)
+            r1_s[m, r] = inverse
+            f_s[r] = normed
+            low_s[r] = bf16(normed)
+            return carry
+
+        lax.fori_loop(0, 8, norm_one, 0)
+
+        @pl.when(m == 0)
+        def _():
+            w_copies[2].wait()
+            w_copies[3].wait()
+
+        nt_s[m] = low_s[...].T
+        acc_s[...] = jnp.zeros_like(acc_s)
+
+        def ffn(jb, carry):
+            c0 = pl.multiple_of(jb * BLOCK, BLOCK)
+            low = low_s[...]
+            gate_s[...] = dot_nn(low, wg[:, pl.ds(c0, BLOCK)])
+            up_s[...] = dot_nn(low, wg[:, pl.ds(c0 + FF, BLOCK)])
+            for k in range(8):
+                r = pl.ds(k * BAND, BAND)
+                gate, up = gate_s[r], up_s[r]
+                act, slope = gelu_terms(gate)
+                gu_s[m, r, pl.ds(c0, BLOCK)] = bf16(up * slope)
+                gu_s[m, r, pl.ds(c0 + FF, BLOCK)] = bf16(act)
+                gate_s[r] = act * up
+            hid = bf16(gate_s[...])
+            ht_s[m, pl.ds(c0, BLOCK)] = hid.T
+            acc_s[...] += dot_nn(hid, wd[pl.ds(c0, BLOCK)])
+            return carry
+
+        lax.fori_loop(0, 6, ffn, 0)
+
+        def norm_two(k, carry):
+            r = band(k)
+            value = f_s[r] + (acc_s[r] + biases[4:5])
+            unit, inverse = normalise(value)
+            n2_s[m, r] = bf16(unit)
+            r2_s[m, r] = inverse
+            result = unit * gains[1:2] + biases[5:6]
+            out_s[m, r] = result
+            send_s[m, r] = bf16(result)
+            return carry
+
+        lax.fori_loop(0, 8, norm_two, 0)
+
+        @pl.when(first)
+        def _():
+            hand_on(m).start()
+
+        @pl.when(second)
+        def _():
+            out_copy(m).start()
+
+        for copy in spill(m):
+            copy.start()
+        return carry
+
+    lax.fori_loop(0, 2, forward, 0)
+
+    def norm_back(grad, unit, inverse, gain):
+        scaled = grad * gain
+        mean_one = jnp.mean(scaled, -1, keepdims=True)
+        mean_two = jnp.mean(scaled * unit, -1, keepdims=True)
+        return inverse * (scaled - mean_one - unit * mean_two)
+
+    def backward(m, carry):
+        @pl.when(first)
+        def _():
+            hand_on(m).wait_send()
+            hand_back(m).wait_recv()
+
+        @pl.when(second)
+        def _():
+            cot_copy(m).wait()
+            out_copy(m).wait()
+
+        def back_two(k, carry):
+            r = band(k)
+            row = lax.broadcasted_iota(jnp.int32, (BAND, 1), 0) + k * BAND
+            limit = jnp.where(m == 0, jnp.where(row < 128, length_a, length_b + 128), length_long)
+            live = jnp.where((row < limit) | first, 1.0, 0.0)
+            grad = f32(g_s[m, r]) * live
+            unit = f32(n2_s[m, r])
+            vec_s[1] += fold_rows(grad * unit)
+            vec_s[7] += fold_rows(grad)
+            grad_in = norm_back(grad, unit, r2_s[m, r], gains[1:2])
+            f_s[r] = grad_in
+            low = bf16(grad_in)
+            gf_s[m, r] = low
+            vec_s[6] += fold_rows(f32(low))
+            return carry
+
+        lax.fori_loop(0, 8, back_two, 0)
+        acc_s[...] = jnp.zeros_like(acc_s)
+
+        def ffn_back(jb, carry):
+            c0 = pl.multiple_of(jb * BLOCK, BLOCK)
+            gate_s[...] = dot_nt(gf_s[m], wd[pl.ds(c0, BLOCK)])
+            for k in range(8):
+                r = pl.ds(k * BAND, BAND)
+                hid = gate_s[r]
+                gu_s[m, r, pl.ds(c0, BLOCK)] = bf16(hid * f32(gu_s[m, r, pl.ds(c0, BLOCK)]))
+                gu_s[m, r, pl.ds(c0 + FF, BLOCK)] = bf16(hid * f32(gu_s[m, r, pl.ds(c0 + FF, BLOCK)]))
+            acc_s[...] += dot_nt(gu_s[m, :, pl.ds(c0, BLOCK)], wg[:, pl.ds(c0, BLOCK)])
+            acc_s[...] += dot_nt(gu_s[m, :, pl.ds(c0 + FF, BLOCK)], wg[:, pl.ds(c0 + FF, BLOCK)])
+            return carry
+
+        lax.fori_loop(0, 6, ffn_back, 0)
+
+        def back_one(k, carry):
+            r = band(k)
+            grad = acc_s[r] + f_s[r]
+            unit = f32(n1_s[m, r])
+            vec_s[0] += fold_rows(grad * unit)
+            vec_s[5] += fold_rows(grad)
+            grad_in = norm_back(grad, unit, r1_s[m, r], gains[0:1])
+            f_s[r] = grad_in
+            low = bf16(grad_in)
+            ga_s[m, r] = low
+            vec_s[4] += fold_rows(f32(low))
+            return carry
+
+        lax.fori_loop(0, 8, back_one, 0)
+        low_s[...] = bf16(dot_nt(ga_s[m], wo[...]))
+
+        def heads_back(hp, carry):
+            lane0 = pl.multiple_of(hp * 128, 128)
+            q2 = qkv_s[m, :, pl.ds(lane0, 128)]
+            k2 = qkv_s[m, :, pl.ds(lane0 + 768, 128)]
+            v2 = qkv_s[m, :, pl.ds(lane0 + 1536, 128)]
+            do2 = low_s[:, pl.ds(lane0, 128)]
+            dq, dk, dv = [], [], []
+            for e in range(2):
+                keep = (lanes < 64) if e == 0 else (lanes >= 64)
+                vm = jnp.where(keep, v2, jnp.zeros_like(v2))
+                probs = p_s[m, 2 * hp + e]
+                grad_probs = dot_nt(vm, do2)
+                weighted = f32(probs) * grad_probs
+                total = jnp.sum(weighted, 0, keepdims=True)
+                grad_scores = bf16(weighted - f32(probs) * total)
+                dv.append(dot_nn(probs, do2))
+                dk.append(dot_nn(grad_scores, q2))
+                dq.append(dot_tn(grad_scores, k2))
+            grad_q = bf16(jnp.where(lanes < 64, dq[0], dq[1]) * 0.125)
+            grad_k = bf16(jnp.where(lanes < 64, dk[0], dk[1]))
+            grad_v = bf16(jnp.where(lanes < 64, dv[0], dv[1]))
+            vec_s[2, :, pl.ds(lane0, 128)] += fold_rows(f32(grad_q))
+            vec_s[3, :, pl.ds(lane0, 128)] += fold_rows(f32(grad_v))
+            qkv_s[m, :, pl.ds(lane0, 128)] = grad_q
+            qkv_s[m, :, pl.ds(lane0 + 768, 128)] = grad_k
+            qkv_s[m, :, pl.ds(lane0 + 1536, 128)] = grad_v
+            return carry
+
+        lax.fori_loop(0, 6, heads_back, 0)
+        grad_a = dot_nt(qkv_s[m], wq[...]) + f_s[...]
+
+        @pl.when(second)
+        def _():
+            send_s[m] = bf16(grad_a)
+            hand_back(m).start()
+
+        @pl.when(first)
+        def _():
+            out_s[m] = grad_a
+            out_copy(m).start()
+
+        for copy in spill_back(m):
+            copy.start()
+        return carry
+
+    lax.fori_loop(0, 2, backward, 0)
+    for k in range(8):
+        o_vec[k:k + 1] = jnp.sum(vec_s[k], 0, keepdims=True)
+
+    for m in range(2):
+        for copy in spill(m) + spill_back(m):
+            copy.wait()
+
+        @pl.when(second)
+        def _():
+            hand_back(m).wait_send()
+
+        @pl.when(first)
+        def _():
+            out_copy(m).wait()
+
+
+def run_layers(short_lens, long_lens, tokens, cotangent, w_qkv, w_out, w_gate_up, w_down, gains, biases):
+    low, wide = jnp.bfloat16, jnp.float32
+    hbm = pl.BlockSpec(memory_space=pl.ANY)
+    vmem = pl.BlockSpec(memory_space=pltpu.VMEM)
+    smem = pl.BlockSpec(memory_space=pltpu.SMEM)
+    dma = pltpu.SemaphoreType.DMA
+    slopes = jnp.exp2(-8.0 * (jnp.arange(HEADS).astype(wide) + 1.0) / HEADS)
+
+    def of(shape, dtype):
+        return pltpu.VMEM(shape, dtype)
+
+    return pl.pallas_call(
+        layers_kernel,
+        out_shape=[
+            jax.ShapeDtypeStruct((2, 256, 768), wide),
+            jax.ShapeDtypeStruct((2, 768, 256), low),
+            jax.ShapeDtypeStruct((2, 768, 256), low),
+            jax.ShapeDtypeStruct((2, 768, 256), low),
+            jax.ShapeDtypeStruct((2, 3072, 256), low),
+            jax.ShapeDtypeStruct((2, 256, 2304), low),
+            jax.ShapeDtypeStruct((2, 256, 768), low),
+            jax.ShapeDtypeStruct((2, 256, 6144), low),
+            jax.ShapeDtypeStruct((2, 256, 768), low),
+            jax.ShapeDtypeStruct((8, 768), wide),
+        ],
+        in_specs=[smem] * 3 + [hbm] * 6 + [vmem] * 2,
+        out_specs=[hbm] * 9 + [vmem],
+        scratch_shapes=[
+            of((768, 2304), low), of((768, 768), low), of((768, 6144), low), of((3072, 768), low),
+            of((2, 256, 768), low), of((2, 256, 768), low), of((2, 256, 2304), low), of((2, 12, 256, 256), low),
+            of((2, 256, 768), low), of((256, 768), low), of((2, 256, 768), low), of((2, 256, 768), low),
+            of((2, 256, 1), wide), of((2, 256, 1), wide), of((2, 256, 6144), low),
+            of((2, 768, 256), low), of((2, 768, 256), low), of((2, 768, 256), low), of((2, 3072, 256), low),
+            of((2, 256, 768), low), of((2, 256, 768), low), of((2, 256, 768), low), of((2, 256, 768), wide),
+            of((256, 768), wide), of((256, 768), wide), of((256, 512), wide), of((256, 512), wide),
+            of((256, 256), wide), of((2, 256, 256), wide), of((8, 8, 768), wide),
+            dma((4,)), dma((2,)), dma((2,)), dma((2,)), dma((2, 8)), dma((2,)), dma((2,)), dma((2,)), dma((2,)),
+        ],
+        compiler_params=pltpu.CompilerParams(
+            collective_id=1, has_side_effects=True, vmem_limit_bytes=60 * 1024 * 1024
+        ),
+        cost_estimate=pl.CostEstimate(flops=2 * 10 ** 10, bytes_accessed=4 * 10 ** 7, transcendentals=10 ** 7),
+        name="run_layers",
+    )(short_lens, long_lens, slopes, tokens, cotangent, w_qkv, w_out, w_gate_up, w_down, gains, biases)
 
 
 S_SLOTS = 5
@@ -242,27 +484,32 @@
         )
 
     half = 512
-    local = [
-        pltpu.make_async_copy(xn, t_n.at[:, pl.ds(0, half)], in_sem.at[0]),
-        pltpu.make_async_copy(gg.at[:, pl.ds(core * 3072, 3072)], w_g.at[pl.ds(0, half)], in_sem.at[1]),
-        pltpu.make_async_copy(xa, t_a.at[:, pl.ds(0, half)], in_sem.at[2]),
-        pltpu.make_async_copy(gq.at[:, pl.ds(core * 1152, 1152)], w_q.at[pl.ds(0, half)], in_sem.at[3]),
-        pltpu.make_async_copy(xm, t_m.at[:, pl.ds(0, half)], in_sem.at[4]),
-        pltpu.make_async_copy(go.at[:, pl.ds(core * 384, 384)], w_o.at[pl.ds(0, half)], in_sem.at[5]),
-        pltpu.make_async_copy(xh.at[:, core], t_h.at[:, :, pl.ds(0, half)], in_sem.at[6]),
-        pltpu.make_async_copy(gf, w_f.at[pl.ds(0, half)], in_sem.at[7]),
-    ]
     other = 1 - core
-    across = [
-        remote(xn, t_n.at[:, pl.ds(half, half)], peer_send.at[0], peer_recv.at[0], peer_core),
-        remote(gg.at[:, pl.ds(other * 3072, 3072)], w_g.at[pl.ds(half, half)], peer_send.at[1], peer_recv.at[1], peer_core),
-        remote(xa, t_a.at[:, pl.ds(half, half)], peer_send.at[2], peer_recv.at[2], peer_core),
-        remote(gq.at[:, pl.ds(other * 1152, 1152)], w_q.at[pl.ds(half, half)], peer_send.at[3], peer_recv.at[3], peer_core),
-        remote(xm, t_m.at[:, pl.ds(half, half)], peer_send.at[4], peer_recv.at[4], peer_core),
-        remote(go.at[:, pl.ds(other * 384, 384)], w_o.at[pl.ds(half, half)], peer_send.at[5], peer_recv.at[5], peer_core),
-        remote(xh.at[:, other], t_h.at[:, :, pl.ds(half, half)], peer_send.at[6], peer_recv.at[6], peer_core),
-        remote(gf, w_f.at[pl.ds(half, half)], peer_send.at[7], peer_recv.at[7], peer_core),
-    ]
+
+    def operand_pair(k):
+        parts = []
+        for m in range(2):
+            to = pl.ds(m * 256, 256)
+            to_far = pl.ds(half + m * 256, 256)
+            src_own, src_far, dst_own, dst_far = (
+                (xn.at[m], xn.at[m], t_n.at[:, to], t_n.at[:, to_far]),
+                (gg.at[m, :, pl.ds(core * 3072, 3072)], gg.at[m, :, pl.ds(other * 3072, 3072)], w_g.at[to], w_g.at[to_far]),
+                (xa.at[m], xa.at[m], t_a.at[:, to], t_a.at[:, to_far]),
+                (gq.at[m, :, pl.ds(core * 1152, 1152)], gq.at[m, :, pl.ds(other * 1152, 1152)], w_q.at[to], w_q.at[to_far]),
+                (xm.at[m], xm.at[m], t_m.at[:, to], t_m.at[:, to_far]),
+                (go.at[m, :, pl.ds(core * 384, 384)], go.at[m, :, pl.ds(other * 384, 384)], w_o.at[to], w_o.at[to_far]),
+                (xh.at[m, :, core], xh.at[m, :, other], t_h.at[:, :, to], t_h.at[:, :, to_far]),
+                (gf.at[m], gf.at[m], w_f.at[to], w_f.at[to_far]),
+            )[k]
+            parts.append((
+                pltpu.make_async_copy(src_own, dst_own, in_sem.at[k, m]),
+                remote(src_far, dst_far, peer_send.at[k, m], peer_recv.at[k, m], peer_core),
+            ))
+        return parts
+
+    pairs = [operand_pair(k) for k in range(8)]
+    local = [pair[0] for both in pairs for pair in both]
+    across = [pair[1] for both in pairs for pair in both]
     for copy in local:
         copy.start()
     barrier = pltpu.get_barrier_semaphore()
@@ -358,8 +605,9 @@
 
     def wait_operands(*which):
         for k in which:
-            local[k].wait()
-            across[k].wait()
+            for pair in pairs[k]:
+                pair[0].wait()
+                pair[1].wait()
 
     def store_rows(j, halves):
         mine = j % OWN_SLOTS
@@ -409,9 +657,6 @@
             rhs = w_f[:, pl.ds(pl.multiple_of((j - 9) * 256, 256), 256)]
             result = product(t_h[...].reshape(1536, 1024), rhs).reshape(16, 2, 48, 256)
             store_rows(j, [result[:, 0], result[:, 1]])
-
-    def f32(value):
-        return value.astype(jnp.float32)
 
     def step(i, carry):
         @pl.when(i < N_CHUNKS)
@@ -612,7 +857,7 @@
             pltpu.VMEM((s, 2, 16, 256), wide),
             pltpu.VMEM((5, 8, 768), wide),
             pltpu.VMEM((8, 8, 768), wide),
-            dma((8,)), dma((8,)), dma((8,)),
+            dma((8, 2)), dma((8, 2)), dma((8, 2)),
             dma((s, 4)), dma((s, 2)), dma((s, 2, 2)), dma((s, 2)),
             dma((s, 4)), dma((s, 2)), dma((s, 2, 2)), dma((s, 2)),
             dma((s,)), dma((s,)), dma((s,)), dma((s,)),
@@ -623,80 +868,18 @@
         ),
         cost_estimate=pl.CostEstimate(flops=10 ** 10, bytes_accessed=2 * 10 ** 7, transcendentals=0),
         name="reduce_weights",
-    )(xa, xm, xn, xh.reshape(32, 2, 48, 512), gq, go, gg, gf, vec)
+    )(xa, xm, xn, xh.reshape(2, 32, 2, 48, 256), gq, go, gg, gf, vec)
 
 
 def on_device(
     tokens, cotangent, short_lens, long_lens, w_qkv, w_out, w_gate_up, w_down, gains, biases
 ):
-    first_section = lax.axis_index("section") == 0
-    params = (w_qkv[0], w_out[0], w_gate_up[0], w_down[0], gains[0], biases[0])
-    rows_dev = tokens.shape[1]
-    layouts = (tables(SHORT_LEN, short_lens), tables(LONG_LEN, long_lens))
-    received = jnp.zeros((rows_dev, D), jnp.bfloat16)
-    section_inputs = []
-    finals = []
-    for period in range(3):
-        section_in = jnp.where(first_section, tokens[min(period, 1)], received)
-        branches = by_section(
-            period, lambda micro: partial(forward_only, params=params, layout=layouts[micro])
-        )
-        result = lax.cond(first_section, branches[0], branches[1], section_in)
-        section_inputs.append(section_in)
-        finals.append(result)
-        if period < 2:
-            received = passed_along(result.astype(jnp.bfloat16), "section", 1)
-    cot_rows = [
-        cotangent[micro].astype(jnp.float32) * layouts[micro][2][:, None].astype(jnp.float32)
-        for micro in range(2)
-    ]
-    grad_gain_rows = jnp.zeros(params[4].shape, jnp.float32)
-    grad_vectors = jnp.zeros(params[5].shape, jnp.float32)
-    operands = [None, None, None]
-    returned = jnp.zeros((rows_dev, D), jnp.bfloat16)
-    grad_rows = [None, None]
-    for rewind in range(3):
-        period = 2 - rewind
-        incoming = jnp.where(
-            first_section, returned.astype(jnp.float32), cot_rows[max(1 - rewind, 0)]
-        )
-        branches = by_section(
-            period, lambda micro: partial(forward, params=params, layout=layouts[micro])
-        )
-        saved = lax.cond(first_section, branches[0], branches[1], section_inputs[period])[1]
-        branches = by_section(period, lambda micro: partial(back_ffn, params=params))
-        grad_resid_one, ffn_terms = lax.cond(
-            first_section, branches[0], branches[1], incoming, saved
-        )
-        grad_vectors = grad_vectors + ffn_terms[2]
-        grad_gain_rows = grad_gain_rows + ffn_terms[3]
-        branches = by_section(
-            period, lambda micro: partial(back_attn, params=params, layout=layouts[micro])
-        )
-        grad_section_in, attn_terms = lax.cond(
-            first_section, branches[0], branches[1], grad_resid_one, saved, section_inputs[period]
-        )
-        operands[period] = (
-            section_inputs[period], attn_terms[3], ffn_terms[4], ffn_terms[5],
-            attn_terms[0], attn_terms[1], ffn_terms[0], ffn_terms[1],
-        )
-        grad_vectors = grad_vectors + attn_terms[2]
-        if rewind < 2:
-            returned = passed_along(grad_section_in.astype(jnp.bfloat16), "section", -1)
-        if rewind > 0:
-            grad_rows[period] = grad_section_in
-    boundary = jnp.where(
-        first_section, jnp.stack([grad_rows[0], grad_rows[1]]), jnp.stack([finals[1], finals[2]])
-    )[None]
-    early = jax.tree.map(lambda u, v: jnp.where(first_section, u, v), operands[0], operands[1])
-    late = jax.tree.map(lambda u, v: jnp.where(first_section, u, v), operands[1], operands[2])
-    both = [jnp.concatenate(pair, 0) for pair in zip(early, late)]
-    vec = jnp.concatenate([grad_gain_rows, grad_vectors], 0)
-    g_qkv, g_out, g_gu, g_dn, g_vec = reduce_weights(
-        both[0].T, both[1].T, both[2].T, both[3].T, both[4], both[5], both[6], both[7], vec
+    boundary, x_a, x_m, x_n, x_h, g_q, g_o, g_g, g_f, vec = run_layers(
+        short_lens, long_lens, tokens, cotangent, w_qkv[0], w_out[0], w_gate_up[0], w_down[0], gains[0], biases[0]
     )
+    g_qkv, g_out, g_gu, g_dn, g_vec = reduce_weights(x_a, x_m, x_n, x_h, g_q, g_o, g_g, g_f, vec)
     mine = lax.dynamic_slice_in_dim(g_vec, lax.axis_index("dp") * 12, 12, axis=1)
-    return (boundary, g_qkv[None], g_out[None], g_gu[None], g_dn[None], mine[None, :2], mine[None, 2:])
+    return (boundary[None], g_qkv[None], g_out[None], g_gu[None], g_dn[None], mine[None, :2], mine[None, 2:])
 
 
 def solution(mesh):

time: 607 us -> 221 us (0.36); the launches traced: 597 us -> 219 us
  matrix products: 148 us -> 0 us
  Pallas kernels: 85 us -> 207 us
  other arithmetic: 119 us -> 0.52 us
  local copies, waits for them, and re-layouts: 126 us -> 10.2 us
  waiting for transfers between devices: 76.9 us -> 0 us
  loops' own time: 22.7 us -> 0 us
  starting transfers between devices: 18.4 us -> 0 us
    dot_general x42 -> x0, matrix products: 148 us -> none  [the longest x4 22.5 us: forward(): jnp.dot(hidden, weight_down, preferred_element_type=jnp.float32)]
    pallas_call x0 -> x1, Pallas kernels: none -> 123 us  [run_layers(): pl.pallas_call(layers_kernel, out_shape=[jax.ShapeDtypeStruct((2, 256, 76...]
    ppermute x4 -> x0, waiting for transfers between devices: 76.9 us -> none  [passed_along(): lax.ppermute(value, axis, [(source, source + steps) for source in range(i...]
    another operation x51 -> x0, local copies, waits for them, and re-layouts: 39.6 us -> none
    convert_element_type x18 -> x0, other arithmetic: 35 us -> none  [the longest x2 15.8 us: forward(): hidden = gated_units(gate_up).astype(jnp.bfloat16)]
    reduce_sum x24 -> x0, other arithmetic: 27.1 us -> none  [the longest x4 5.58 us: layer_norm(): average = jnp.mean(values_in, -1, keepdims=True)]
    slice x14 -> x0, local copies, waits for them, and re-layouts: 21.7 us -> none  [the longest x8 15.3 us: forward(): keys = projected[:, D:2 * D].astype(jnp.bfloat16)]
    ppermute x4 -> x0, starting transfers between devices: 18.4 us -> none  [passed_along(): lax.ppermute(value, axis, [(source, source + steps) for source in range(i...]
  transfers between devices with their start and end apart: 4 -> 0, of which waited for: 3 -> 0; matrix products, arithmetic and copies ran while one was open for 15% -> 0% of each run, Pallas kernels for 0% -> 0%
where the time goes in v2:
time: 221 us; the launch traced here: 219 us
  Pallas kernels  207 us (94%)
  local copies, waits for them, and re-layouts  10.2 us (5%)
    pallas_call x1, Pallas kernels, run_layers(): pl.pallas_call(layers_kernel, out_shape=[jax.ShapeDtypeStruct((2, 256, 76...  123 us
    pallas_call x1, Pallas kernels, reduce_weights(): pl.pallas_call(reduce_kernel, out_shape=[jax.ShapeDtypeStruct((12, 2304),...  83.4 us
    unnamed x11, local copies, waits for them, and re-layouts  8.9 us

profile of v2, /device:TPU:1, one launch (start us, length us, event | category | flops | bytes accessed | tf_op | source)
XLA Modules:
  0.0 218.9 jit_solution(469049238547176806)
XLA Ops:
  0.6 1.3 copy.23
  2.6 0.5 multiply_exponential_fusion.slopes
  3.1 123.5 %run_layers.1 = (f32[2,256,768]{2,1,0:T(8,128)}, bf16[2,768,256]{2,1,0:T(8,128)(2,1)}, bf16[2,768,256]{2,1,0:T(8,128)(2,1)}, bf16[2,768,256]{2,1,0:T(8,128)(2,1)...) custom-call(s32[2]{0:T(128)} %short_lens.1, ...), custom_call_target="tpu_custom_call" | custom-call | flops 20000000000 | bytes 40000000 | tf_op jit(solution)/shard_map/run_layers/pallas_call | solution.py:413
  126.6 0.0 copy-start
  126.6 83.4 %reduce_weights.1 = (f32[12,2304]{1,0:T(8,128)}, f32[12,768]{1,0:T(8,128)}, f32[12,6144]{1,0:T(8,128)}, f32[48,768]{1,0:T(8,128)}, f32[8,768]{1,0:T(8,128)}) custom-call(bf16[2,768,256]{2,1,0:T(8,128)(2,1)} %get-tuple-element.23.xa, bf16[2,768,256]{2,1,0:T(8,128)(2,1)} %get-tuple-element.24.xm, bf16[2,768,256]{2,1,0:T(8,128)(2,1)} %get-tuple-element.25.xn, ...), custom_call_target="tpu_custom_call" | custom-call | flops 10000000000 | bytes 20000000 | tf_op jit(solution)/shard_map/reduce_weights/pallas_call | solution.py:823
  210.0 0.0 copy-start.1
  210.0 2.0 copy.19
  212.1 1.7 copy.17
  213.7 1.5 copy.18
  215.2 0.8 constant_dynamic-slice_fusion
  216.0 0.6 copy.20
  216.5 0.6 slice_bitcast_fusion.1
  217.1 0.0 copy-done
  217.1 1.1 copy.27
  218.3 0.0 copy-done.1
  218.3 0.7 copy.28
  (1 shorter events, 0.0 us)
Async XLA Ops:
  126.6 90.5 %copy-start = (f32[2,256,768]{2,1,0:T(8,128)S(1)}, f32[2,256,768]{2,1,0:T(8,128)}, u32[]{:S(2)}) copy-start(f32[2,256,768]{2,1,0:T(8,128)} %get-tuple-element.22) | copy-start | bytes 4718596
  210.0 8.3 %copy-start.1 = (f32[48,768]{1,0:T(8,128)S(1)}, f32[48,768]{1,0:T(8,128)}, u32[]{:S(2)}) copy-start(f32[48,768]{1,0:T(8,128)} %get-tuple-element.35) | copy-start | bytes 442372

commit v3 on v2

--- a/solution.py
+++ b/solution.py
@@ -51,9 +51,9 @@
 
 
 def layers_kernel(
-    short_lens, long_lens, slopes, tokens, cotangent, w_qkv, w_out, w_gate_up, w_down, gains, biases,
+    short_lens, long_lens, tokens, cotangent, w_qkv, w_out, w_gate_up, w_down, gains, biases,
     boundary, o_at, o_mt, o_nt, o_ht, o_gq, o_go, o_gg, o_gf, o_vec,
-    wq, wo, wg, wd, x_s, g_s, qkv_s, p_s, mixed_s, low_s, n1_s, n2_s, r1_s, r2_s, gu_s, at_s, mt_s, nt_s, ht_s,
+    wq, wo, wg, wd, x_s, g_s, qkv_s, p_s, mixed_s, nl_s, low_s, n1_s, n2_s, r1_s, r2_s, gu_s, ht_s,
     gf_s, ga_s, send_s, out_s, acc_s, f_s, gate_s, up_s, dist_s, mask_s, vec_s,
     w_sem, x_sem, g_sem, out_sem, spill_sem, f_send, f_recv, b_send, b_recv,
 ):
@@ -134,11 +134,10 @@
         return centred * inverse, inverse
 
     def spill(m):
-        cols = pl.ds(m * 256, 256)
         return [
-            pltpu.make_async_copy(at_s.at[m], o_at.at[m], spill_sem.at[m, 0]),
-            pltpu.make_async_copy(mt_s.at[m], o_mt.at[m], spill_sem.at[m, 1]),
-            pltpu.make_async_copy(nt_s.at[m], o_nt.at[m], spill_sem.at[m, 2]),
+            pltpu.make_async_copy(x_s.at[m], o_at.at[m], spill_sem.at[m, 0]),
+            pltpu.make_async_copy(mixed_s.at[m], o_mt.at[m], spill_sem.at[m, 1]),
+            pltpu.make_async_copy(nl_s.at[m], o_nt.at[m], spill_sem.at[m, 2]),
             pltpu.make_async_copy(ht_s.at[m], o_ht.at[m], spill_sem.at[m, 3]),
         ]
 
@@ -169,14 +168,13 @@
             w_copies[0].wait()
 
         x = x_s[m]
-        at_s[m] = x.T
-        query = dot_nn(x, wq[:, 0:768]) + biases[0:1]
+        query = dot_nn(x, wq[:, 0:768]) + biases[0]
         qkv_s[m, :, 0:768] = bf16(f32(bf16(query)) * 0.125)
         qkv_s[m, :, 768:1536] = bf16(dot_nn(x, wq[:, 768:1536]))
-        qkv_s[m, :, 1536:2304] = bf16(dot_nn(x, wq[:, 1536:2304]) + biases[1:2])
+        qkv_s[m, :, 1536:2304] = bf16(dot_nn(x, wq[:, 1536:2304]) + biases[1])
 
         def heads(hp, carry):
-            lane0 = pl.multiple_of(hp * 128, 128)
+            lane0 = hp * 128
             q2 = qkv_s[m, :, pl.ds(lane0, 128)]
             k2 = qkv_s[m, :, pl.ds(lane0 + 768, 128)]
             v2 = qkv_s[m, :, pl.ds(lane0 + 1536, 128)]
@@ -184,7 +182,7 @@
             for e in range(2):
                 keep = (lanes < 64) if e == 0 else (lanes >= 64)
                 qm = jnp.where(keep, q2, jnp.zeros_like(q2))
-                scores = dot_nt(k2, qm) - slopes[2 * hp + e] * dist_s[...]
+                scores = dot_nt(k2, qm) - 2.0 ** (-8.0 * (2 * hp + e + 1) / HEADS) * dist_s[...]
                 scores = jnp.where(mask_s[m] > 0.5, scores, masked_value)
                 expo = jnp.exp(scores - jnp.max(scores, 0, keepdims=True))
                 total = jnp.sum(expo, 0, keepdims=True)
@@ -194,40 +192,39 @@
             mixed_s[m, :, pl.ds(lane0, 128)] = bf16(jnp.where(lanes < 64, outs[0], outs[1]))
             return carry
 
-        lax.fori_loop(0, 6, heads, 0)
+        for index in range(6):
+            heads(index, 0)
 
         @pl.when(m == 0)
         def _():
             w_copies[1].wait()
 
         mixed = mixed_s[m]
-        mt_s[m] = mixed.T
         acc_s[...] = dot_nn(mixed, wo[...])
 
         def norm_one(k, carry):
             r = band(k)
-            value = f32(x_s[m, r]) + (acc_s[r] + biases[2:3])
+            value = f32(x_s[m, r]) + (acc_s[r] + biases[2])
             unit, inverse = normalise(value)
-            normed = unit * gains[0:1] + biases[3:4]
+            normed = unit * gains[0:1] + biases[3]
             n1_s[m, r] = bf16(unit)
             r1_s[m, r] = inverse
             f_s[r] = normed
-            low_s[r] = bf16(normed)
+            nl_s[m, r] = bf16(normed)
             return carry
 
-        lax.fori_loop(0, 8, norm_one, 0)
+        lax.fori_loop(0, 8, norm_one, 0, unroll=True)
 
         @pl.when(m == 0)
         def _():
             w_copies[2].wait()
             w_copies[3].wait()
 
-        nt_s[m] = low_s[...].T
         acc_s[...] = jnp.zeros_like(acc_s)
 
         def ffn(jb, carry):
-            c0 = pl.multiple_of(jb * BLOCK, BLOCK)
-            low = low_s[...]
+            c0 = jb * BLOCK
+            low = nl_s[m]
             gate_s[...] = dot_nn(low, wg[:, pl.ds(c0, BLOCK)])
             up_s[...] = dot_nn(low, wg[:, pl.ds(c0 + FF, BLOCK)])
             for k in range(8):
@@ -242,20 +239,21 @@
             acc_s[...] += dot_nn(hid, wd[pl.ds(c0, BLOCK)])
             return carry
 
-        lax.fori_loop(0, 6, ffn, 0)
+        for index in range(6):
+            ffn(index, 0)
 
         def norm_two(k, carry):
             r = band(k)
-            value = f_s[r] + (acc_s[r] + biases[4:5])
+            value = f_s[r] + (acc_s[r] + biases[4])
             unit, inverse = normalise(value)
             n2_s[m, r] = bf16(unit)
             r2_s[m, r] = inverse
-            result = unit * gains[1:2] + biases[5:6]
+            result = unit * gains[1:2] + biases[5]
             out_s[m, r] = result
             send_s[m, r] = bf16(result)
             return carry
 
-        lax.fori_loop(0, 8, norm_two, 0)
+        lax.fori_loop(0, 8, norm_two, 0, unroll=True)
 
         @pl.when(first)
         def _():
@@ -304,11 +302,11 @@
             vec_s[6] += fold_rows(f32(low))
             return carry
 
-        lax.fori_loop(0, 8, back_two, 0)
+        lax.fori_loop(0, 8, back_two, 0, unroll=True)
         acc_s[...] = jnp.zeros_like(acc_s)
 
         def ffn_back(jb, carry):
-            c0 = pl.multiple_of(jb * BLOCK, BLOCK)
+            c0 = jb * BLOCK
             gate_s[...] = dot_nt(gf_s[m], wd[pl.ds(c0, BLOCK)])
             for k in range(8):
                 r = pl.ds(k * BAND, BAND)
@@ -319,7 +317,8 @@
             acc_s[...] += dot_nt(gu_s[m, :, pl.ds(c0 + FF, BLOCK)], wg[:, pl.ds(c0 + FF, BLOCK)])
             return carry
 
-        lax.fori_loop(0, 6, ffn_back, 0)
+        for index in range(6):
+            ffn_back(index, 0)
 
         def back_one(k, carry):
             r = band(k)
@@ -334,11 +333,11 @@
             vec_s[4] += fold_rows(f32(low))
             return carry
 
-        lax.fori_loop(0, 8, back_one, 0)
+        lax.fori_loop(0, 8, back_one, 0, unroll=True)
         low_s[...] = bf16(dot_nt(ga_s[m], wo[...]))
 
         def heads_back(hp, carry):
-            lane0 = pl.multiple_of(hp * 128, 128)
+            lane0 = hp * 128
             q2 = qkv_s[m, :, pl.ds(lane0, 128)]
             k2 = qkv_s[m, :, pl.ds(lane0 + 768, 128)]
             v2 = qkv_s[m, :, pl.ds(lane0 + 1536, 128)]
@@ -365,7 +364,8 @@
             qkv_s[m, :, pl.ds(lane0 + 1536, 128)] = grad_v
             return carry
 
-        lax.fori_loop(0, 6, heads_back, 0)
+        for index in range(6):
+            heads_back(index, 0)
         grad_a = dot_nt(qkv_s[m], wq[...]) + f_s[...]
 
         @pl.when(second)
@@ -405,7 +405,6 @@
     vmem = pl.BlockSpec(memory_space=pltpu.VMEM)
     smem = pl.BlockSpec(memory_space=pltpu.SMEM)
     dma = pltpu.SemaphoreType.DMA
-    slopes = jnp.exp2(-8.0 * (jnp.arange(HEADS).astype(wide) + 1.0) / HEADS)
 
     def of(shape, dtype):
         return pltpu.VMEM(shape, dtype)
@@ -414,9 +413,9 @@
         layers_kernel,
         out_shape=[
             jax.ShapeDtypeStruct((2, 256, 768), wide),
-            jax.ShapeDtypeStruct((2, 768, 256), low),
-            jax.ShapeDtypeStruct((2, 768, 256), low),
-            jax.ShapeDtypeStruct((2, 768, 256), low),
+            jax.ShapeDtypeStruct((2, 256, 768), low),
+            jax.ShapeDtypeStruct((2, 256, 768), low),
+            jax.ShapeDtypeStruct((2, 256, 768), low),
             jax.ShapeDtypeStruct((2, 3072, 256), low),
             jax.ShapeDtypeStruct((2, 256, 2304), low),
             jax.ShapeDtypeStruct((2, 256, 768), low),
@@ -424,14 +423,14 @@
             jax.ShapeDtypeStruct((2, 256, 768), low),
             jax.ShapeDtypeStruct((8, 768), wide),
         ],
-        in_specs=[smem] * 3 + [hbm] * 6 + [vmem] * 2,
+        in_specs=[smem] * 2 + [hbm] * 6 + [vmem] * 2,
         out_specs=[hbm] * 9 + [vmem],
         scratch_shapes=[
             of((768, 2304), low), of((768, 768), low), of((768, 6144), low), of((3072, 768), low),
             of((2, 256, 768), low), of((2, 256, 768), low), of((2, 256, 2304), low), of((2, 12, 256, 256), low),
-            of((2, 256, 768), low), of((256, 768), low), of((2, 256, 768), low), of((2, 256, 768), low),
+            of((2, 256, 768), low), of((2, 256, 768), low), of((256, 768), low), of((2, 256, 768), low), of((2, 256, 768), low),
             of((2, 256, 1), wide), of((2, 256, 1), wide), of((2, 256, 6144), low),
-            of((2, 768, 256), low), of((2, 768, 256), low), of((2, 768, 256), low), of((2, 3072, 256), low),
+            of((2, 3072, 256), low),
             of((2, 256, 768), low), of((2, 256, 768), low), of((2, 256, 768), low), of((2, 256, 768), wide),
             of((256, 768), wide), of((256, 768), wide), of((256, 512), wide), of((256, 512), wide),
             of((256, 256), wide), of((2, 256, 256), wide), of((8, 8, 768), wide),
@@ -442,7 +441,7 @@
         ),
         cost_estimate=pl.CostEstimate(flops=2 * 10 ** 10, bytes_accessed=4 * 10 ** 7, transcendentals=10 ** 7),
         name="run_layers",
-    )(short_lens, long_lens, slopes, tokens, cotangent, w_qkv, w_out, w_gate_up, w_down, gains, biases)
+    )(short_lens, long_lens, tokens, cotangent, w_qkv, w_out, w_gate_up, w_down, gains, biases)
 
 
 S_SLOTS = 5
@@ -492,11 +491,11 @@
             to = pl.ds(m * 256, 256)
             to_far = pl.ds(half + m * 256, 256)
             src_own, src_far, dst_own, dst_far = (
-                (xn.at[m], xn.at[m], t_n.at[:, to], t_n.at[:, to_far]),
+                (xn.at[m], xn.at[m], t_n.at[to], t_n.at[to_far]),
                 (gg.at[m, :, pl.ds(core * 3072, 3072)], gg.at[m, :, pl.ds(other * 3072, 3072)], w_g.at[to], w_g.at[to_far]),
-                (xa.at[m], xa.at[m], t_a.at[:, to], t_a.at[:, to_far]),
+                (xa.at[m], xa.at[m], t_a.at[to], t_a.at[to_far]),
                 (gq.at[m, :, pl.ds(core * 1152, 1152)], gq.at[m, :, pl.ds(other * 1152, 1152)], w_q.at[to], w_q.at[to_far]),
-                (xm.at[m], xm.at[m], t_m.at[:, to], t_m.at[:, to_far]),
+                (xm.at[m], xm.at[m], t_m.at[to], t_m.at[to_far]),
                 (go.at[m, :, pl.ds(core * 384, 384)], go.at[m, :, pl.ds(other * 384, 384)], w_o.at[to], w_o.at[to_far]),
                 (xh.at[m, :, core], xh.at[m, :, other], t_h.at[:, :, to], t_h.at[:, :, to_far]),
                 (gf.at[m], gf.at[m], w_f.at[to], w_f.at[to_far]),
@@ -620,7 +619,7 @@
                     own[mine, h, first, second] = halves[h][y * 4 + z]
 
     def product(lhs, rhs):
-        return jnp.dot(lhs, rhs, preferred_element_type=jnp.float32).astype(jnp.bfloat16)
+        return bf16(dot_tn(lhs, rhs))
 
     def split_halves(result):
         return [result[:, h * 256:(h + 1) * 256].reshape(16, 48, 256) for h in range(2)]
@@ -655,7 +654,7 @@
             def _():
                 wait_operands(6, 7)
             rhs = w_f[:, pl.ds(pl.multiple_of((j - 9) * 256, 256), 256)]
-            result = product(t_h[...].reshape(1536, 1024), rhs).reshape(16, 2, 48, 256)
+            result = bf16(dot_nn(t_h[...].reshape(1536, 1024), rhs)).reshape(16, 2, 48, 256)
             store_rows(j, [result[:, 0], result[:, 1]])
 
     def step(i, carry):
@@ -787,19 +786,19 @@
                 def _():
                     for h in range(2):
                         column = pl.multiple_of(who * 3072 + j6 * 512 + h * 256, 256)
-                        o_gu[:, pl.ds(column, 256)] = source[slot, h, 0:12]
+                        o_gu[:, 0, pl.ds(column, 256)] = source[slot, h, 0:12]
 
                 @pl.when((j6 >= 6) & (j6 < 8))
                 def _():
                     for h in range(2):
                         column = pl.multiple_of(who * 1152 + (j6 - 6) * 512 + h * 256, 128)
-                        o_qkv[:, pl.ds(column, 256)] = source[slot, h, 0:12]
+                        o_qkv[:, 0, pl.ds(column, 256)] = source[slot, h, 0:12]
 
                 @pl.when(j6 == 8)
                 def _():
-                    o_qkv[:, pl.ds(pl.multiple_of(who * 1152 + 1024, 128), 128)] = source[slot, 0, 0:12, 0:128]
-                    o_out[:, pl.ds(pl.multiple_of(who * 384, 128), 128)] = source[slot, 0, 0:12, 128:256]
-                    o_out[:, pl.ds(pl.multiple_of(who * 384 + 128, 128), 256)] = source[slot, 1, 0:12]
+                    o_qkv[:, 0, pl.ds(pl.multiple_of(who * 1152 + 1024, 128), 128)] = source[slot, 0, 0:12, 0:128]
+                    o_out[:, 0, pl.ds(pl.multiple_of(who * 384, 128), 128)] = source[slot, 0, 0:12, 128:256]
+                    o_out[:, 0, pl.ds(pl.multiple_of(who * 384 + 128, 128), 256)] = source[slot, 1, 0:12]
 
         for stage in range(4):
             @pl.when(i == 2 * stage + 2)
@@ -823,18 +822,18 @@
     return pl.pallas_call(
         reduce_kernel,
         out_shape=[
-            jax.ShapeDtypeStruct((12, 2304), wide),
-            jax.ShapeDtypeStruct((12, 768), wide),
-            jax.ShapeDtypeStruct((12, 6144), wide),
+            jax.ShapeDtypeStruct((12, 1, 2304), wide),
+            jax.ShapeDtypeStruct((12, 1, 768), wide),
+            jax.ShapeDtypeStruct((12, 1, 6144), wide),
             jax.ShapeDtypeStruct((48, 768), wide),
             jax.ShapeDtypeStruct((8, 768), wide),
         ],
         in_specs=[hbm] * 8 + [vmem],
         out_specs=[vmem] * 5,
         scratch_shapes=[
-            pltpu.VMEM((768, 1024), low),
-            pltpu.VMEM((768, 1024), low),
-            pltpu.VMEM((768, 1024), low),
+            pltpu.VMEM((1024, 768), low),
+            pltpu.VMEM((1024, 768), low),
+            pltpu.VMEM((1024, 768), low),
             pltpu.VMEM((32, 48, 1024), low),
             pltpu.VMEM((1024, 1152), low),
             pltpu.VMEM((1024, 384), low),
@@ -871,15 +870,56 @@
     )(xa, xm, xn, xh.reshape(2, 32, 2, 48, 256), gq, go, gg, gf, vec)
 
 
+def place_kernel(start, boundary, qkv, out, gate_up, down, vec, o_b, o_q, o_o, o_g, o_d, o_gains, o_biases, sems):
+    copies = [
+        pltpu.make_async_copy(source, target, sems.at[k])
+        for k, (source, target) in enumerate(
+            ((boundary, o_b.at[0]), (gate_up, o_g), (qkv, o_q), (out, o_o), (down, o_d.at[0]))
+        )
+    ]
+    for copy in copies:
+        copy.start()
+    mine = pltpu.roll(vec[...], lax.rem(D - start[0], D), axis=1)
+    o_gains[0] = mine[:2, :12]
+    o_biases[:, 0] = mine[2:, :12]
+    for copy in copies:
+        copy.wait()
+
+
+def place(start, boundary, qkv, out, gate_up, down, vec):
+    wide = jnp.float32
+    hbm = pl.BlockSpec(memory_space=pl.ANY)
+    vmem = pl.BlockSpec(memory_space=pltpu.VMEM)
+    return pl.pallas_call(
+        place_kernel,
+        out_shape=[
+            jax.ShapeDtypeStruct((1, 2, 256, 768), wide),
+            jax.ShapeDtypeStruct((12, 1, 2304), wide),
+            jax.ShapeDtypeStruct((12, 1, 768), wide),
+            jax.ShapeDtypeStruct((12, 1, 6144), wide),
+            jax.ShapeDtypeStruct((1, 48, 768), wide),
+            jax.ShapeDtypeStruct((1, 2, 12), wide),
+            jax.ShapeDtypeStruct((6, 1, 12), wide),
+        ],
+        in_specs=[pl.BlockSpec(memory_space=pltpu.SMEM)] + [hbm] * 5 + [vmem],
+        out_specs=[hbm] * 5 + [vmem] * 2,
+        scratch_shapes=[pltpu.SemaphoreType.DMA((5,))],
+        name="place",
+    )(start, boundary, qkv, out, gate_up, down, vec)
+
+
 def on_device(
     tokens, cotangent, short_lens, long_lens, w_qkv, w_out, w_gate_up, w_down, gains, biases
 ):
     boundary, x_a, x_m, x_n, x_h, g_q, g_o, g_g, g_f, vec = run_layers(
-        short_lens, long_lens, tokens, cotangent, w_qkv[0], w_out[0], w_gate_up[0], w_down[0], gains[0], biases[0]
+        short_lens, long_lens, tokens, cotangent, w_qkv[0], w_out[0], w_gate_up[0], w_down[0], gains[0],
+        jnp.transpose(biases, (1, 0, 2)),
     )
     g_qkv, g_out, g_gu, g_dn, g_vec = reduce_weights(x_a, x_m, x_n, x_h, g_q, g_o, g_g, g_f, vec)
-    mine = lax.dynamic_slice_in_dim(g_vec, lax.axis_index("dp") * 12, 12, axis=1)
-    return (boundary[None], g_qkv[None], g_out[None], g_gu[None], g_dn[None], mine[None, :2], mine[None, 2:])
+    start = jnp.full((1,), lax.axis_index("dp") * 12, jnp.int32)
+    b, q, o, g, d, gains_out, biases_out = place(start, boundary, g_qkv, g_out, g_gu, g_dn, g_vec)
+    q, o, g, biases_out = (jnp.transpose(rows, (1, 0, 2)) for rows in (q, o, g, biases_out))
+    return (b, q, o, g, d, gains_out, biases_out)
 
 
 def solution(mesh):

time: 221 us -> 240 us (1.086)
  Pallas kernels: 207 us -> 236 us
  local copies, waits for them, and re-layouts: 10.2 us -> 0 us
    pallas_call x1 -> x2, Pallas kernels: 83.4 us -> 151 us  [the longest x1 83.4 us: reduce_weights(): pl.pallas_call(reduce_kernel, out_shape=[jax.ShapeDtypeStruct((12, 1, 230...]
    pallas_call x1, Pallas kernels: 123 us -> 84.7 us  [run_layers(): pl.pallas_call(layers_kernel, out_shape=[jax.ShapeDtypeStruct((2, 256, 76...]
    unnamed x11 -> x0, local copies, waits for them, and re-layouts: 8.9 us -> none
where the time goes in v3:
time: 240 us; the launch traced here: 238 us
  Pallas kernels  236 us (98%)
    pallas_call x1, Pallas kernels, run_layers(): pl.pallas_call(layers_kernel, out_shape=[jax.ShapeDtypeStruct((2, 256, 76...  84.7 us
    pallas_call x1, Pallas kernels, reduce_weights(): pl.pallas_call(reduce_kernel, out_shape=[jax.ShapeDtypeStruct((12, 1, 230...  83.4 us
    pallas_call x1, Pallas kernels, place(): pl.pallas_call(place_kernel, out_shape=[jax.ShapeDtypeStruct((1, 2, 256,...  68 us

profile of v3, /device:TPU:1, one launch (start us, length us, event | category | flops | bytes accessed | tf_op | source)
XLA Modules:
  0.0 237.6 jit_solution(11563497934881305226)
XLA Ops:
  1.3 84.7 %run_layers.1 = (f32[2,256,768]{2,1,0:T(8,128)}, bf16[2,256,768]{2,1,0:T(8,128)(2,1)}, bf16[2,256,768]{2,1,0:T(8,128)(2,1)}, bf16[2,256,768]{2,1,0:T(8,128)(2,1)...) custom-call(s32[2]{0:T(128)} %short_lens.1, ...), custom_call_target="tpu_custom_call" | custom-call | flops 20000000000 | bytes 40000000 | tf_op jit(solution)/shard_map/run_layers/pallas_call | solution.py:412
  86.0 83.4 %reduce_weights.1 = (f32[12,1,2304]{2,1,0:T(1,128)}, f32[12,1,768]{2,1,0:T(1,128)}, f32[12,1,6144]{2,1,0:T(1,128)}, f32[48,768]{1,0:T(8,128)}, f32[8,768]{1,0:T(8,128)}) custom-call(bf16[2,256,768]{2,1,0:T(8,128)(2,1)} %get-tuple-element.30.xa, bf16[2,256,768]{2,1,0:T(8,128)(2,1)} %get-tuple-element.31.xm, bf16[2,256,768]{2,1,0:T(8,128)(2,1)} %get-tuple-element.32.xn, ...), custom_call_target="tpu_custom_call" | custom-call | flops 10000000000 | bytes 20000000 | tf_op jit(solution)/shard_map/reduce_weights/pallas_call | solution.py:822
  169.4 68.0 %place.1 = (f32[1,2,256,768]{3,2,1,0:T(8,128)}, f32[12,1,2304]{2,1,0:T(1,128)}, f32[12,1,768]{2,1,0:T(1,128)}, f32[12,1,6144]{2,1,0:T(1,128)}, f32[1,48,768]{2,1...) custom-call(s32[1]{0:T(128)} %bitcast.start, f32[2,256,768]{2,1,0:T(8,128)} %get-tuple-element.29.boundary, ...), custom_call_target="tpu_custom_call" | custom-call | tf_op jit(solution)/shard_map/place/pallas_call | solution.py:893

commit v4 on v0

v4 whole, which is shorter than its diff:
```python
import jax
import jax.numpy as jnp
from jax import lax
from jax.experimental import pallas as pl
from jax.experimental.pallas import tpu as pltpu
from jax.sharding import PartitionSpec as P

D = 768
HEADS = 12
FF = 3072
BLOCK = 768
BAND = 32
N_CHUNKS = 12
N_DOWN = 3
SLOTS = 5
OWN_SLOTS = 3
VMEM_LIMIT = 62 * 1024 * 1024
MESH_IDS = pl.DeviceIdType.MESH

epsilon = 1e-05
masked_value = -1000000000.0


def dot_nn(lhs, rhs):
    return jnp.dot(lhs, rhs, preferred_element_type=jnp.float32)


def dot_nt(lhs, rhs):
    return lax.dot_general(lhs, rhs, (((1,), (1,)), ((), ())), preferred_element_type=jnp.float32)


def dot_tn(lhs, rhs):
    return lax.dot_general(lhs, rhs, (((0,), (0,)), ((), ())), preferred_element_type=jnp.float32)


def f32(value):
    return value.astype(jnp.float32)


def bf16(value):
    return value.astype(jnp.bfloat16)


def fold_rows(value):
    return jnp.sum(value.reshape(value.shape[0] // 8, 8, value.shape[1]), 0)


def gelu_terms(gate):
    cdf = 0.5 * (1.0 + lax.erf(gate * 0.7071067811865476))
    density = jnp.exp(-0.5 * gate * gate) * 0.3989422804014327
    return gate * cdf, cdf + gate * density


def when(condition):
    if isinstance(condition, bool):
        return (lambda body: body()) if condition else (lambda body: None)
    return pl.when(condition)


def both(value):
    return value.reshape(512, value.shape[-1])


def layers_kernel(
    short_lens, long_lens, tokens, cotangent, w_qkv, w_out, w_gate_up, w_down, gains, biases,
    boundary, o_qkv, o_out, o_gu, o_dn, o_vec,
    wq, wo, wg, wd, x_s, g_s, qkv_s, p_s, mixed_s, nl_s, low_s, n1_s, n2_s, r1_s, r2_s, gu_s, ht_s,
    gf_s, ga_s, send_s, out_s, acc_s, f_s, gate_s, up_s, dist_s, mask_s, vec_s,
    peer_n, peer_h, peer_f, peer_g,
    own, ra_relay, ra_fin, sa, own_b, rb_relay, rb_fin, sb, x_send, x_keep, x_recv, c_tmp, c_send, c_keep, c_recv,
    v_acc, v_recv,
    w_sem, x_sem, g_sem, out_sem, f_send, f_recv, b_send, b_recv, pair_send, pair_recv,
    a_send, a_relay_recv, a_fin_recv, a2_send,
    bb_send, bb_relay_recv, bb_fin_recv, b2_send,
    xs_sem, xr_sem, cs_sem, cr_sem, vs_sem, vr_sem,
):
    sec = lax.axis_index("section")
    first = sec == 0
    second = sec == 1
    me = lax.axis_index("dp")
    core = me % 2
    xhi = (me // 2) % 2
    zz = (me // 4) % 4
    yy = me // 16
    other = 1 - core

    def dev(y, z, x, c):
        return ((y * 4 + z) * 2 + x) * 2 + c

    peer_core = dev(yy, zz, xhi, other)
    peer_x = dev(yy, zz, 1 - xhi, core)
    y_ids = [dev((yy + k) % 4, zz, xhi, core) for k in (1, 2, 3)]
    z_ids = [dev(yy, (zz + k) % 4, xhi, core) for k in (1, 2, 3)]

    def remote(src, dst, send, recv, target):
        return pltpu.make_async_remote_copy(
            src_ref=src, dst_ref=dst, send_sem=send, recv_sem=recv,
            device_id={"dp": target}, device_id_type=MESH_IDS,
        )

    def across(src, dst, send, recv):
        return pltpu.make_async_remote_copy(
            src_ref=src, dst_ref=dst, send_sem=send, recv_sem=recv,
            device_id={"section": 1 - sec}, device_id_type=MESH_IDS,
        )

    w_copies = [
        pltpu.make_async_copy(w_qkv, wq, w_sem.at[0]),
        pltpu.make_async_copy(w_out, wo, w_sem.at[1]),
        pltpu.make_async_copy(w_gate_up, wg, w_sem.at[2]),
        pltpu.make_async_copy(w_down, wd, w_sem.at[3]),
    ]

    def token_copy(m):
        return pltpu.make_async_copy(tokens.at[m], x_s.at[m], x_sem.at[m])

    def cot_copy(m):
        return pltpu.make_async_copy(cotangent.at[m], g_s.at[m], g_sem.at[m])

    def hand_on(m):
        return across(send_s.at[m], x_s.at[m], f_send.at[m], f_recv.at[m])

    def hand_back(m):
        return across(send_s.at[m], g_s.at[m], b_send.at[m], b_recv.at[m])

    def out_copy(m):
        return pltpu.make_async_copy(out_s, boundary.at[m], out_sem.at[m])

    def pair(k, m):
        rows = pl.ds(m * 256, 256)
        src, dst = (
            lambda: (nl_s.at[m], peer_n.at[m]),
            lambda: (ht_s.at[m, :, other], peer_h.at[m]),
            lambda: (gf_s.at[m], peer_f.at[m]),
            lambda: (gu_s.at[m, :, pl.ds(other * FF, FF)], peer_g.at[m]),
            lambda: (x_s.at[m], wg.at[rows, pl.ds(0, 768)]),
            lambda: (mixed_s.at[m], wg.at[rows, pl.ds(768, 768)]),
            lambda: (qkv_s.at[m, :, pl.ds(other * 1152, 1152)], wg.at[rows, pl.ds(1536, 1152)]),
            lambda: (ga_s.at[m, :, pl.ds(other * 384, 384)], wg.at[rows, pl.ds(2688, 384)]),
        )[k]()
        return remote(src, dst, pair_send.at[k, m], pair_recv.at[k, m], peer_core)

    def pair_wait(*which):
        for k in which:
            for m in range(2):
                pair(k, m).wait()

    @pl.when(first)
    def _():
        token_copy(0).start()

    w_copies[0].start()
    w_copies[1].start()

    @pl.when(first)
    def _():
        token_copy(1).start()

    w_copies[2].start()
    w_copies[3].start()

    @pl.when(second)
    def _():
        cot_copy(0).start()
        cot_copy(1).start()

    barrier = pltpu.get_barrier_semaphore()
    pl.semaphore_signal(barrier, inc=1, device_id={"section": 1 - sec}, device_id_type=MESH_IDS)
    for target in [peer_core, peer_x] + y_ids + z_ids:
        pl.semaphore_signal(barrier, inc=1, device_id={"dp": target}, device_id_type=MESH_IDS)
    pl.semaphore_wait(barrier, 9)

    vec_s[...] = jnp.zeros_like(vec_s)
    rows_j = lax.broadcasted_iota(jnp.int32, (256, 256), 0)
    cols_i = lax.broadcasted_iota(jnp.int32, (256, 256), 1)
    dist_s[...] = f32(jnp.abs(rows_j - cols_i))
    length_a, length_b, length_long = short_lens[0], short_lens[1], long_lens[0]
    for m in range(2):
        if m == 0:
            limit = jnp.where(rows_j < 128, length_a, length_b + 128)
            apart = jnp.where((rows_j >> 7) == (cols_i >> 7), 0, 1024)
            ok = rows_j + apart < limit
        else:
            ok = rows_j < length_long
        mask_s[m] = jnp.where(ok, 1.0, 0.0)


    def v_sends(stage):
        targets = ([peer_core], [peer_x], y_ids, z_ids)[stage]
        base = (0, 1, 2, 5)[stage]
        count = len(targets)
        return [
            remote(
                v_acc.at[stage], v_recv.at[base + (count - 1 - k)],
                vs_sem.at[base + k], vr_sem.at[base + (count - 1 - k)], targets[k],
            )
            for k in range(count)
        ]

    def v_start(stage):
        for copy in v_sends(stage):
            copy.start()

    def v_finish(stage):
        base = (0, 1, 2, 5)[stage]
        copies = v_sends(stage)
        for copy in copies:
            copy.wait_send()
        for copy in copies:
            copy.wait_recv()
        total = v_acc[stage]
        for k in range(len(copies)):
            total = total + v_recv[base + k]
        v_acc[stage + 1] = total

    def ring(par):
        right = y_ids[0] * (1 - par) + z_ids[0] * par
        left = y_ids[2] * (1 - par) + z_ids[2] * par
        place = yy * (1 - par) + zz * par
        return right, left, place

    def a1_copies(j):
        slot, mine = j % SLOTS, j % OWN_SLOTS
        right, left, p = ring(j % 2)
        far, nxt, prv = (p + 2) % 4, (p + 1) % 4, (p + 3) % 4
        return (
            remote(own.at[mine, 0, far], ra_relay.at[slot, 0], a_send.at[slot, 0], a_relay_recv.at[slot, 0], right),
            remote(own.at[mine, 1, far], ra_relay.at[slot, 1], a_send.at[slot, 1], a_relay_recv.at[slot, 1], left),
            remote(own.at[mine, 1, nxt], ra_fin.at[slot, 0, 1], a_send.at[slot, 2], a_fin_recv.at[slot, 0, 1], right),
            remote(own.at[mine, 0, prv], ra_fin.at[slot, 1, 0], a_send.at[slot, 3], a_fin_recv.at[slot, 1, 0], left),
        )

    def a2_copies(j):
        slot, mine = j % SLOTS, j % 2
        right, left, _ = ring(j % 2)
        return (
            remote(sa.at[mine, 0], ra_fin.at[slot, 0, 0], a2_send.at[mine, 0], a_fin_recv.at[slot, 0, 0], right),
            remote(sa.at[mine, 1], ra_fin.at[slot, 1, 1], a2_send.at[mine, 1], a_fin_recv.at[slot, 1, 1], left),
        )

    def b1_copies(j):
        slot, mine = j % SLOTS, j % OWN_SLOTS
        right, left, p = ring(1 - j % 2)
        far, nxt, prv = (p + 2) % 4, (p + 1) % 4, (p + 3) % 4
        return (
            remote(own_b.at[mine, 0, far], rb_relay.at[slot, 0], bb_send.at[slot, 0], bb_relay_recv.at[slot, 0], right),
            remote(own_b.at[mine, 1, far], rb_relay.at[slot, 1], bb_send.at[slot, 1], bb_relay_recv.at[slot, 1], left),
            remote(own_b.at[mine, 1, nxt], rb_fin.at[slot, 0, 1], bb_send.at[slot, 2], bb_fin_recv.at[slot, 0, 1], right),
            remote(own_b.at[mine, 0, prv], rb_fin.at[slot, 1, 0], bb_send.at[slot, 3], bb_fin_recv.at[slot, 1, 0], left),
        )

    def b2_copies(j):
        slot, mine = j % SLOTS, j % 2
        right, left, _ = ring(1 - j % 2)
        return (
            remote(sb.at[mine, 0], rb_fin.at[slot, 0, 0], b2_send.at[mine, 0], bb_fin_recv.at[slot, 0, 0], right),
            remote(sb.at[mine, 1], rb_fin.at[slot, 1, 1], b2_send.at[mine, 1], bb_fin_recv.at[slot, 1, 1], left),
        )

    def x_copy(j):
        slot, mine = j % SLOTS, j % 2
        return remote(x_send.at[mine], x_recv.at[slot], xs_sem.at[mine], xr_sem.at[slot], peer_x)

    def c_copy(j):
        slot, mine = j % SLOTS, j % 2
        return remote(c_send.at[mine], c_recv.at[slot], cs_sem.at[mine], cr_sem.at[slot], peer_core)

    def place_rows(j, piece):
        mine = j % OWN_SLOTS
        par = j % 2
        for y in range(4):
            for z in range(4):
                i1 = y * (1 - par) + z * par
                i2 = z * (1 - par) + y * par
                for x in range(2):
                    own[mine, x, i1, i2] = bf16(piece(y * 4 + z, x))

    def place_regular(j, result):
        def piece(block, x):
            rows = result[block * 48 + x * 24:block * 48 + x * 24 + 24]
            return jnp.concatenate([rows[:, :256], rows[:, 256:]], 0)

        place_rows(j, piece)

    def compute(j):
        @when(j < N_DOWN)
        def _():
            @when(j == 0)
            def _():
                pair_wait(1, 2)

            cols = pl.ds(pl.multiple_of(j * 256, 256), 256) if not isinstance(j, int) else pl.ds(j * 256, 256)
            result = None
            for m in range(2):
                for left, right in ((ht_s[m, :, core], gf_s[m, :, cols]), (peer_h[m], peer_f[m, :, cols])):
                    term = dot_nn(left.reshape(1536, 256), right)
                    result = term if result is None else result + term
            place_rows(j, lambda block, x: result[(block * 2 + x) * 48:(block * 2 + x + 1) * 48])

        @when((j >= N_DOWN) & (j < N_DOWN + 6))
        def _():
            @when(j == N_DOWN)
            def _():
                pair_wait(0, 3)
                for k in (4, 5, 6, 7):
                    for m in range(2):
                        pair(k, m).start()

            column = pl.multiple_of((j - N_DOWN) * 512, 512)
            mine = gu_s[:, :, pl.ds(pl.multiple_of(core * FF + column, 512), 512)]
            place_regular(j, dot_tn(both(nl_s[...]), both(mine)) + dot_tn(both(peer_n[...]), both(peer_g[:, :, pl.ds(column, 512)])))

        def qkv_part(column, width):
            mine = qkv_s[:, :, pl.ds(pl.multiple_of(core * 1152 + column, 128), width)]
            far = wg[0:512, pl.ds(pl.multiple_of(1536 + column, 128), width)]
            return dot_tn(both(x_s[...]), both(mine)) + dot_tn(wg[0:512, 0:768], far)

        @when((j >= N_DOWN + 6) & (j < N_DOWN + 8))
        def _():
            @when(j == N_DOWN + 6)
            def _():
                pair_wait(4, 5, 6, 7)

            place_regular(j, qkv_part((j - N_DOWN - 6) * 512, 512))

        @when(j == N_DOWN + 8)
        def _():
            mine = ga_s[:, :, pl.ds(pl.multiple_of(core * 384, 128), 384)]
            out_part = dot_tn(both(mixed_s[...]), both(mine)) + dot_tn(wg[0:512, 768:1536], wg[0:512, 2688:3072])
            place_regular(j, jnp.concatenate([qkv_part(1024, 128), out_part], 1))

    def step(i, carry):
        @when(i < N_CHUNKS)
        def _():
            compute(i)
            for copy in a1_copies(i):
                copy.start()

        j1 = i - 1

        @when((j1 >= 0) & (j1 < N_CHUNKS))
        def _():
            slot, mine, buf = j1 % SLOTS, j1 % OWN_SLOTS, j1 % 2
            _, _, p = ring(j1 % 2)
            before = a1_copies(j1)
            after = a2_copies(j1)
            before[0].wait_recv()
            sa[buf, 0] = bf16(f32(own[mine, 0, (p + 1) % 4]) + f32(ra_relay[slot, 0]))
            after[0].start()
            before[1].wait_recv()
            sa[buf, 1] = bf16(f32(own[mine, 1, (p + 3) % 4]) + f32(ra_relay[slot, 1]))
            after[1].start()

        j2 = i - 2

        @when((j2 >= 0) & (j2 < N_CHUNKS))
        def _():
            slot, mine = j2 % SLOTS, j2 % OWN_SLOTS
            _, _, p = ring(j2 % 2)
            before = a1_copies(j2)
            after = a2_copies(j2)
            for copy in before + after:
                copy.wait_send()
            for copy in before[2:] + after:
                copy.wait_recv()
            for h in range(2):
                own_b[mine, h] = bf16(f32(own[mine, h, p]) + f32(ra_fin[slot, 0, h]) + f32(ra_fin[slot, 1, h]))
            for copy in b1_copies(j2):
                copy.start()

        j3 = i - 3

        @when((j3 >= 0) & (j3 < N_CHUNKS))
        def _():
            slot, mine, buf = j3 % SLOTS, j3 % OWN_SLOTS, j3 % 2
            _, _, p = ring(1 - j3 % 2)
            before = b1_copies(j3)
            after = b2_copies(j3)
            before[0].wait_recv()
            sb[buf, 0] = bf16(f32(own_b[mine, 0, (p + 1) % 4]) + f32(rb_relay[slot, 0]))
            after[0].start()
            before[1].wait_recv()
            sb[buf, 1] = bf16(f32(own_b[mine, 1, (p + 3) % 4]) + f32(rb_relay[slot, 1]))
            after[1].start()

        j4 = i - 4

        @when((j4 >= 0) & (j4 < N_CHUNKS))
        def _():
            slot, mine, buf = j4 % SLOTS, j4 % OWN_SLOTS, j4 % 2
            _, _, p = ring(1 - j4 % 2)
            before = b1_copies(j4)
            after = b2_copies(j4)
            for copy in before + after:
                copy.wait_send()
            for copy in before[2:] + after:
                copy.wait_recv()
            total = [f32(own_b[mine, h, p]) + f32(rb_fin[slot, 0, h]) + f32(rb_fin[slot, 1, h]) for h in range(2)]
            x_send[buf] = jnp.where(xhi == 0, total[1], total[0])
            x_keep[buf] = jnp.where(xhi == 0, total[0], total[1])
            x_copy(j4).start()

        j5 = i - 5

        @when((j5 >= 0) & (j5 < N_CHUNKS))
        def _():
            slot, buf = j5 % SLOTS, j5 % 2
            x_copy(j5).wait()

            @when(j5 < N_DOWN)
            def _():
                cols = pl.ds(pl.multiple_of(j5 * 256, 256), 256)
                o_dn[:, cols] = x_keep[buf] + x_recv[slot]

            @when(j5 >= N_DOWN)
            def _():
                c_tmp[...] = x_keep[buf] + x_recv[slot]
                for h in range(2):
                    upper, lower = c_tmp[24 * h:24 * h + 12], c_tmp[24 * h + 12:24 * h + 24]
                    c_send[buf, h, 0:12] = jnp.where(core == 0, lower, upper)
                    c_keep[buf, h, 0:12] = jnp.where(core == 0, upper, lower)
                c_copy(j5).start()

        j6 = i - 6

        @when((j6 >= N_DOWN) & (j6 < N_CHUNKS))
        def _():
            slot, buf = j6 % SLOTS, j6 % 2
            c_copy(j6).wait()
            for source, at, who in ((c_keep, buf, core), (c_recv, slot, other)):
                @when(j6 < N_DOWN + 6)
                def _():
                    for h in range(2):
                        column = pl.multiple_of(who * FF + (j6 - N_DOWN) * 512 + h * 256, 256)
                        o_gu[:, 0, pl.ds(column, 256)] = source[at, h, 0:12]

                @when((j6 >= N_DOWN + 6) & (j6 < N_DOWN + 8))
                def _():
                    for h in range(2):
                        column = pl.multiple_of(who * 1152 + (j6 - N_DOWN - 6) * 512 + h * 256, 128)
                        o_qkv[:, 0, pl.ds(column, 256)] = source[at, h, 0:12]

                @when(j6 == N_DOWN + 8)
                def _():
                    o_qkv[:, 0, pl.ds(pl.multiple_of(who * 1152 + 1024, 128), 128)] = source[at, 0, 0:12, 0:128]
                    o_out[:, 0, pl.ds(pl.multiple_of(who * 384, 128), 128)] = source[at, 0, 0:12, 128:256]
                    o_out[:, 0, pl.ds(pl.multiple_of(who * 384 + 128, 128), 256)] = source[at, 1, 0:12]

        return carry


    def band(k):
        return pl.ds(k * BAND, BAND)

    def normalise(value):
        average = jnp.mean(value, -1, keepdims=True)
        centred = value - average
        inverse = lax.rsqrt(jnp.mean(centred * centred, -1, keepdims=True) + epsilon)
        return centred * inverse, inverse

    lanes = lax.broadcasted_iota(jnp.int32, (256, 128), 1)

    def own_lanes(e):
        return (lanes < 64) if e == 0 else (lanes >= 64)

    def forward(m, carry):
        @pl.when(first)
        def _():
            token_copy(m).wait()

        @pl.when(second)
        def _():
            hand_on(m).wait_recv()

        @pl.when(m == 0)
        def _():
            w_copies[0].wait()

        x = x_s[m]
        query = dot_nn(x, wq[:, 0:768]) + biases[0]
        qkv_s[m, :, 0:768] = bf16(f32(bf16(query)) * 0.125)
        qkv_s[m, :, 768:1536] = bf16(dot_nn(x, wq[:, 768:1536]))
        qkv_s[m, :, 1536:2304] = bf16(dot_nn(x, wq[:, 1536:2304]) + biases[1])

        for hp in range(6):
            at = pl.ds(hp * 128, 128)
            q2 = qkv_s[m, :, at]
            k2 = qkv_s[m, :, pl.ds(hp * 128 + 768, 128)]
            v2 = qkv_s[m, :, pl.ds(hp * 128 + 1536, 128)]
            outs = []
            for e in range(2):
                head = 2 * hp + e
                qm = jnp.where(own_lanes(e), q2, jnp.zeros_like(q2))
                scores = dot_nt(k2, qm) - 2.0 ** (-8.0 * (head + 1) / HEADS) * dist_s[...]
                scores = jnp.where(mask_s[m] > 0.5, scores, masked_value)
                expo = jnp.exp(scores - jnp.max(scores, 0, keepdims=True))
                probs = bf16(expo * (1.0 / jnp.sum(expo, 0, keepdims=True)))
                p_s[m, head] = probs
                outs.append(dot_tn(probs, v2))
            mixed_s[m, :, at] = bf16(jnp.where(lanes < 64, outs[0], outs[1]))

        @pl.when(m == 0)
        def _():
            w_copies[1].wait()

        acc_s[...] = dot_nn(mixed_s[m], wo[...])
        for k in range(256 // BAND):
            r = band(k)
            value = f32(x_s[m, r]) + (acc_s[r] + biases[2])
            unit, inverse = normalise(value)
            normed = unit * gains[0:1] + biases[3]
            n1_s[m, r] = bf16(unit)
            r1_s[m, r] = inverse
            f_s[r] = normed
            nl_s[m, r] = bf16(normed)

        pair(0, m).start()

        @pl.when(m == 0)
        def _():
            w_copies[2].wait()
            w_copies[3].wait()

        for jb in range(FF // BLOCK):
            c0 = jb * BLOCK
            low = nl_s[m]
            gate_s[...] = dot_nn(low, wg[:, c0:c0 + BLOCK])
            up_s[...] = dot_nn(low, wg[:, c0 + FF:c0 + FF + BLOCK])
            for k in range(256 // BAND):
                r = band(k)
                gate, up = gate_s[r], up_s[r]
                act, slope = gelu_terms(gate)
                gu_s[m, r, c0:c0 + BLOCK] = bf16(up * slope)
                gu_s[m, r, c0 + FF:c0 + FF + BLOCK] = bf16(act)
                gate_s[r] = act * up
            hid = bf16(gate_s[...])
            ht_s[m, 8 * jb:8 * jb + 8] = hid.T.reshape(8, 2, 48, 256)
            term = dot_nn(hid, wd[c0:c0 + BLOCK])
            if jb == 0:
                acc_s[...] = term
            else:
                acc_s[...] += term

        @pl.when(second & (m == 1))
        def _():
            out_copy(0).wait()

        for k in range(256 // BAND):
            r = band(k)
            value = f_s[r] + (acc_s[r] + biases[4])
            unit, inverse = normalise(value)
            n2_s[m, r] = bf16(unit)
            r2_s[m, r] = inverse
            result = unit * gains[1:2] + biases[5]
            out_s[r] = result
            send_s[m, r] = bf16(result)

        @pl.when(first)
        def _():
            hand_on(m).start()

        @pl.when(second)
        def _():
            out_copy(m).start()

        pair(1, m).start()
        return carry

    lax.fori_loop(0, 2, forward, 0)

    def norm_back(grad, unit, inverse, gain):
        scaled = grad * gain
        mean_one = jnp.mean(scaled, -1, keepdims=True)
        mean_two = jnp.mean(scaled * unit, -1, keepdims=True)
        return inverse * (scaled - mean_one - unit * mean_two)

    def backward(m, carry):
        early = first & (m == 1)

        @pl.when(first)
        def _():
            hand_on(m).wait_send()
            hand_back(m).wait_recv()

        @pl.when(second)
        def _():
            cot_copy(m).wait()

        for k in range(256 // BAND):
            r = band(k)
            row = lax.broadcasted_iota(jnp.int32, (BAND, 1), 0) + k * BAND
            limit = jnp.where(m == 0, jnp.where(row < 128, length_a, length_b + 128), length_long)
            live = jnp.where((row < limit) | first, 1.0, 0.0)
            grad = f32(g_s[m, r]) * live
            unit = f32(n2_s[m, r])
            vec_s[1] += fold_rows(grad * unit)
            vec_s[7] += fold_rows(grad)
            grad_in = norm_back(grad, unit, r2_s[m, r], gains[1:2])
            f_s[r] = grad_in
            low = bf16(grad_in)
            gf_s[m, r] = low
            vec_s[6] += fold_rows(f32(low))

        pair(2, m).start()

        for jb in range(FF // BLOCK):
            c0 = jb * BLOCK
            gate_s[...] = dot_nt(gf_s[m], wd[c0:c0 + BLOCK])
            for k in range(256 // BAND):
                r = band(k)
                hid = gate_s[r]
                for c in (c0, c0 + FF):
                    gu_s[m, r, c:c + BLOCK] = bf16(hid * f32(gu_s[m, r, c:c + BLOCK]))
            term = dot_nt(gu_s[m, :, c0:c0 + BLOCK], wg[:, c0:c0 + BLOCK])
            term = term + dot_nt(gu_s[m, :, c0 + FF:c0 + FF + BLOCK], wg[:, c0 + FF:c0 + FF + BLOCK])
            if jb == 0:
                acc_s[...] = term
            else:
                acc_s[...] += term
            if jb == 1:
                @pl.when(early)
                def _():
                    step(0, 0)

        pair(3, m).start()

        @pl.when(early)
        def _():
            step(1, 0)

        for k in range(256 // BAND):
            r = band(k)
            grad = acc_s[r] + f_s[r]
            unit = f32(n1_s[m, r])
            vec_s[0] += fold_rows(grad * unit)
            vec_s[5] += fold_rows(grad)
            grad_in = norm_back(grad, unit, r1_s[m, r], gains[0:1])
            f_s[r] = grad_in
            low = bf16(grad_in)
            ga_s[m, r] = low
            vec_s[4] += fold_rows(f32(low))

        low_s[...] = bf16(dot_nt(ga_s[m], wo[...]))

        for hp in range(6):
            at = pl.ds(hp * 128, 128)
            q2 = qkv_s[m, :, at]
            k2 = qkv_s[m, :, pl.ds(hp * 128 + 768, 128)]
            v2 = qkv_s[m, :, pl.ds(hp * 128 + 1536, 128)]
            do2 = low_s[:, at]
            dq, dk, dv = [], [], []
            for e in range(2):
                vm = jnp.where(own_lanes(e), v2, jnp.zeros_like(v2))
                probs = p_s[m, 2 * hp + e]
                weighted = f32(probs) * dot_nt(vm, do2)
                total = jnp.sum(weighted, 0, keepdims=True)
                grad_scores = bf16(weighted - f32(probs) * total)
                dv.append(dot_nn(probs, do2))
                dk.append(dot_nn(grad_scores, q2))
                dq.append(dot_tn(grad_scores, k2))
            grad_q = bf16(jnp.where(lanes < 64, dq[0], dq[1]) * 0.125)
            grad_k = bf16(jnp.where(lanes < 64, dk[0], dk[1]))
            grad_v = bf16(jnp.where(lanes < 64, dv[0], dv[1]))
            vec_s[2, :, at] += fold_rows(f32(grad_q))
            vec_s[3, :, at] += fold_rows(f32(grad_v))
            qkv_s[m, :, at] = grad_q
            qkv_s[m, :, pl.ds(hp * 128 + 768, 128)] = grad_k
            qkv_s[m, :, pl.ds(hp * 128 + 1536, 128)] = grad_v

        @pl.when(early)
        def _():
            step(2, 0)

        @pl.when(first & (m == 1))
        def _():
            out_copy(0).wait()

        grad_a = dot_nt(qkv_s[m], wq[...]) + f_s[...]

        @pl.when(second)
        def _():
            send_s[m] = bf16(grad_a)
            hand_back(m).start()

        @pl.when(first)
        def _():
            out_s[...] = grad_a
            out_copy(m).start()

        return carry

    lax.fori_loop(0, 2, backward, 0)
    for k in range(8):
        v_acc[0, k:k + 1] = jnp.sum(vec_s[k], 0, keepdims=True)
    v_start(0)

    def tail_step(i, carry):
        step(i, carry)
        for stage in range(4):
            @pl.when(i == 2 * stage + 5)
            def _():
                v_finish(stage)
                if stage < 3:
                    v_start(stage + 1)

        return carry

    lax.fori_loop(3 * (1 - sec), N_CHUNKS + 6, tail_step, 0)
    o_vec[...] = v_acc[4]

    @pl.when(second)
    def _():
        hand_back(0).wait_send()
        hand_back(1).wait_send()

    out_copy(1).wait()


def run_layers(short_lens, long_lens, tokens, cotangent, w_qkv, w_out, w_gate_up, w_down, gains, biases):
    low, wide = jnp.bfloat16, jnp.float32
    hbm = pl.BlockSpec(memory_space=pl.ANY)
    vmem = pl.BlockSpec(memory_space=pltpu.VMEM)
    smem = pl.BlockSpec(memory_space=pltpu.SMEM)
    dma = pltpu.SemaphoreType.DMA
    of = pltpu.VMEM
    s = SLOTS
    return pl.pallas_call(
        layers_kernel,
        out_shape=[
            jax.ShapeDtypeStruct((2, 256, 768), wide),
            jax.ShapeDtypeStruct((12, 1, 2304), wide),
            jax.ShapeDtypeStruct((12, 1, 768), wide),
            jax.ShapeDtypeStruct((12, 1, 6144), wide),
            jax.ShapeDtypeStruct((48, 768), wide),
            jax.ShapeDtypeStruct((8, 768), wide),
        ],
        in_specs=[smem] * 2 + [hbm] * 6 + [vmem] * 2,
        out_specs=[hbm] + [vmem] * 5,
        scratch_shapes=[
            of((768, 2304), low), of((768, 768), low), of((768, 6144), low), of((3072, 768), low),
            of((2, 256, 768), low), of((2, 256, 768), low), of((2, 256, 2304), low), of((2, 12, 256, 256), low),
            of((2, 256, 768), low), of((2, 256, 768), low), of((256, 768), low),
            of((2, 256, 768), low), of((2, 256, 768), low),
            of((2, 256, 1), wide), of((2, 256, 1), wide), of((2, 256, 6144), low), of((2, 32, 2, 48, 256), low),
            of((2, 256, 768), low), of((2, 256, 768), low), of((2, 256, 768), low), of((256, 768), wide),
            of((256, 768), wide), of((256, 768), wide), of((256, BLOCK), wide), of((256, BLOCK), wide),
            of((256, 256), wide), of((2, 256, 256), wide), of((8, 8, 768), wide),
            of((2, 256, 768), low), of((2, 32, 48, 256), low), of((2, 256, 768), low), of((2, 256, 3072), low),
            of((OWN_SLOTS, 2, 4, 4, 48, 256), low),
            of((s, 2, 4, 48, 256), low), of((s, 2, 2, 4, 48, 256), low), of((2, 2, 4, 48, 256), low),
            of((OWN_SLOTS, 2, 4, 48, 256), low),
            of((s, 2, 48, 256), low), of((s, 2, 2, 48, 256), low), of((2, 2, 48, 256), low),
            of((2, 48, 256), wide), of((2, 48, 256), wide), of((s, 48, 256), wide),
            of((48, 256), wide), of((2, 2, 16, 256), wide), of((2, 2, 16, 256), wide), of((s, 2, 16, 256), wide),
            of((5, 8, 768), wide), of((8, 8, 768), wide),
            dma((4,)), dma((2,)), dma((2,)), dma((2,)), dma((2,)), dma((2,)), dma((2,)), dma((2,)),
            dma((8, 2)), dma((8, 2)),
            dma((s, 4)), dma((s, 2)), dma((s, 2, 2)), dma((2, 2)),
            dma((s, 4)), dma((s, 2)), dma((s, 2, 2)), dma((2, 2)),
            dma((2,)), dma((s,)), dma((2,)), dma((s,)), dma((8,)), dma((8,)),
        ],
        compiler_params=pltpu.CompilerParams(
            collective_id=0, has_side_effects=True, vmem_limit_bytes=VMEM_LIMIT
        ),
        cost_estimate=pl.CostEstimate(flops=3 * 10 ** 10, bytes_accessed=4 * 10 ** 7, transcendentals=10 ** 7),
        name="run_layers",
    )(short_lens, long_lens, tokens, cotangent, w_qkv, w_out, w_gate_up, w_down, gains, biases)


def place_kernel(start, boundary, qkv, out, gate_up, down, vec, o_b, o_q, o_o, o_g, o_d, o_gains, o_biases):
    o_b[0] = boundary[...]
    o_g[...] = gate_up[...]
    o_q[...] = qkv[...]
    o_o[...] = out[...]
    o_d[0] = down[...]
    mine = pltpu.roll(vec[...], lax.rem(D - start[0], D), axis=1)
    o_gains[0] = mine[:2, :12]
    o_biases[:, 0] = mine[2:, :12]


def place(start, boundary, qkv, out, gate_up, down, vec):
    wide = jnp.float32
    vmem = pl.BlockSpec(memory_space=pltpu.VMEM)
    return pl.pallas_call(
        place_kernel,
        out_shape=[
            jax.ShapeDtypeStruct((1, 2, 256, 768), wide),
            jax.ShapeDtypeStruct((12, 1, 2304), wide),
            jax.ShapeDtypeStruct((12, 1, 768), wide),
            jax.ShapeDtypeStruct((12, 1, 6144), wide),
            jax.ShapeDtypeStruct((1, 48, 768), wide),
            jax.ShapeDtypeStruct((1, 2, 12), wide),
            jax.ShapeDtypeStruct((6, 1, 12), wide),
        ],
        in_specs=[pl.BlockSpec(memory_space=pltpu.SMEM)] + [vmem] * 6,
        out_specs=[vmem] * 7,
        compiler_params=pltpu.CompilerParams(vmem_limit_bytes=32 * 1024 * 1024),
        name="place",
    )(start, boundary, qkv, out, gate_up, down, vec)


def on_device(
    tokens, cotangent, short_lens, long_lens, w_qkv, w_out, w_gate_up, w_down, gains, biases
):
    boundary, q, o, g, d, vec = run_layers(
        short_lens, long_lens, tokens, cotangent, w_qkv[0], w_out[0], w_gate_up[0], w_down[0], gains[0],
        jnp.transpose(biases, (1, 0, 2)),
    )
    start = jnp.full((1,), lax.axis_index("dp") * 12, jnp.int32)
    b, q, o, g, d, gains_out, biases_out = place(start, boundary, q, o, g, d, vec)
    q, o, g, biases_out = (jnp.transpose(rows, (1, 0, 2)) for rows in (q, o, g, biases_out))
    return (b, q, o, g, d, gains_out, biases_out)


def solution(mesh):
    placed = (
        P(None, "dp", None),
        P(None, "dp", None),
        P("dp"),
        P("dp"),
        P("section", None, None),
        P("section", None, None),
        P("section", None, None),
        P("section", None, None),
        P("section", None, None),
        P("section", None, None),
    )
    return jax.shard_map(
        on_device,
        mesh=mesh,
        in_specs=placed,
        out_specs=(
            P("section", None, "dp", None),
            P("section", "dp", None),
            P("section", "dp", None),
            P("section", "dp", None),
            P("section", "dp", None),
            P("section", None, "dp"),
            P("section", None, "dp"),
        ),
        check_vma=False,
    )
```

time: 2280 us -> 163 us (0.07)
  waiting for transfers between devices: 1270 us -> 0 us
  blocking collectives: 328 us -> 0 us
  local copies, waits for them, and re-layouts: 226 us -> 5.67 us
  matrix products: 220 us -> 0 us
  Pallas kernels: 0 us -> 155 us
  other arithmetic: 152 us -> 0 us
  loops' own time: 35.1 us -> 0 us
    unnamed x5 -> x0, waiting for transfers between devices: 987 us -> none
    unnamed x1 -> x0, blocking collectives: 328 us -> none
    dot_general x50 -> x0, matrix products: 220 us -> none  [the longest x4 24.2 us: forward(): jnp.dot(hidden, weight_down, preferred_element_type=jnp.float32)]
    reduce_scatter x1 -> x0, waiting for transfers between devices: 179 us -> none  [on_device(): lax.psum_scatter(grad_weight_down[None], 'dp', scatter_dimension=1, tiled...]
    pallas_call x0 -> x2, Pallas kernels: none -> 155 us  [the longest x1 154 us: run_layers(): pl.pallas_call(layers_kernel, out_shape=[jax.ShapeDtypeStruct((2, 256, 76...]
    ppermute x4 -> x0, waiting for transfers between devices: 107 us -> none  [passed_along(): lax.ppermute(value, axis, [(source, source + steps) for source in range(i...]
    cond x126 -> x0, local copies, waits for them, and re-layouts: 84.9 us -> none  [the longest x4 56.5 us: on_device(): lax.cond(first_section, branches[0], branches[1], incoming, saved)]
    another operation x46 -> x0, local copies, waits for them, and re-layouts: 55.7 us -> none
  transfers between devices with their start and end apart: 7 -> 0, of which waited for: 7 -> 0; matrix products, arithmetic and copies ran while one was open for 7% -> 0% of each run, Pallas kernels for 0% -> 0%
where the time goes in v4:
time: 163 us; the launch traced here: 162 us
  Pallas kernels  155 us (95%)
  local copies, waits for them, and re-layouts  5.67 us (3%)
    pallas_call x1, Pallas kernels, run_layers(): pl.pallas_call(layers_kernel, out_shape=[jax.ShapeDtypeStruct((2, 256, 76...  154 us
    unnamed x12, local copies, waits for them, and re-layouts  5.67 us

profile of v4, /device:TPU:1, one launch (start us, length us, event | category | flops | bytes accessed | tf_op | source)
XLA Modules:
  0.0 162.4 jit_solution(13028042120529625986)
XLA Ops:
  1.3 154.0 %run_layers.1 = (f32[2,256,768]{2,1,0:T(8,128)}, f32[12,1,2304]{2,1,0:T(1,128)}, f32[12,1,768]{2,1,0:T(1,128)}, f32[12,1,6144]{2,1,0:T(1,128)}, f32[48,768]{1,0:T(8,128)}, /*index=5*/f32[8,768]{1,0:T(8,128)}) custom-call(s32[2]{0:T(128)} %short_lens.1, s32[1]{0:T(128)S(6)} %copy.17.long_lens, bf16[2,256,768]{2,1,0:T(8,128)(2,1)} %tokens.1, ...), custom_call_target="tpu_custom_call" | custom-call | flops 30000001024 | bytes 40000000 | tf_op jit(solution)/shard_map/run_layers/pallas_call | solution.py:727
  155.3 0.0 copy-start
  155.3 1.4 copy-done
  156.7 0.0 copy-start.1
  156.7 1.0 copy-done.1
  157.7 0.0 copy-start.2
  157.7 0.9 copy-done.2
  158.6 0.0 copy-start.3
  158.6 0.9 copy-done.3
  159.5 0.0 copy-start.4
  159.5 0.8 copy-done.4
  160.3 0.0 copy-start.5
  160.3 0.7 copy-done.5
  161.0 1.3 place.1
Async XLA Ops:
  155.3 1.4 copy-start
  156.7 1.0 copy-start.1
  157.7 0.9 copy-start.2
  158.6 0.9 copy-start.3
  159.5 0.8 copy-start.4
  160.3 0.7 copy-start.5

commit v5 on v4

--- a/solution.py
+++ b/solution.py
@@ -18,7 +18,7 @@
 MESH_IDS = pl.DeviceIdType.MESH
 
 epsilon = 1e-05
-masked_value = -1000000000.0
+masked_distance = 1e12
 
 
 def dot_nn(lhs, rhs):
@@ -65,7 +65,7 @@
     short_lens, long_lens, tokens, cotangent, w_qkv, w_out, w_gate_up, w_down, gains, biases,
     boundary, o_qkv, o_out, o_gu, o_dn, o_vec,
     wq, wo, wg, wd, x_s, g_s, qkv_s, p_s, mixed_s, nl_s, low_s, n1_s, n2_s, r1_s, r2_s, gu_s, ht_s,
-    gf_s, ga_s, send_s, out_s, acc_s, f_s, gate_s, up_s, dist_s, mask_s, vec_s,
+    gf_s, ga_s, send_s, out_s, acc_s, f_s, gate_s, up_s, dist_s, vec_s,
     peer_n, peer_h, peer_f, peer_g,
     own, ra_relay, ra_fin, sa, own_b, rb_relay, rb_fin, sb, x_send, x_keep, x_recv, c_tmp, c_send, c_keep, c_recv,
     v_acc, v_recv,
@@ -152,18 +152,6 @@
     w_copies[0].start()
     w_copies[1].start()
 
-    @pl.when(first)
-    def _():
-        token_copy(1).start()
-
-    w_copies[2].start()
-    w_copies[3].start()
-
-    @pl.when(second)
-    def _():
-        cot_copy(0).start()
-        cot_copy(1).start()
-
     barrier = pltpu.get_barrier_semaphore()
     pl.semaphore_signal(barrier, inc=1, device_id={"section": 1 - sec}, device_id_type=MESH_IDS)
     for target in [peer_core, peer_x] + y_ids + z_ids:
@@ -173,7 +161,7 @@
     vec_s[...] = jnp.zeros_like(vec_s)
     rows_j = lax.broadcasted_iota(jnp.int32, (256, 256), 0)
     cols_i = lax.broadcasted_iota(jnp.int32, (256, 256), 1)
-    dist_s[...] = f32(jnp.abs(rows_j - cols_i))
+    distance = f32(jnp.abs(rows_j - cols_i))
     length_a, length_b, length_long = short_lens[0], short_lens[1], long_lens[0]
     for m in range(2):
         if m == 0:
@@ -182,7 +170,20 @@
             ok = rows_j + apart < limit
         else:
             ok = rows_j < length_long
-        mask_s[m] = jnp.where(ok, 1.0, 0.0)
+        dist_s[m] = jnp.where(ok, distance, masked_distance)
+
+    w_copies[0].wait()
+    w_copies[2].start()
+    w_copies[3].start()
+
+    @pl.when(first)
+    def _():
+        token_copy(1).start()
+
+    @pl.when(second)
+    def _():
+        cot_copy(0).start()
+        cot_copy(1).start()
 
 
     def v_sends(stage):
@@ -472,10 +473,6 @@
         def _():
             hand_on(m).wait_recv()
 
-        @pl.when(m == 0)
-        def _():
-            w_copies[0].wait()
-
         x = x_s[m]
         query = dot_nn(x, wq[:, 0:768]) + biases[0]
         qkv_s[m, :, 0:768] = bf16(f32(bf16(query)) * 0.125)
@@ -487,17 +484,19 @@
             q2 = qkv_s[m, :, at]
             k2 = qkv_s[m, :, pl.ds(hp * 128 + 768, 128)]
             v2 = qkv_s[m, :, pl.ds(hp * 128 + 1536, 128)]
-            outs = []
+            none = jnp.zeros_like(q2)
+            qs = jnp.concatenate([jnp.where(own_lanes(e), q2, none) for e in range(2)], 0)
+            vs = jnp.concatenate([jnp.where(own_lanes(e), v2, none) for e in range(2)], 0)
+            scores_two = dot_nt(k2, qs)
+            probs_two = []
             for e in range(2):
                 head = 2 * hp + e
-                qm = jnp.where(own_lanes(e), q2, jnp.zeros_like(q2))
-                scores = dot_nt(k2, qm) - 2.0 ** (-8.0 * (head + 1) / HEADS) * dist_s[...]
-                scores = jnp.where(mask_s[m] > 0.5, scores, masked_value)
+                scores = scores_two[:, 256 * e:256 * e + 256] - 2.0 ** (-8.0 * (head + 1) / HEADS) * dist_s[m]
                 expo = jnp.exp(scores - jnp.max(scores, 0, keepdims=True))
                 probs = bf16(expo * (1.0 / jnp.sum(expo, 0, keepdims=True)))
                 p_s[m, head] = probs
-                outs.append(dot_tn(probs, v2))
-            mixed_s[m, :, at] = bf16(jnp.where(lanes < 64, outs[0], outs[1]))
+                probs_two.append(probs)
+            mixed_s[m, :, at] = bf16(dot_tn(jnp.concatenate(probs_two, 0), vs))
 
         @pl.when(m == 0)
         def _():
@@ -640,33 +639,51 @@
             ga_s[m, r] = low
             vec_s[4] += fold_rows(f32(low))
 
-        low_s[...] = bf16(dot_nt(ga_s[m], wo[...]))
-
-        for hp in range(6):
+        def mixed_back(g):
+            c = g * 256
+            low_s[:, c:c + 256] = bf16(dot_nt(ga_s[m], wo[c:c + 256]))
+
+        def attend_back(hp):
             at = pl.ds(hp * 128, 128)
             q2 = qkv_s[m, :, at]
             k2 = qkv_s[m, :, pl.ds(hp * 128 + 768, 128)]
             v2 = qkv_s[m, :, pl.ds(hp * 128 + 1536, 128)]
             do2 = low_s[:, at]
-            dq, dk, dv = [], [], []
+            none = jnp.zeros_like(q2)
+            qs, ks, ds = (
+                jnp.concatenate([jnp.where(own_lanes(e), wide, none) for e in range(2)], 0) for wide in (q2, k2, do2)
+            )
+            grad_probs_two = dot_nt(v2, ds)
+            probs_two = [p_s[m, 2 * hp + e] for e in range(2)]
+            scores_two = []
             for e in range(2):
-                vm = jnp.where(own_lanes(e), v2, jnp.zeros_like(v2))
-                probs = p_s[m, 2 * hp + e]
-                weighted = f32(probs) * dot_nt(vm, do2)
+                weighted = f32(probs_two[e]) * grad_probs_two[:, 256 * e:256 * e + 256]
                 total = jnp.sum(weighted, 0, keepdims=True)
-                grad_scores = bf16(weighted - f32(probs) * total)
-                dv.append(dot_nn(probs, do2))
-                dk.append(dot_nn(grad_scores, q2))
-                dq.append(dot_tn(grad_scores, k2))
-            grad_q = bf16(jnp.where(lanes < 64, dq[0], dq[1]) * 0.125)
-            grad_k = bf16(jnp.where(lanes < 64, dk[0], dk[1]))
-            grad_v = bf16(jnp.where(lanes < 64, dv[0], dv[1]))
+                scores_two.append(bf16(weighted - f32(probs_two[e]) * total))
+            grad_v = bf16(dot_nn(jnp.concatenate(probs_two, 1), ds))
+            grad_k = bf16(dot_nn(jnp.concatenate(scores_two, 1), qs))
+            grad_q = bf16(dot_tn(jnp.concatenate(scores_two, 0), ks) * 0.125)
             vec_s[2, :, at] += fold_rows(f32(grad_q))
             vec_s[3, :, at] += fold_rows(f32(grad_v))
             qkv_s[m, :, at] = grad_q
             qkv_s[m, :, pl.ds(hp * 128 + 768, 128)] = grad_k
             qkv_s[m, :, pl.ds(hp * 128 + 1536, 128)] = grad_v
 
+        mixed_back(0)
+        for g in range(3):
+            if g < 2:
+                mixed_back(g + 1)
+            attend_back(2 * g)
+            attend_back(2 * g + 1)
+            c = g * 256
+            term = dot_nt(qkv_s[m, :, c:c + 256], wq[:, c:c + 256])
+            for c in (g * 256 + 768, g * 256 + 1536):
+                term = term + dot_nt(qkv_s[m, :, c:c + 256], wq[:, c:c + 256])
+            if g == 0:
+                acc_s[...] = term
+            else:
+                acc_s[...] += term
+
         @pl.when(early)
         def _():
             step(2, 0)
@@ -675,7 +692,7 @@
         def _():
             out_copy(0).wait()
 
-        grad_a = dot_nt(qkv_s[m], wq[...]) + f_s[...]
+        grad_a = acc_s[...] + f_s[...]
 
         @pl.when(second)
         def _():
@@ -744,7 +761,7 @@
             of((2, 256, 1), wide), of((2, 256, 1), wide), of((2, 256, 6144), low), of((2, 32, 2, 48, 256), low),
             of((2, 256, 768), low), of((2, 256, 768), low), of((2, 256, 768), low), of((256, 768), wide),
             of((256, 768), wide), of((256, 768), wide), of((256, BLOCK), wide), of((256, BLOCK), wide),
-            of((256, 256), wide), of((2, 256, 256), wide), of((8, 8, 768), wide),
+            of((2, 256, 256), wide), of((8, 8, 768), wide),
             of((2, 256, 768), low), of((2, 32, 48, 256), low), of((2, 256, 768), low), of((2, 256, 3072), low),
             of((OWN_SLOTS, 2, 4, 4, 48, 256), low),
             of((s, 2, 4, 48, 256), low), of((s, 2, 2, 4, 48, 256), low), of((2, 2, 4, 48, 256), low),
@@ -767,15 +784,20 @@
     )(short_lens, long_lens, tokens, cotangent, w_qkv, w_out, w_gate_up, w_down, gains, biases)
 
 
-def place_kernel(start, boundary, qkv, out, gate_up, down, vec, o_b, o_q, o_o, o_g, o_d, o_gains, o_biases):
-    o_b[0] = boundary[...]
-    o_g[...] = gate_up[...]
-    o_q[...] = qkv[...]
-    o_o[...] = out[...]
-    o_d[0] = down[...]
+def place_kernel(start, boundary, qkv, out, gate_up, down, vec, o_b, o_q, o_o, o_g, o_d, o_gains, o_biases, sems):
+    copies = [
+        pltpu.make_async_copy(source, target, sems.at[k])
+        for k, (source, target) in enumerate(
+            ((boundary, o_b.at[0]), (gate_up, o_g), (qkv, o_q), (out, o_o), (down, o_d.at[0]))
+        )
+    ]
+    for copy in copies:
+        copy.start()
     mine = pltpu.roll(vec[...], lax.rem(D - start[0], D), axis=1)
     o_gains[0] = mine[:2, :12]
     o_biases[:, 0] = mine[2:, :12]
+    for copy in copies:
+        copy.wait()
 
 
 def place(start, boundary, qkv, out, gate_up, down, vec):
@@ -792,8 +814,9 @@
             jax.ShapeDtypeStruct((1, 2, 12), wide),
             jax.ShapeDtypeStruct((6, 1, 12), wide),
         ],
-        in_specs=[pl.BlockSpec(memory_space=pltpu.SMEM)] + [vmem] * 6,
+        in_specs=[pl.BlockSpec(memory_space=pltpu.SMEM)] + [pl.BlockSpec(memory_space=pltpu.HBM)] * 5 + [vmem],
         out_specs=[vmem] * 7,
+        scratch_shapes=[pltpu.SemaphoreType.DMA((5,))],
         compiler_params=pltpu.CompilerParams(vmem_limit_bytes=32 * 1024 * 1024),
         name="place",
     )(start, boundary, qkv, out, gate_up, down, vec)

time: 163 us -> 161 us (0.988)
  Pallas kernels: 155 us -> 153 us
    pallas_call x1, Pallas kernels: 154 us -> 151 us  [run_layers(): pl.pallas_call(layers_kernel, out_shape=[jax.ShapeDtypeStruct((2, 256, 76...]
where the time goes in v5:
time: 161 us; the launch traced here: 160 us
  Pallas kernels  153 us (95%)
  local copies, waits for them, and re-layouts  5.67 us (4%)
    pallas_call x1, Pallas kernels, run_layers(): pl.pallas_call(layers_kernel, out_shape=[jax.ShapeDtypeStruct((2, 256, 76...  151 us
    unnamed x12, local copies, waits for them, and re-layouts  5.67 us

profile of v5, /device:TPU:1, one launch (start us, length us, event | category | flops | bytes accessed | tf_op | source)
XLA Modules:
  0.0 160.2 jit_solution(7815796705177119423)
XLA Ops:
  1.3 151.0 %run_layers.1 = (f32[2,256,768]{2,1,0:T(8,128)}, f32[12,1,2304]{2,1,0:T(1,128)}, f32[12,1,768]{2,1,0:T(1,128)}, f32[12,1,6144]{2,1,0:T(1,128)}, f32[48,768]{1,0:T(8,128)}, /*index=5*/f32[8,768]{1,0:T(8,128)}) custom-call(s32[2]{0:T(128)} %short_lens.1, s32[1]{0:T(128)S(6)} %copy.17.long_lens, bf16[2,256,768]{2,1,0:T(8,128)(2,1)} %tokens.1, ...), custom_call_target="tpu_custom_call" | custom-call | flops 30000001024 | bytes 40000000 | tf_op jit(solution)/shard_map/run_layers/pallas_call | solution.py:744
  152.3 0.0 copy-start
  152.3 1.4 copy-done
  153.7 0.0 copy-start.1
  153.7 1.0 copy-done.1
  154.7 0.0 copy-start.2
  154.7 0.9 copy-done.2
  155.6 0.0 copy-start.3
  155.6 0.9 copy-done.3
  156.5 0.0 copy-start.4
  156.5 0.8 copy-done.4
  157.2 0.0 copy-start.5
  157.2 0.7 copy-done.5
  158.0 2.0 %place.1 = (f32[1,2,256,768]{3,2,1,0:T(8,128)}, f32[12,1,2304]{2,1,0:T(1,128)}, f32[12,1,768]{2,1,0:T(1,128)}, f32[12,1,6144]{2,1,0:T(1,128)}, f32[1,48,768]{2,1...) custom-call(s32[1]{0:T(128)} %bitcast.start, f32[2,256,768]{2,1,0:T(8,128)S(1)} %copy-done, ...), custom_call_target="tpu_custom_call" | custom-call | tf_op jit(solution)/shard_map/place/pallas_call | solution.py:806
Async XLA Ops:
  152.3 1.4 copy-start
  153.7 1.0 copy-start.1
  154.7 0.9 copy-start.2
  155.6 0.9 copy-start.3
  156.5 0.8 copy-start.4
  157.2 0.7 copy-start.5

commit v6 on v5

--- a/solution.py
+++ b/solution.py
@@ -817,7 +817,7 @@
         in_specs=[pl.BlockSpec(memory_space=pltpu.SMEM)] + [pl.BlockSpec(memory_space=pltpu.HBM)] * 5 + [vmem],
         out_specs=[vmem] * 7,
         scratch_shapes=[pltpu.SemaphoreType.DMA((5,))],
-        compiler_params=pltpu.CompilerParams(vmem_limit_bytes=32 * 1024 * 1024),
+        compiler_params=pltpu.CompilerParams(vmem_limit_bytes=VMEM_LIMIT),
         name="place",
     )(start, boundary, qkv, out, gate_up, down, vec)
 

time: 161 us -> 156 us (0.969)
  local copies, waits for them, and re-layouts: 5.67 us -> 0 us
  Pallas kernels: 153 us -> 155 us
    unnamed x12 -> x0, local copies, waits for them, and re-layouts: 5.67 us -> none
where the time goes in v6:
time: 156 us
  Pallas kernels  155 us (99%)
    pallas_call x1, Pallas kernels, run_layers(): pl.pallas_call(layers_kernel, out_shape=[jax.ShapeDtypeStruct((2, 256, 76...  151 us
    pallas_call x1, Pallas kernels, place(): pl.pallas_call(place_kernel, out_shape=[jax.ShapeDtypeStruct((1, 2, 256,...  3.64 us

profile of v6, /device:TPU:1, one launch (start us, length us, event | category | flops | bytes accessed | tf_op | source)
XLA Modules:
  0.0 156.1 jit_solution(11704240560022576015)
XLA Ops:
  1.3 151.0 %run_layers.1 = (f32[2,256,768]{2,1,0:T(8,128)}, f32[12,1,2304]{2,1,0:T(1,128)}, f32[12,1,768]{2,1,0:T(1,128)}, f32[12,1,6144]{2,1,0:T(1,128)}, f32[48,768]{1,0:T(8,128)}, /*index=5*/f32[8,768]{1,0:T(8,128)}) custom-call(s32[2]{0:T(128)} %short_lens.1, s32[1]{0:T(128)S(6)} %copy.17.long_lens, bf16[2,256,768]{2,1,0:T(8,128)(2,1)} %tokens.1, ...), custom_call_target="tpu_custom_call" | custom-call | flops 30000001024 | bytes 40000000 | tf_op jit(solution)/shard_map/run_layers/pallas_call | solution.py:744
  152.3 3.6 %place.1 = (f32[1,2,256,768]{3,2,1,0:T(8,128)}, f32[12,1,2304]{2,1,0:T(1,128)}, f32[12,1,768]{2,1,0:T(1,128)}, f32[12,1,6144]{2,1,0:T(1,128)}, f32[1,48,768]{2,1...) custom-call(s32[1]{0:T(128)} %bitcast.start, f32[2,256,768]{2,1,0:T(8,128)} %get-tuple-element.20.boundary, ...), custom_call_target="tpu_custom_call" | custom-call | tf_op jit(solution)/shard_map/place/pallas_call | solution.py:806

commit v7 on v6

--- a/solution.py
+++ b/solution.py
@@ -12,6 +12,7 @@
 BAND = 32
 N_CHUNKS = 12
 N_DOWN = 3
+DIRECT = 9
 SLOTS = 5
 OWN_SLOTS = 3
 VMEM_LIMIT = 62 * 1024 * 1024
@@ -64,15 +65,17 @@
 def layers_kernel(
     short_lens, long_lens, tokens, cotangent, w_qkv, w_out, w_gate_up, w_down, gains, biases,
     boundary, o_qkv, o_out, o_gu, o_dn, o_vec,
-    wq, wo, wg, wd, x_s, g_s, qkv_s, p_s, mixed_s, nl_s, low_s, n1_s, n2_s, r1_s, r2_s, gu_s, ht_s,
-    gf_s, ga_s, send_s, out_s, acc_s, f_s, gate_s, up_s, dist_s, vec_s,
+    wq, wo, wg, wd, x_s, g_s, qkv_s, p_s, mixed_s, nl_s, n1_s, n2_s, r_s, gu_s, ht_s,
+    gf_s, ga_s, send_s, out_s, acc_s, f_s, gate_s, dist_s, vec_s,
     peer_n, peer_h, peer_f, peer_g,
     own, ra_relay, ra_fin, sa, own_b, rb_relay, rb_fin, sb, x_send, x_keep, x_recv, c_tmp, c_send, c_keep, c_recv,
+    rz, cz_send, cz_keep, cz_recv,
     v_acc, v_recv,
     w_sem, x_sem, g_sem, out_sem, f_send, f_recv, b_send, b_recv, pair_send, pair_recv,
     a_send, a_relay_recv, a_fin_recv, a2_send,
     bb_send, bb_relay_recv, bb_fin_recv, b2_send,
     xs_sem, xr_sem, cs_sem, cr_sem, vs_sem, vr_sem,
+    z_send, z_recv, czs_sem, czr_sem,
 ):
     sec = lax.axis_index("section")
     first = sec == 0
@@ -91,6 +94,9 @@
     peer_x = dev(yy, zz, 1 - xhi, core)
     y_ids = [dev((yy + k) % 4, zz, xhi, core) for k in (1, 2, 3)]
     z_ids = [dev(yy, (zz + k) % 4, xhi, core) for k in (1, 2, 3)]
+
+    yx_ids = [dev((yy + k) % 4, zz, 1 - xhi, core) for k in (1, 2, 3)]
+    zx_ids = [dev(yy, (zz + k) % 4, 1 - xhi, core) for k in (1, 2, 3)]
 
     def remote(src, dst, send, recv, target):
         return pltpu.make_async_remote_copy(
@@ -154,9 +160,9 @@
 
     barrier = pltpu.get_barrier_semaphore()
     pl.semaphore_signal(barrier, inc=1, device_id={"section": 1 - sec}, device_id_type=MESH_IDS)
-    for target in [peer_core, peer_x] + y_ids + z_ids:
+    for target in [peer_core, peer_x] + y_ids + z_ids + yx_ids + zx_ids:
         pl.semaphore_signal(barrier, inc=1, device_id={"dp": target}, device_id_type=MESH_IDS)
-    pl.semaphore_wait(barrier, 9)
+    pl.semaphore_wait(barrier, 15)
 
     vec_s[...] = jnp.zeros_like(vec_s)
     rows_j = lax.broadcasted_iota(jnp.int32, (256, 256), 0)
@@ -262,6 +268,29 @@
         slot, mine = j % SLOTS, j % 2
         return remote(x_send.at[mine], x_recv.at[slot], xs_sem.at[mine], xr_sem.at[slot], peer_x)
 
+    def direct_copies(j):
+        late, mine = j - DIRECT, j % OWN_SLOTS
+        par = 1 - j % 2
+        _, _, p = ring(par)
+        copies = []
+        for k in range(1, 8):
+            ahead, flip = k // 2, k % 2
+            if ahead == 0:
+                target = peer_x
+            else:
+                along_y, along_z = ((yx_ids, zx_ids) if flip else (y_ids, z_ids))
+                target = along_y[ahead - 1] * (1 - par) + along_z[ahead - 1] * par
+            seen = (4 - ahead) % 4 * 2 + flip
+            copies.append(remote(
+                own_b.at[mine, (xhi + flip) % 2, (p + ahead) % 4], rz.at[late, seen],
+                z_send.at[late, k], z_recv.at[late, seen], target,
+            ))
+        return copies
+
+    def cz_copy(j):
+        late = j - DIRECT
+        return remote(cz_send.at[late], cz_recv.at[late], czs_sem.at[late], czr_sem.at[late], peer_core)
+
     def c_copy(j):
         slot, mine = j % SLOTS, j % 2
         return remote(c_send.at[mine], c_recv.at[slot], cs_sem.at[mine], cr_sem.at[slot], peer_core)
@@ -366,12 +395,19 @@
                 copy.wait_recv()
             for h in range(2):
                 own_b[mine, h] = bf16(f32(own[mine, h, p]) + f32(ra_fin[slot, 0, h]) + f32(ra_fin[slot, 1, h]))
-            for copy in b1_copies(j2):
-                copy.start()
+            @when(j2 < DIRECT)
+            def _():
+                for copy in b1_copies(j2):
+                    copy.start()
+
+            @when(j2 >= DIRECT)
+            def _():
+                for copy in direct_copies(j2):
+                    copy.start()
 
         j3 = i - 3
 
-        @when((j3 >= 0) & (j3 < N_CHUNKS))
+        @when((j3 >= 0) & (j3 < DIRECT))
         def _():
             slot, mine, buf = j3 % SLOTS, j3 % OWN_SLOTS, j3 % 2
             _, _, p = ring(1 - j3 % 2)
@@ -386,7 +422,7 @@
 
         j4 = i - 4
 
-        @when((j4 >= 0) & (j4 < N_CHUNKS))
+        @when((j4 >= 0) & (j4 < DIRECT))
         def _():
             slot, mine, buf = j4 % SLOTS, j4 % OWN_SLOTS, j4 % 2
             _, _, p = ring(1 - j4 % 2)
@@ -403,7 +439,7 @@
 
         j5 = i - 5
 
-        @when((j5 >= 0) & (j5 < N_CHUNKS))
+        @when((j5 >= 0) & (j5 < DIRECT))
         def _():
             slot, buf = j5 % SLOTS, j5 % 2
             x_copy(j5).wait()
@@ -424,28 +460,54 @@
 
         j6 = i - 6
 
-        @when((j6 >= N_DOWN) & (j6 < N_CHUNKS))
+        @when((j6 >= N_DOWN) & (j6 < DIRECT))
         def _():
             slot, buf = j6 % SLOTS, j6 % 2
             c_copy(j6).wait()
             for source, at, who in ((c_keep, buf, core), (c_recv, slot, other)):
-                @when(j6 < N_DOWN + 6)
+                for h in range(2):
+                    column = pl.multiple_of(who * FF + (j6 - N_DOWN) * 512 + h * 256, 256)
+                    o_gu[:, 0, pl.ds(column, 256)] = source[at, h, 0:12]
+
+        j7 = i - 3
+
+        @when((j7 >= DIRECT) & (j7 < N_CHUNKS))
+        def _():
+            late, mine = j7 - DIRECT, j7 % OWN_SLOTS
+            _, _, p = ring(1 - j7 % 2)
+            copies = direct_copies(j7)
+            for copy in copies:
+                copy.wait_send()
+            for copy in copies:
+                copy.wait_recv()
+            total = f32(own_b[mine, xhi, p])
+            for k in range(1, 8):
+                total = total + f32(rz[late, k])
+            c_tmp[...] = total
+            for h in range(2):
+                upper, lower = c_tmp[24 * h:24 * h + 12], c_tmp[24 * h + 12:24 * h + 24]
+                cz_send[late, h, 0:12] = jnp.where(core == 0, lower, upper)
+                cz_keep[late, h, 0:12] = jnp.where(core == 0, upper, lower)
+            cz_copy(j7).start()
+
+        j8 = i - 4
+
+        @when((j8 >= DIRECT) & (j8 < N_CHUNKS))
+        def _():
+            late = j8 - DIRECT
+            cz_copy(j8).wait()
+            for source, who in ((cz_keep, core), (cz_recv, other)):
+                @when(j8 < N_DOWN + 8)
                 def _():
                     for h in range(2):
-                        column = pl.multiple_of(who * FF + (j6 - N_DOWN) * 512 + h * 256, 256)
-                        o_gu[:, 0, pl.ds(column, 256)] = source[at, h, 0:12]
-
-                @when((j6 >= N_DOWN + 6) & (j6 < N_DOWN + 8))
+                        column = pl.multiple_of(who * 1152 + (j8 - N_DOWN - 6) * 512 + h * 256, 128)
+                        o_qkv[:, 0, pl.ds(column, 256)] = source[late, h, 0:12]
+
+                @when(j8 == N_DOWN + 8)
                 def _():
-                    for h in range(2):
-                        column = pl.multiple_of(who * 1152 + (j6 - N_DOWN - 6) * 512 + h * 256, 128)
-                        o_qkv[:, 0, pl.ds(column, 256)] = source[at, h, 0:12]
-
-                @when(j6 == N_DOWN + 8)
-                def _():
-                    o_qkv[:, 0, pl.ds(pl.multiple_of(who * 1152 + 1024, 128), 128)] = source[at, 0, 0:12, 0:128]
-                    o_out[:, 0, pl.ds(pl.multiple_of(who * 384, 128), 128)] = source[at, 0, 0:12, 128:256]
-                    o_out[:, 0, pl.ds(pl.multiple_of(who * 384 + 128, 128), 256)] = source[at, 1, 0:12]
+                    o_qkv[:, 0, pl.ds(pl.multiple_of(who * 1152 + 1024, 128), 128)] = source[late, 0, 0:12, 0:128]
+                    o_out[:, 0, pl.ds(pl.multiple_of(who * 384, 128), 128)] = source[late, 0, 0:12, 128:256]
+                    o_out[:, 0, pl.ds(pl.multiple_of(who * 384 + 128, 128), 256)] = source[late, 1, 0:12]
 
         return carry
 
@@ -509,7 +571,7 @@
             unit, inverse = normalise(value)
             normed = unit * gains[0:1] + biases[3]
             n1_s[m, r] = bf16(unit)
-            r1_s[m, r] = inverse
+            r_s[m, r, 0:1] = inverse
             f_s[r] = normed
             nl_s[m, r] = bf16(normed)
 
@@ -519,15 +581,19 @@
         def _():
             w_copies[2].wait()
             w_copies[3].wait()
+
+        @pl.when(second & (m == 1))
+        def _():
+            out_copy(0).wait()
 
         for jb in range(FF // BLOCK):
             c0 = jb * BLOCK
             low = nl_s[m]
             gate_s[...] = dot_nn(low, wg[:, c0:c0 + BLOCK])
-            up_s[...] = dot_nn(low, wg[:, c0 + FF:c0 + FF + BLOCK])
+            out_s[...] = dot_nn(low, wg[:, c0 + FF:c0 + FF + BLOCK])
             for k in range(256 // BAND):
                 r = band(k)
-                gate, up = gate_s[r], up_s[r]
+                gate, up = gate_s[r], out_s[r]
                 act, slope = gelu_terms(gate)
                 gu_s[m, r, c0:c0 + BLOCK] = bf16(up * slope)
                 gu_s[m, r, c0 + FF:c0 + FF + BLOCK] = bf16(act)
@@ -540,16 +606,12 @@
             else:
                 acc_s[...] += term
 
-        @pl.when(second & (m == 1))
-        def _():
-            out_copy(0).wait()
-
         for k in range(256 // BAND):
             r = band(k)
             value = f_s[r] + (acc_s[r] + biases[4])
             unit, inverse = normalise(value)
             n2_s[m, r] = bf16(unit)
-            r2_s[m, r] = inverse
+            r_s[m, r, 1:2] = inverse
             result = unit * gains[1:2] + biases[5]
             out_s[r] = result
             send_s[m, r] = bf16(result)
@@ -594,7 +656,7 @@
             unit = f32(n2_s[m, r])
             vec_s[1] += fold_rows(grad * unit)
             vec_s[7] += fold_rows(grad)
-            grad_in = norm_back(grad, unit, r2_s[m, r], gains[1:2])
+            grad_in = norm_back(grad, unit, r_s[m, r, 1:2], gains[1:2])
             f_s[r] = grad_in
             low = bf16(grad_in)
             gf_s[m, r] = low
@@ -633,7 +695,7 @@
             unit = f32(n1_s[m, r])
             vec_s[0] += fold_rows(grad * unit)
             vec_s[5] += fold_rows(grad)
-            grad_in = norm_back(grad, unit, r1_s[m, r], gains[0:1])
+            grad_in = norm_back(grad, unit, r_s[m, r, 0:1], gains[0:1])
             f_s[r] = grad_in
             low = bf16(grad_in)
             ga_s[m, r] = low
@@ -641,14 +703,14 @@
 
         def mixed_back(g):
             c = g * 256
-            low_s[:, c:c + 256] = bf16(dot_nt(ga_s[m], wo[c:c + 256]))
+            send_s[m, :, c:c + 256] = bf16(dot_nt(ga_s[m], wo[c:c + 256]))
 
         def attend_back(hp):
             at = pl.ds(hp * 128, 128)
             q2 = qkv_s[m, :, at]
             k2 = qkv_s[m, :, pl.ds(hp * 128 + 768, 128)]
             v2 = qkv_s[m, :, pl.ds(hp * 128 + 1536, 128)]
-            do2 = low_s[:, at]
+            do2 = send_s[m, :, at]
             none = jnp.zeros_like(q2)
             qs, ks, ds = (
                 jnp.concatenate([jnp.where(own_lanes(e), wide, none) for e in range(2)], 0) for wide in (q2, k2, do2)
@@ -722,7 +784,7 @@
 
         return carry
 
-    lax.fori_loop(3 * (1 - sec), N_CHUNKS + 6, tail_step, 0)
+    lax.fori_loop(3 * (1 - sec), N_CHUNKS + 4, tail_step, 0)
     o_vec[...] = v_acc[4]
 
     @pl.when(second)
@@ -756,11 +818,11 @@
         scratch_shapes=[
             of((768, 2304), low), of((768, 768), low), of((768, 6144), low), of((3072, 768), low),
             of((2, 256, 768), low), of((2, 256, 768), low), of((2, 256, 2304), low), of((2, 12, 256, 256), low),
-            of((2, 256, 768), low), of((2, 256, 768), low), of((256, 768), low),
             of((2, 256, 768), low), of((2, 256, 768), low),
-            of((2, 256, 1), wide), of((2, 256, 1), wide), of((2, 256, 6144), low), of((2, 32, 2, 48, 256), low),
+            of((2, 256, 768), low), of((2, 256, 768), low),
+            of((2, 256, 2), wide), of((2, 256, 6144), low), of((2, 32, 2, 48, 256), low),
             of((2, 256, 768), low), of((2, 256, 768), low), of((2, 256, 768), low), of((256, 768), wide),
-            of((256, 768), wide), of((256, 768), wide), of((256, BLOCK), wide), of((256, BLOCK), wide),
+            of((256, 768), wide), of((256, 768), wide), of((256, BLOCK), wide),
             of((2, 256, 256), wide), of((8, 8, 768), wide),
             of((2, 256, 768), low), of((2, 32, 48, 256), low), of((2, 256, 768), low), of((2, 256, 3072), low),
             of((OWN_SLOTS, 2, 4, 4, 48, 256), low),
@@ -769,12 +831,14 @@
             of((s, 2, 48, 256), low), of((s, 2, 2, 48, 256), low), of((2, 2, 48, 256), low),
             of((2, 48, 256), wide), of((2, 48, 256), wide), of((s, 48, 256), wide),
             of((48, 256), wide), of((2, 2, 16, 256), wide), of((2, 2, 16, 256), wide), of((s, 2, 16, 256), wide),
+            of((3, 8, 48, 256), low), of((3, 2, 16, 256), wide), of((3, 2, 16, 256), wide), of((3, 2, 16, 256), wide),
             of((5, 8, 768), wide), of((8, 8, 768), wide),
             dma((4,)), dma((2,)), dma((2,)), dma((2,)), dma((2,)), dma((2,)), dma((2,)), dma((2,)),
             dma((8, 2)), dma((8, 2)),
             dma((s, 4)), dma((s, 2)), dma((s, 2, 2)), dma((2, 2)),
             dma((s, 4)), dma((s, 2)), dma((s, 2, 2)), dma((2, 2)),
             dma((2,)), dma((s,)), dma((2,)), dma((s,)), dma((8,)), dma((8,)),
+            dma((3, 8)), dma((3, 8)), dma((3,)), dma((3,)),
         ],
         compiler_params=pltpu.CompilerParams(
             collective_id=0, has_side_effects=True, vmem_limit_bytes=VMEM_LIMIT

time: 156 us -> 153 us (0.981)
  Pallas kernels: 155 us -> 151 us
    pallas_call x1, Pallas kernels: 151 us -> 147 us  [run_layers(): pl.pallas_call(layers_kernel, out_shape=[jax.ShapeDtypeStruct((2, 256, 76...]
where the time goes in v7:
time: 153 us
  Pallas kernels  151 us (99%)
    pallas_call x1, Pallas kernels, run_layers(): pl.pallas_call(layers_kernel, out_shape=[jax.ShapeDtypeStruct((2, 256, 76...  147 us
    pallas_call x1, Pallas kernels, place(): pl.pallas_call(place_kernel, out_shape=[jax.ShapeDtypeStruct((1, 2, 256,...  3.64 us

profile of v7, /device:TPU:1, one launch (start us, length us, event | category | flops | bytes accessed | tf_op | source)
XLA Modules:
  0.0 152.6 jit_solution(17149634619842680292)
XLA Ops:
  1.3 147.5 %run_layers.1 = (f32[2,256,768]{2,1,0:T(8,128)}, f32[12,1,2304]{2,1,0:T(1,128)}, f32[12,1,768]{2,1,0:T(1,128)}, f32[12,1,6144]{2,1,0:T(1,128)}, f32[48,768]{1,0:T(8,128)}, /*index=5*/f32[8,768]{1,0:T(8,128)}) custom-call(s32[2]{0:T(128)} %short_lens.1, s32[1]{0:T(128)S(6)} %copy.17.long_lens, bf16[2,256,768]{2,1,0:T(8,128)(2,1)} %tokens.1, ...), custom_call_target="tpu_custom_call" | custom-call | flops 30000001024 | bytes 40000000 | tf_op jit(solution)/shard_map/run_layers/pallas_call | solution.py:806
  148.8 3.6 %place.1 = (f32[1,2,256,768]{3,2,1,0:T(8,128)}, f32[12,1,2304]{2,1,0:T(1,128)}, f32[12,1,768]{2,1,0:T(1,128)}, f32[12,1,6144]{2,1,0:T(1,128)}, f32[1,48,768]{2,1...) custom-call(s32[1]{0:T(128)} %bitcast.start, f32[2,256,768]{2,1,0:T(8,128)} %get-tuple-element.20.boundary, ...), custom_call_target="tpu_custom_call" | custom-call | tf_op jit(solution)/shard_map/place/pallas_call | solution.py:870

commit v8 on v7

--- a/solution.py
+++ b/solution.py
@@ -678,7 +678,7 @@
                 acc_s[...] = term
             else:
                 acc_s[...] += term
-            if jb == 1:
+            if jb == 0:
                 @pl.when(early)
                 def _():
                     step(0, 0)

time: 153 us -> 152 us (level)
  no operation moved by 1% of the time
where the time goes in v8:
time: 152 us
  Pallas kernels  150 us (99%)
    pallas_call x1, Pallas kernels, run_layers(): pl.pallas_call(layers_kernel, out_shape=[jax.ShapeDtypeStruct((2, 256, 76...  146 us
    pallas_call x1, Pallas kernels, place(): pl.pallas_call(place_kernel, out_shape=[jax.ShapeDtypeStruct((1, 2, 256,...  3.64 us

profile of v8, /device:TPU:1, one launch (start us, length us, event | category | flops | bytes accessed | tf_op | source)
XLA Modules:
  0.0 151.6 jit_solution(17130640552343742628)
XLA Ops:
  1.3 146.4 %run_layers.1 = (f32[2,256,768]{2,1,0:T(8,128)}, f32[12,1,2304]{2,1,0:T(1,128)}, f32[12,1,768]{2,1,0:T(1,128)}, f32[12,1,6144]{2,1,0:T(1,128)}, f32[48,768]{1,0:T(8,128)}, /*index=5*/f32[8,768]{1,0:T(8,128)}) custom-call(s32[2]{0:T(128)} %short_lens.1, s32[1]{0:T(128)S(6)} %copy.17.long_lens, bf16[2,256,768]{2,1,0:T(8,128)(2,1)} %tokens.1, ...), custom_call_target="tpu_custom_call" | custom-call | flops 30000001024 | bytes 40000000 | tf_op jit(solution)/shard_map/run_layers/pallas_call | solution.py:806
  147.7 3.6 %place.1 = (f32[1,2,256,768]{3,2,1,0:T(8,128)}, f32[12,1,2304]{2,1,0:T(1,128)}, f32[12,1,768]{2,1,0:T(1,128)}, f32[12,1,6144]{2,1,0:T(1,128)}, f32[1,48,768]{2,1...) custom-call(s32[1]{0:T(128)} %bitcast.start, f32[2,256,768]{2,1,0:T(8,128)} %get-tuple-element.20.boundary, ...), custom_call_target="tpu_custom_call" | custom-call | tf_op jit(solution)/shard_map/place/pallas_call | solution.py:870

commit v9 on v8

--- a/solution.py
+++ b/solution.py
@@ -678,16 +678,12 @@
                 acc_s[...] = term
             else:
                 acc_s[...] += term
-            if jb == 0:
+            if jb in (0, 2):
                 @pl.when(early)
                 def _():
-                    step(0, 0)
+                    step(jb // 2, 0)
 
         pair(3, m).start()
-
-        @pl.when(early)
-        def _():
-            step(1, 0)
 
         for k in range(256 // BAND):
             r = band(k)

time: 152 us -> 155 us (1.020)
  Pallas kernels: 150 us -> 153 us
    pallas_call x1, Pallas kernels: 146 us -> 150 us  [run_layers(): pl.pallas_call(layers_kernel, out_shape=[jax.ShapeDtypeStruct((2, 256, 76...]
where the time goes in v9:
time: 155 us
  Pallas kernels  153 us (99%)
    pallas_call x1, Pallas kernels, run_layers(): pl.pallas_call(layers_kernel, out_shape=[jax.ShapeDtypeStruct((2, 256, 76...  150 us
    pallas_call x1, Pallas kernels, place(): pl.pallas_call(place_kernel, out_shape=[jax.ShapeDtypeStruct((1, 2, 256,...  3.64 us

profile of v9, /device:TPU:1, one launch (start us, length us, event | category | flops | bytes accessed | tf_op | source)
XLA Modules:
  0.0 154.9 jit_solution(12878849257686602050)
XLA Ops:
  1.3 149.8 %run_layers.1 = (f32[2,256,768]{2,1,0:T(8,128)}, f32[12,1,2304]{2,1,0:T(1,128)}, f32[12,1,768]{2,1,0:T(1,128)}, f32[12,1,6144]{2,1,0:T(1,128)}, f32[48,768]{1,0:T(8,128)}, /*index=5*/f32[8,768]{1,0:T(8,128)}) custom-call(s32[2]{0:T(128)} %short_lens.1, s32[1]{0:T(128)S(6)} %copy.17.long_lens, bf16[2,256,768]{2,1,0:T(8,128)(2,1)} %tokens.1, ...), custom_call_target="tpu_custom_call" | custom-call | flops 30000001024 | bytes 40000000 | tf_op jit(solution)/shard_map/run_layers/pallas_call | solution.py:802
  151.1 3.6 %place.1 = (f32[1,2,256,768]{3,2,1,0:T(8,128)}, f32[12,1,2304]{2,1,0:T(1,128)}, f32[12,1,768]{2,1,0:T(1,128)}, f32[12,1,6144]{2,1,0:T(1,128)}, f32[1,48,768]{2,1...) custom-call(s32[1]{0:T(128)} %bitcast.start, f32[2,256,768]{2,1,0:T(8,128)} %get-tuple-element.20.boundary, ...), custom_call_target="tpu_custom_call" | custom-call | tf_op jit(solution)/shard_map/place/pallas_call | solution.py:866
